TPU v7x, 32 devices: a whole 2x2x4 slice. The times are simulated.
32 devices in a mesh: ctx: 8 (over z, core), fsdp: 4 (over y, x).
Axes of the slice: x: 2, y: 2, z: 4, core: 2. Of those that a mesh axis runs over, the one named last changes fastest.
Arguments:
- tokens: bfloat16 [4096, 8192], P('ctx', 'fsdp'), may hold values from -6 to 6
- gain: float32 [8192], replicated, may hold values from 0.5 to 1.5
- in_weight: bfloat16 [8192, 3, 4096], P('ctx', None, 'fsdp'), may hold values from -0.0625 to 0.0625
- short_filter: float32 [3, 3, 4096], P(None, None, 'fsdp'), may hold values from -3.5 to 3.5
- long_filter: float32 [128, 4096], P(None, 'fsdp'), may hold values from -0.5 to 0.5
Outputs:
- gated_out: bfloat16 [4096, 4096], P('ctx', 'fsdp')
All inputs are finite; a program needn't handle non-finite values.
Results may differ from a plain program's by a relative error of at most 0.0086.
Values may be sent and summed in bfloat16 or wider, within the bound.
No kernel may reach another device: no remote copies, remote signals or barrier semaphores. Data moves between devices by JAX's collectives and lax.ppermute only.
A program may use at most 128 MiB of HBM per device.

v0:
```python
import jax
import jax.numpy as jnp
from jax import lax
from jax.sharding import PartitionSpec as P


def passed_along(value, axis, steps):
    count = lax.axis_size(axis)
    leading, last = (max(0, -steps), min(count, count - steps))
    return lax.ppermute(value, axis, [(source, source + steps) for source in range(leading, last)])


def short_mix(extended_rows, short_taps, row_count):
    extended = extended_rows.astype(jnp.float32)
    tap_count = short_taps.shape[0]
    result = jnp.zeros((row_count, extended.shape[1]), jnp.float32)
    for offset in range(tap_count):
        result = (
            result
            + short_taps[offset]
            * extended[tap_count - 1 - offset : tap_count - 1 - offset + row_count]
        )
    return result


def long_mix(signal_rows, filters, row_count):
    signal = signal_rows.astype(jnp.float32)
    tap_count = filters.shape[0]

    def group_step(counter, accumulated):
        for within in range(16):
            lag_value = counter * 16 + within
            window_rows = lax.dynamic_slice_in_dim(signal, tap_count - 1 - lag_value, row_count, 0)
            tap_weights = lax.dynamic_slice_in_dim(filters, lag_value, 1, 0)
            accumulated = accumulated + tap_weights * window_rows
        return accumulated

    initial = jnp.zeros((row_count, signal.shape[1]), jnp.float32)
    return lax.fori_loop(0, tap_count // 16, group_step, initial)


def on_device(tokens, gain, in_weight, short_filter, long_filter):
    row_count = tokens.shape[0]
    features = lax.all_gather(tokens, "fsdp", axis=1, tiled=True)
    widened = features.astype(jnp.float32)
    mean_square = jnp.mean(widened * widened, axis=1, keepdims=True)
    normed = (widened * lax.rsqrt(mean_square + 1e-06) * gain).astype(jnp.bfloat16)
    channels = in_weight.shape[2]
    panel_rows = lax.all_gather(in_weight, "ctx", axis=0, tiled=True)
    projected = jnp.dot(
        normed,
        panel_rows.reshape(panel_rows.shape[0], 3 * channels),
        preferred_element_type=jnp.float32,
    )
    projected = projected.astype(jnp.bfloat16)
    short_taps = short_filter.reshape(short_filter.shape[0], 3 * channels)
    short_count = short_taps.shape[0]
    long_count = long_filter.shape[0]
    upper_rim = passed_along(projected[row_count - (short_count - 1) :], "ctx", 1)
    featurized = short_mix(jnp.concatenate([upper_rim, projected], axis=0), short_taps, row_count)
    query = featurized[:, :channels]
    gated = (featurized[:, channels : 2 * channels] * featurized[:, 2 * channels :]).astype(
        jnp.bfloat16
    )
    gated_rim = passed_along(gated[row_count - (long_count - 1) :], "ctx", 1)
    signal_rows = jnp.concatenate([gated_rim, gated], axis=0)
    response = long_mix(signal_rows, long_filter, row_count)
    return (query * response).astype(jnp.bfloat16)


def solution(mesh):
    return jax.shard_map(
        on_device,
        mesh=mesh,
        in_specs=(
            P("ctx", "fsdp"),
            P(),
            P("ctx", None, "fsdp"),
            P(None, None, "fsdp"),
            P(None, "fsdp"),
        ),
        out_specs=P("ctx", "fsdp"),
        check_vma=False,
    )
```

profile of v0, /device:TPU:0, one launch (start us, length us, event | category | flops | bytes accessed | tf_op | source)
XLA Modules:
  0.0 660.9 jit_solution(5348810685153612755)
XLA Ops:
  7.3 8.6 %copy.6 = bf16[1024,3,1024]{0,2,1:T(8,128)(2,1)} copy(bf16[1024,3,1024]{2,0,1:T(8,128)(2,1)} %param.9) | data formatting | bytes 12582912 | tf_op args[2]
  16.0 83.6 %all-gather.3.cloned.1.call-done = bf16[512,8192]{1,0:T(8,128)(2,1)} async-done(((bf16[512,2048]{1,0:T(8,128)(2,1)}), bf16[512,8192]{1,0:T(8,128)(2,1)}) %all-gather.3.cloned.1.call-update) | async-done | bytes 8388624 | tf_op jit(solution)/shard_map/all_gather | solution.py:44
  99.5 5.1 fusion.15
  104.7 423.9 %all-gather.5.cloned.1.call-done = bf16[8192,3,1024]{0,2,1:T(8,128)(2,1)} async-done(((bf16[1024,3,1024]{0,2,1:T(8,128)(2,1)}), bf16[8192,3,1024]{0,2,1:T(8,128)(2,1)}) %all-gather.5.cloned.1.call-update) | async-done | bytes 50331664 | tf_op jit(solution)/shard_map/all_gather | solution.py:49
  528.6 33.9 %fusion.24 = bf16[512,3072]{1,0:T(8,128)(2,1)} fusion(bf16[8192,3072]{0,1:T(8,128)(2,1)} %bitcast.66, bf16[512,8192]{1,0:T(8,128)(2,1)} %all-gather.3.cloned.1.call-done, f32[8192]{0:T(1024)S(1)} %copy-done.3, f32[512]{0:T(512)S(1)} %add_rsqrt_fusion), kind=kOutput, calls=%fused_computation.45 | convolution fusion | flops 25788153856 | bytes 61900800 | tf_op jit(solution)/shard_map/dot_general | solution.py:50
  562.5 0.8 slice.47
  563.3 2.1 collective-permute-start
  565.6 0.7 collective-permute-done
  566.3 2.8 maximum_convert_fusion
  569.1 1.9 fusion.22
  571.0 2.6 copy-done
  574.0 2.3 collective-permute-start.1
  576.3 1.1 collective-permute-done.1
  577.5 1.6 maximum_convert_fusion.1
  579.0 71.5 %while.17 = (s32[]{:T(128)}, f32[512,1024]{1,0:T(8,128)}, f32[128,1024]{1,0:T(8,128)}, f32[639,1024]{1,0:T(8,128)S(1)}, s32[]{:T(128)}, /*index=5*/s32[]{:T(128)...) while((s32[]{:T(128)}, f32[512,1024]{1,0:T(8,128)}, ...), condition=%wide.region_2.0_spmd.clone, body=%wide.region_1.0_spmd.clone.sunk | while | flops 17301636 | bytes 37947292 | solution.py:39
  579.2 1.3 constant_dynamic-slice_fusion.17
  580.6 6.7 %fusion.32 = f32[512,1024]{1,0:T(8,128)} fusion(f32[512,1024]{1,0:T(8,128)} %get-tuple-element.328, f32[639,1024]{1,0:T(8,128)S(1)} %get-tuple-element.369, s32[]{:T(128)S(6)} %select_n.416, s32[]{:T(128)S(6)} %select_n.417, s32[]{:T(128)S(6)} %select_n.418, s32[]{:T(128)S(6)} %select_n.419, s32[]{:T(128)S(6)} %select_n.420, s32[]{:T(128)S(6)} %select_n.421, ...), kind=kLoop, calls=%fused_computation.15.clone.1 | loop fusion | flops 17301504 | bytes 37814336 | tf_op jit(solution)/shard_map/while/body/eval_jaxpr/add | solution.py:35
  587.3 1.3 constant_dynamic-slice_fusion.17
  588.6 7.7 %fusion.32 = f32[512,1024]{1,0:T(8,128)} fusion(f32[512,1024]{1,0:T(8,128)} %get-tuple-element.328, f32[639,1024]{1,0:T(8,128)S(1)} %get-tuple-element.369, s32[]{:T(128)S(6)} %select_n.416, s32[]{:T(128)S(6)} %select_n.417, s32[]{:T(128)S(6)} %select_n.418, s32[]{:T(128)S(6)} %select_n.419, s32[]{:T(128)S(6)} %select_n.420, s32[]{:T(128)S(6)} %select_n.421, ...), kind=kLoop, calls=%fused_computation.15.clone.1 | loop fusion | flops 17301504 | bytes 37814336 | tf_op jit(solution)/shard_map/while/body/eval_jaxpr/add | solution.py:35
  596.3 1.3 constant_dynamic-slice_fusion.17
  597.6 7.7 %fusion.32 = f32[512,1024]{1,0:T(8,128)} fusion(f32[512,1024]{1,0:T(8,128)} %get-tuple-element.328, f32[639,1024]{1,0:T(8,128)S(1)} %get-tuple-element.369, s32[]{:T(128)S(6)} %select_n.416, s32[]{:T(128)S(6)} %select_n.417, s32[]{:T(128)S(6)} %select_n.418, s32[]{:T(128)S(6)} %select_n.419, s32[]{:T(128)S(6)} %select_n.420, s32[]{:T(128)S(6)} %select_n.421, ...), kind=kLoop, calls=%fused_computation.15.clone.1 | loop fusion | flops 17301504 | bytes 37814336 | tf_op jit(solution)/shard_map/while/body/eval_jaxpr/add | solution.py:35
  605.4 1.3 constant_dynamic-slice_fusion.17
  606.7 7.7 %fusion.32 = f32[512,1024]{1,0:T(8,128)} fusion(f32[512,1024]{1,0:T(8,128)} %get-tuple-element.328, f32[639,1024]{1,0:T(8,128)S(1)} %get-tuple-element.369, s32[]{:T(128)S(6)} %select_n.416, s32[]{:T(128)S(6)} %select_n.417, s32[]{:T(128)S(6)} %select_n.418, s32[]{:T(128)S(6)} %select_n.419, s32[]{:T(128)S(6)} %select_n.420, s32[]{:T(128)S(6)} %select_n.421, ...), kind=kLoop, calls=%fused_computation.15.clone.1 | loop fusion | flops 17301504 | bytes 37814336 | tf_op jit(solution)/shard_map/while/body/eval_jaxpr/add | solution.py:35
  614.4 1.3 constant_dynamic-slice_fusion.17
  615.7 7.7 %fusion.32 = f32[512,1024]{1,0:T(8,128)} fusion(f32[512,1024]{1,0:T(8,128)} %get-tuple-element.328, f32[639,1024]{1,0:T(8,128)S(1)} %get-tuple-element.369, s32[]{:T(128)S(6)} %select_n.416, s32[]{:T(128)S(6)} %select_n.417, s32[]{:T(128)S(6)} %select_n.418, s32[]{:T(128)S(6)} %select_n.419, s32[]{:T(128)S(6)} %select_n.420, s32[]{:T(128)S(6)} %select_n.421, ...), kind=kLoop, calls=%fused_computation.15.clone.1 | loop fusion | flops 17301504 | bytes 37814336 | tf_op jit(solution)/shard_map/while/body/eval_jaxpr/add | solution.py:35
  623.4 1.3 constant_dynamic-slice_fusion.17
  624.7 7.7 %fusion.32 = f32[512,1024]{1,0:T(8,128)} fusion(f32[512,1024]{1,0:T(8,128)} %get-tuple-element.328, f32[639,1024]{1,0:T(8,128)S(1)} %get-tuple-element.369, s32[]{:T(128)S(6)} %select_n.416, s32[]{:T(128)S(6)} %select_n.417, s32[]{:T(128)S(6)} %select_n.418, s32[]{:T(128)S(6)} %select_n.419, s32[]{:T(128)S(6)} %select_n.420, s32[]{:T(128)S(6)} %select_n.421, ...), kind=kLoop, calls=%fused_computation.15.clone.1 | loop fusion | flops 17301504 | bytes 37814336 | tf_op jit(solution)/shard_map/while/body/eval_jaxpr/add | solution.py:35
  632.5 1.3 constant_dynamic-slice_fusion.17
  633.8 7.7 %fusion.32 = f32[512,1024]{1,0:T(8,128)} fusion(f32[512,1024]{1,0:T(8,128)} %get-tuple-element.328, f32[639,1024]{1,0:T(8,128)S(1)} %get-tuple-element.369, s32[]{:T(128)S(6)} %select_n.416, s32[]{:T(128)S(6)} %select_n.417, s32[]{:T(128)S(6)} %select_n.418, s32[]{:T(128)S(6)} %select_n.419, s32[]{:T(128)S(6)} %select_n.420, s32[]{:T(128)S(6)} %select_n.421, ...), kind=kLoop, calls=%fused_computation.15.clone.1 | loop fusion | flops 17301504 | bytes 37814336 | tf_op jit(solution)/shard_map/while/body/eval_jaxpr/add | solution.py:35
  641.5 1.3 constant_dynamic-slice_fusion.17
  642.8 7.7 %fusion.32 = f32[512,1024]{1,0:T(8,128)} fusion(f32[512,1024]{1,0:T(8,128)} %get-tuple-element.328, f32[639,1024]{1,0:T(8,128)S(1)} %get-tuple-element.369, s32[]{:T(128)S(6)} %select_n.416, s32[]{:T(128)S(6)} %select_n.417, s32[]{:T(128)S(6)} %select_n.418, s32[]{:T(128)S(6)} %select_n.419, s32[]{:T(128)S(6)} %select_n.420, s32[]{:T(128)S(6)} %select_n.421, ...), kind=kLoop, calls=%fused_computation.15.clone.1 | loop fusion | flops 17301504 | bytes 37814336 | tf_op jit(solution)/shard_map/while/body/eval_jaxpr/add | solution.py:35
  650.5 3.5 fusion.28
  (19 shorter events, 1.2 us)
Async XLA Ops:
  6.5 93.0 %all-gather.3.cloned.1.call-start = ((), (), s32[]{:S(2)}) async-start(), calls=%async_computation | async-start | bytes 10485760 | tf_op jit(solution)/shard_map/all_gather | solution.py:44
  7.3 521.3 %all-gather.5.cloned.1.call-start = ((), (), s32[]{:S(2)}) async-start(), calls=%async_computation.1 | async-start | bytes 56623104 | tf_op jit(solution)/shard_map/all_gather | solution.py:49
  16.0 512.6 %copy-start.3 = (f32[8192]{0:T(1024)S(1)}, f32[8192]{0:T(1024)}, u32[]{:S(2)}) copy-start(f32[8192]{0:T(1024)} %param.8) | copy-start | bytes 98308
  528.6 36.9 %copy-start.2 = (f32[3,3,1024]{2,1,0:T(4,128)S(1)}, f32[3,3,1024]{2,1,0:T(4,128)}, u32[]{:S(2)}) copy-start(f32[3,3,1024]{2,1,0:T(4,128)} %param.10) | copy-start | bytes 110596
  563.3 2.9 collective-permute-start
  571.0 2.7 copy-start
  574.0 2.4 copy-start.1
  574.0 3.4 collective-permute-start.1
Sparse Core Ops, SparseCore 0:
  9.2 90.2 all-gather.2
  101.2 427.3 all-gather.4
where the time goes:
time: 666 us; the launch traced here: 661 us
  waiting for transfers between devices  510 us (77%)
  other arithmetic  76.1 us (11%)
  matrix products  33.9 us (5%)
  local copies, waits for them, and re-layouts  22.6 us (3%)
  between operations  13.5 us (2%)
    all_gather x1, waiting for transfers between devices, on_device(): panel_rows = lax.all_gather(in_weight, 'ctx', axis=0, tiled=True)  424 us
    all_gather x1, waiting for transfers between devices, on_device(): features = lax.all_gather(tokens, 'fsdp', axis=1, tiled=True)  83.6 us
    add x8, other arithmetic, group_step(): accumulated = accumulated + tap_weights * window_rows  60.9 us
    dot_general x1, matrix products, on_device(): jnp.dot(normed, panel_rows.reshape(panel_rows.shape[0], 3 * channels), pr...  33.9 us
  transfers between devices with their start and end apart: 4, of which 4 were waited for; matrix products, arithmetic and copies ran while one was open for 2% of the time, Pallas kernels for 0%

commit v1 on v0

v1 whole, which is shorter than its diff:
```python
import jax
import jax.numpy as jnp
import numpy as np
from jax import lax
from jax.sharding import PartitionSpec as P

CORES = 2
STAGES = 4
EPS = 1e-06


def pick(stack, index):
    return lax.dynamic_index_in_dim(stack, index, 0, keepdims=False)


def swap(value, count, bits):
    if bits == 0:
        return value
    return lax.ppermute(value, "fsdp", [(j, j ^ bits) for j in range(count)])


def plane_shift(value, edges):
    return lax.ppermute(
        value, "ctx", [(a * CORES + c, b * CORES + c) for a, b in edges for c in range(CORES)]
    )


def line_sum(partials):
    planes = len(partials)
    right, left = None, None

    def onward(term, arrived):
        if arrived is not None:
            term = term + arrived.astype(jnp.float32)
        return term.astype(jnp.bfloat16)

    for step in range(1, planes):
        right = plane_shift(
            onward(partials[planes - step], right),
            [(p, p + 1) for p in range(planes - 1) if p < step],
        )
        left = plane_shift(
            onward(partials[step], left),
            [(p, p - 1) for p in range(1, planes) if p >= planes - step],
        )
    return partials[0] + right.astype(jnp.float32) + left.astype(jnp.float32)


def dft_matrices(length, taps):
    bins = length // 2 + 1
    k = np.arange(bins)[:, None]
    angle = 2.0 * np.pi * ((k * np.arange(length)[None, :]) % length) / length
    weight = np.where((k == 0) | (k == length // 2), 1.0, 2.0) / length
    analysis = np.stack([np.cos(angle), -np.sin(angle)])
    synthesis = np.stack([weight * np.cos(angle), -weight * np.sin(angle)])
    return analysis.astype(np.float32), synthesis[:, :, taps:].astype(np.float32)


def long_mix(signal, filters, row_count):
    taps = filters.shape[0]
    length = 2 * taps
    blocks = row_count // taps
    analysis, synthesis = dft_matrices(length, taps)
    pieces = jnp.stack([signal[b * taps : b * taps + length] for b in range(blocks)])
    pieces = pieces.astype(jnp.float32)
    high = lax.Precision.HIGH
    spectrum = jnp.einsum("pkn,bnc->pbkc", analysis, pieces, precision=high)
    tones = jnp.einsum("pkn,nc->pkc", analysis[:, :, :taps], filters, precision=high)
    real = spectrum[0] * tones[0] - spectrum[1] * tones[1]
    imag = spectrum[0] * tones[1] + spectrum[1] * tones[0]
    result = jnp.einsum("kn,bkc->bnc", synthesis[0], real, precision=high) + jnp.einsum(
        "kn,bkc->bnc", synthesis[1], imag, precision=high
    )
    return result.reshape(row_count, -1)


def on_device(tokens, gain, in_weight, short_filter, long_filter):
    planes = lax.axis_size("ctx") // CORES
    columns = lax.axis_size("fsdp")
    plane = lax.axis_index("ctx") // CORES
    column = lax.axis_index("fsdp")
    row_count, width = tokens.shape
    channels = in_weight.shape[2]

    pairs = [[p * CORES + c for c in range(CORES)] for p in range(planes)]
    weight = lax.all_gather(in_weight, "ctx", axis=0, tiled=True, axis_index_groups=pairs)
    weight = weight.reshape(weight.shape[0], 3 * channels)
    gains = gain.reshape(columns, width)

    stage_rows = row_count // STAGES
    share = stage_rows // columns
    projected = []
    for stage in range(STAGES):
        own = tokens[stage * stage_rows : (stage + 1) * stage_rows].reshape(columns, share, width)
        wide = jnp.stack([swap(pick(own, column ^ t), columns, t) for t in range(columns)])
        wide = wide.astype(jnp.float32)
        mean_square = jnp.sum(wide * wide, axis=(0, 2), keepdims=True) / (columns * width)
        gain_here = jnp.stack([pick(gains, column ^ t) for t in range(columns)])
        normed = wide * lax.rsqrt(mean_square + EPS) * gain_here[:, None, :]
        normed = normed.astype(jnp.bfloat16)
        rows_of = [None] * planes
        for d in range(planes):
            piece = pick(normed, column ^ ((plane + d) % planes))
            if d > 0:
                piece = plane_shift(piece, [(p, (p + d) % planes) for p in range(planes)])
            rows_of[(planes - d) % planes] = piece
        mine = jnp.stack(rows_of)
        lhs = jnp.stack([swap(mine, columns, t) for t in range(columns)], axis=1)
        partial = jnp.dot(
            lhs.reshape(planes * stage_rows, -1), weight, preferred_element_type=jnp.float32
        ).reshape(planes, stage_rows, 3 * channels)
        total = line_sum([partial[m] for m in range(planes)])
        total = total.astype(jnp.bfloat16).reshape(columns, share, 3 * channels)
        projected += [pick(total, column ^ t) for t in range(columns)]
    projected = jnp.concatenate(projected, axis=0)

    short_taps = short_filter.reshape(short_filter.shape[0], 3 * channels)
    short_count, long_count = short_taps.shape[0], long_filter.shape[0]
    edge = short_count - 1

    def short_mix(extended, taps, count):
        extended = extended.astype(jnp.float32)
        result = taps[0] * extended[edge : edge + count]
        for offset in range(1, short_count):
            result = result + taps[offset] * extended[edge - offset : edge - offset + count]
        return result

    def gate(mixed):
        return (mixed[:, channels : 2 * channels] * mixed[:, 2 * channels :]).astype(jnp.bfloat16)

    shards = lax.axis_size("ctx")
    onward = [(i, i + 1) for i in range(shards - 1)]
    last = gate(short_mix(projected[row_count - long_count - edge :], short_taps, long_count))
    upper_rim = lax.ppermute(projected[row_count - edge :], "ctx", onward)
    gated_rim = lax.ppermute(last, "ctx", onward)
    featurized = short_mix(jnp.concatenate([upper_rim, projected], axis=0), short_taps, row_count)
    signal = jnp.concatenate([gated_rim, gate(featurized)], axis=0)
    response = long_mix(signal, long_filter, row_count)
    return (featurized[:, :channels] * response).astype(jnp.bfloat16)


def solution(mesh):
    return jax.shard_map(
        on_device,
        mesh=mesh,
        in_specs=(
            P("ctx", "fsdp"),
            P(),
            P("ctx", None, "fsdp"),
            P(None, None, "fsdp"),
            P(None, "fsdp"),
        ),
        out_specs=P("ctx", "fsdp"),
        check_vma=False,
    )
```

time: 666 us -> 503 us (0.76)
  the two profiles are of different devices: /device:TPU:0 before, /device:TPU:1 now
where the time goes in v1:
time: 503 us; the launch traced here: 499 us
  starting transfers between devices  181 us (36%)
  waiting for transfers between devices  156 us (31%)
  local copies, waits for them, and re-layouts  73.9 us (15%)
  matrix products  45.6 us (9%)
  other arithmetic  28.3 us (6%)
  between operations  14.4 us (3%)
    ppermute x36, starting transfers between devices, plane_shift(): lax.ppermute(value, 'ctx', [(a * CORES + c, b * CORES + c) for a, b in ed...  105 us
    ppermute x36, waiting for transfers between devices, plane_shift(): lax.ppermute(value, 'ctx', [(a * CORES + c, b * CORES + c) for a, b in ed...  90.4 us
    ppermute x24, waiting for transfers between devices, swap(): return lax.ppermute(value, 'fsdp', [(j, j ^ bits) for j in range(count)])  65.5 us
    concatenate x1, local copies, waits for them, and re-layouts, on_device(): jnp.concatenate([upper_rim, projected], axis=0)  47.2 us
    dot_general x4, matrix products, on_device(): jnp.dot(lhs.reshape(planes * stage_rows, -1), weight, preferred_element_t...  38.7 us
    ppermute x1, starting transfers between devices, on_device(): upper_rim = lax.ppermute(projected[row_count - edge:], 'ctx', onward)  29.9 us
    ppermute x24, starting transfers between devices, swap(): return lax.ppermute(value, 'fsdp', [(j, j ^ bits) for j in range(count)])  25.4 us
    ppermute x1, starting transfers between devices, on_device(): gated_rim = lax.ppermute(last, 'ctx', onward)  20.3 us
  transfers between devices with their start and end apart: 63, of which 24 were waited for; matrix products, arithmetic and copies ran while one was open for 23% of the time, Pallas kernels for 0%

profile of v1, /device:TPU:1, one launch (start us, length us, event | category | flops | bytes accessed | tf_op | source)
XLA Modules:
  0.0 499.2 jit_solution(9313939141630609629)
XLA Ops:
  6.5 8.8 %copy.14 = bf16[1024,3,1024]{0,2,1:T(8,128)(2,1)} copy(bf16[1024,3,1024]{2,0,1:T(8,128)(2,1)} %param.11) | data formatting | bytes 12582912 | tf_op args[2]
  53.2 6.5 %collective-permute-start.51 = (bf16[32,2048]{1,0:T(8,128)(2,1)S(1)}, bf16[32,2048]{1,0:T(8,128)(2,1)S(1)}, u32[]{:S(2)}, u32[]{:S(2)}) collective-permute-start(bf16[32,2048]{1,0:T(8,128)(2,1)S(1)} %get-tuple-element.55), channel_id=1, source_target_pairs={{0,8},{4,12},{8,16},{12,20},{16,24},{20,28},{24,0},{28,4},{1,9},{5... | collective-permute-start | bytes 393224 | tf_op jit(solution)/shard_map/ppermute | solution.py:23
  59.7 5.7 %collective-permute-done.20 = bf16[32,2048]{1,0:T(8,128)(2,1)S(1)} collective-permute-done((bf16[32,2048]{1,0:T(8,128)(2,1)S(1)}, bf16[32,2048]{1,0:T(8,128)(2,1)S(1)}, u32[]{:S(2)}, u32[]{:S(2)}) %collective-permute-start.20) | collective-permute-done | bytes 131104 | tf_op jit(solution)/shard_map/ppermute | solution.py:23
  68.0 4.3 collective-permute-start.36
  73.6 4.9 collective-permute-done.49
  78.5 5.0 collective-permute-start.34
  96.3 4.2 collective-permute-done.22
  101.7 11.0 %collective-permute-done.54 = bf16[4,32,2048]{2,1,0:T(8,128)(2,1)} collective-permute-done((bf16[4,32,2048]{2,1,0:T(8,128)(2,1)}, bf16[4,32,2048]{2,1,0:T(8,128)(2,1)}, u32[]{:S(2)}, u32[]{:S(2)}) %collective-permute-start.54) | collective-permute-done | bytes 524320 | tf_op jit(solution)/shard_map/ppermute | solution.py:19
  117.4 5.6 %collective-permute-done.52 = bf16[4,32,2048]{2,1,0:T(8,128)(2,1)} collective-permute-done((bf16[4,32,2048]{2,1,0:T(8,128)(2,1)}, bf16[4,32,2048]{2,1,0:T(8,128)(2,1)}, u32[]{:S(2)}, u32[]{:S(2)}) %collective-permute-start.52) | collective-permute-done | bytes 524320 | tf_op jit(solution)/shard_map/ppermute | solution.py:19
  124.3 11.0 %collective-permute-done.39 = bf16[4,32,2048]{2,1,0:T(8,128)(2,1)} collective-permute-done((bf16[4,32,2048]{2,1,0:T(8,128)(2,1)}, bf16[4,32,2048]{2,1,0:T(8,128)(2,1)}, u32[]{:S(2)}, u32[]{:S(2)}) %collective-permute-start.39) | collective-permute-done | bytes 524320 | tf_op jit(solution)/shard_map/ppermute | solution.py:19
  139.6 5.9 %collective-permute-done.37 = bf16[4,32,2048]{2,1,0:T(8,128)(2,1)S(1)} collective-permute-done((bf16[4,32,2048]{2,1,0:T(8,128)(2,1)}, bf16[4,32,2048]{2,1,0:T(8,128)(2,1)S(1)}, u32[]{:S(2)}, u32[]{:S(2)}) %collective-permute-start.37) | collective-permute-done | bytes 524320 | tf_op jit(solution)/shard_map/ppermute | solution.py:19
  148.2 9.4 %collective-permute-done.8 = bf16[4,32,2048]{2,1,0:T(8,128)(2,1)S(1)} collective-permute-done((bf16[4,32,2048]{2,1,0:T(8,128)(2,1)S(1)}, bf16[4,32,2048]{2,1,0:T(8,128)(2,1)S(1)}, u32[]{:S(2)}, u32[]{:S(2)}) %collective-permute-start.8) | collective-permute-done | bytes 524320 | tf_op jit(solution)/shard_map/ppermute | solution.py:19
  159.3 8.7 %collective-permute-done.6 = bf16[4,32,2048]{2,1,0:T(8,128)(2,1)S(1)} collective-permute-done((bf16[4,32,2048]{2,1,0:T(8,128)(2,1)S(1)}, bf16[4,32,2048]{2,1,0:T(8,128)(2,1)S(1)}, u32[]{:S(2)}, u32[]{:S(2)}) %collective-permute-start.6) | collective-permute-done | bytes 524320 | tf_op jit(solution)/shard_map/ppermute | solution.py:19
  169.5 10.0 %fusion.63 = f32[512,3072]{1,0:T(8,128)S(1)} fusion(bf16[512,2048]{1,0:T(8,128)(2,1)} %bitcast.227, bf16[2048,3072]{0,1:T(8,128)(2,1)} %bitcast.275), kind=kOutput, calls=%fused_computation.192 | convolution fusion | flops 6442450944 | bytes 20971520 | tf_op jit(solution)/shard_map/dot_general | solution.py:109
  184.3 9.3 %fusion.64 = f32[512,3072]{1,0:T(8,128)S(1)} fusion(bf16[512,2048]{1,0:T(8,128)(2,1)S(1)} %bitcast.224, bf16[2048,3072]{0,1:T(8,128)(2,1)} %bitcast.276), kind=kOutput, calls=%fused_computation.193 | convolution fusion | flops 6442450944 | bytes 20971520 | tf_op jit(solution)/shard_map/dot_general | solution.py:109
  197.9 9.3 %fusion.66 = f32[512,3072]{1,0:T(8,128)S(1)} fusion(bf16[512,2048]{1,0:T(8,128)(2,1)S(1)} %bitcast.225, bf16[2048,3072]{0,1:T(8,128)(2,1)} %bitcast.277), kind=kOutput, calls=%fused_computation.195 | convolution fusion | flops 6442450944 | bytes 20971520 | tf_op jit(solution)/shard_map/dot_general | solution.py:109
  210.8 10.0 %fusion.65 = f32[512,3072]{1,0:T(8,128)S(1)} fusion(bf16[512,2048]{1,0:T(8,128)(2,1)} %bitcast.226, bf16[2048,3072]{0,1:T(8,128)(2,1)} %bitcast.278), kind=kOutput, calls=%fused_computation.194 | convolution fusion | flops 6442450944 | bytes 20971520 | tf_op jit(solution)/shard_map/dot_general | solution.py:109
  226.8 5.3 %collective-permute-done.55 = bf16[128,3072]{1,0:T(8,128)(2,1)} collective-permute-done((bf16[128,3072]{1,0:T(8,128)(2,1)}, bf16[128,3072]{1,0:T(8,128)(2,1)}, u32[]{:S(2)}, u32[]{:S(2)}) %collective-permute-start.55) | collective-permute-done | bytes 786464 | tf_op jit(solution)/shard_map/ppermute | solution.py:23
  237.6 11.3 %collective-permute-done.40 = bf16[128,3072]{1,0:T(8,128)(2,1)S(1)} collective-permute-done((bf16[128,3072]{1,0:T(8,128)(2,1)S(1)}, bf16[128,3072]{1,0:T(8,128)(2,1)S(1)}, u32[]{:S(2)}, u32[]{:S(2)}) %collective-permute-start.40) | collective-permute-done | bytes 786464 | tf_op jit(solution)/shard_map/ppermute | solution.py:23
  253.9 11.8 %collective-permute-done.10 = bf16[128,3072]{1,0:T(8,128)(2,1)S(1)} collective-permute-done((bf16[128,3072]{1,0:T(8,128)(2,1)S(1)}, bf16[128,3072]{1,0:T(8,128)(2,1)S(1)}, u32[]{:S(2)}, u32[]{:S(2)}) %collective-permute-start.10) | collective-permute-done | bytes 786464 | tf_op jit(solution)/shard_map/ppermute | solution.py:23
  272.3 10.3 %collective-permute-done.26 = bf16[128,3072]{1,0:T(8,128)(2,1)S(1)} collective-permute-done((bf16[128,3072]{1,0:T(8,128)(2,1)S(1)}, bf16[128,3072]{1,0:T(8,128)(2,1)S(1)}, u32[]{:S(2)}, u32[]{:S(2)}) %collective-permute-start.26) | collective-permute-done | bytes 786464 | tf_op jit(solution)/shard_map/ppermute | solution.py:23
  283.7 4.7 collective-permute-start.11
  288.5 10.9 %collective-permute-done.56 = bf16[128,3072]{1,0:T(8,128)(2,1)S(1)} collective-permute-done((bf16[128,3072]{1,0:T(8,128)(2,1)S(1)}, bf16[128,3072]{1,0:T(8,128)(2,1)S(1)}, u32[]{:S(2)}, u32[]{:S(2)}) %collective-permute-start.56) | collective-permute-done | bytes 786464 | tf_op jit(solution)/shard_map/ppermute | solution.py:23
  300.6 4.7 collective-permute-start.27
  305.3 10.9 %collective-permute-done.41 = bf16[128,3072]{1,0:T(8,128)(2,1)S(1)} collective-permute-done((bf16[128,3072]{1,0:T(8,128)(2,1)S(1)}, bf16[128,3072]{1,0:T(8,128)(2,1)S(1)}, u32[]{:S(2)}, u32[]{:S(2)}) %collective-permute-start.41) | collective-permute-done | bytes 786464 | tf_op jit(solution)/shard_map/ppermute | solution.py:23
  317.5 4.7 collective-permute-start.57
  325.1 29.2 %collective-permute-start.42 = (bf16[128,3072]{1,0:T(8,128)(2,1)S(1)}, bf16[128,3072]{1,0:T(8,128)(2,1)S(1)}, u32[]{:S(2)}, u32[]{:S(2)}) collective-permute-start(bf16[128,3072]{1,0:T(8,128)(2,1)S(1)} %get-tuple-element.19), channel_id=1, source_target_pairs={{0,8},{4,12},{8,16},{12,20},{16,24},{20,28},{1,9},{5,13},{9,17},{1... | collective-permute-start | bytes 2359304 | tf_op jit(solution)/shard_map/ppermute | solution.py:23
  358.6 8.5 %collective-permute-done.30 = bf16[128,3072]{1,0:T(8,128)(2,1)S(1)} collective-permute-done((bf16[128,3072]{1,0:T(8,128)(2,1)S(1)}, bf16[128,3072]{1,0:T(8,128)(2,1)S(1)}, u32[]{:S(2)}, u32[]{:S(2)}) %collective-permute-start.30) | collective-permute-done | bytes 786464 | tf_op jit(solution)/shard_map/ppermute | solution.py:23
  367.1 29.9 %collective-permute-start.15 = (bf16[2,3072]{1,0:T(2,128)(2,1)S(1)}, bf16[2,3072]{1,0:T(2,128)(2,1)S(1)}, u32[]{:S(2)}, u32[]{:S(2)}) collective-permute-start(bf16[2,3072]{1,0:T(2,128)(2,1)S(1)} %fusion.51), channel_id=1, source_target_pairs={{0,4},{4,8},{8,12},{12,16},{16,20},{20,24},{24,28},{1,5},{5,9},{9,... | collective-permute-start | bytes 36872 | tf_op jit(solution)/shard_map/ppermute | solution.py:134
  398.5 7.5 %collective-permute-done.45 = bf16[128,3072]{1,0:T(8,128)(2,1)S(1)} collective-permute-done((bf16[128,3072]{1,0:T(8,128)(2,1)S(1)}, bf16[128,3072]{1,0:T(8,128)(2,1)S(1)}, u32[]{:S(2)}, u32[]{:S(2)}) %collective-permute-start.45) | collective-permute-done | bytes 786464 | tf_op jit(solution)/shard_map/ppermute | solution.py:23
  410.8 20.3 %collective-permute-start.61 = (bf16[128,1024]{1,0:T(8,128)(2,1)}, bf16[128,1024]{1,0:T(8,128)(2,1)}, u32[]{:S(2)}, u32[]{:S(2)}) collective-permute-start(bf16[128,1024]{1,0:T(8,128)(2,1)} %fusion.48), channel_id=1, source_target_pairs={{0,4},{4,8},{8,12},{12,16},{16,20},{20,24},{24,28},{1,5},{5,9},{9,... | collective-permute-start | bytes 786440 | tf_op jit(solution)/shard_map/ppermute | solution.py:135
  431.1 47.2 %concatenate.11 = bf16[514,3072]{1,0:T(8,128)(2,1)} concatenate(bf16[2,3072]{1,0:T(2,128)(2,1)S(1)} %collective-permute-done.15, bf16[32,3072]{1,0:T(8,128)(2,1)S(1)} %get-tuple-element.51, bf16[32,3072]{1,0:T(8,128)(2,1)S(1)} %get-tuple-element.50, bf16[32,3072]{1,0:T(8,128)(2,1)S(1)} %get-tuple-element.49, bf16[32,3072]{1,0:T(8,128)(2,1)S(1)} %get-tuple-element.48, ...), dimensions={0} | concatenate | bytes 6316032 | tf_op jit(solution)/shard_map/concatenate | solution.py:136
  (218 shorter events, 137.9 us)
Async XLA Ops:
  6.5 163.0 %all-gather.2.cloned.1.call-start = ((), (), s32[]{:S(2)}) async-start(), calls=%async_computation | async-start | bytes 18874368 | tf_op jit(solution)/shard_map/all_gather | solution.py:86
  65.5 26.9 %collective-permute-start.24 = (bf16[4,32,2048]{2,1,0:T(8,128)(2,1)S(1)}, bf16[4,32,2048]{2,1,0:T(8,128)(2,1)S(1)}, u32[]{:S(2)}, u32[]{:S(2)}) collective-permute-start(bf16[4,32,2048]{2,1,0:T(8,128)(2,1)S(1)} %get-tuple-element.73), channel_id=1, source_target_pairs={{0,3},{1,2},{2,1},{3,0},{4,7},{5,6},{6,5},{7,4},{8,11},{9,10},{10,... | collective-permute-start | bytes 1572872 | tf_op jit(solution)/shard_map/ppermute | solution.py:19
  65.8 27.8 %collective-permute-start.23 = (bf16[4,32,2048]{2,1,0:T(8,128)(2,1)S(1)}, bf16[4,32,2048]{2,1,0:T(8,128)(2,1)S(1)}, u32[]{:S(2)}, u32[]{:S(2)}) collective-permute-start(bf16[4,32,2048]{2,1,0:T(8,128)(2,1)S(1)} %get-tuple-element.73), channel_id=1, source_target_pairs={{0,2},{1,3},{2,0},{3,1},{4,6},{5,7},{6,4},{7,5},{8,10},{9,11},{10,... | collective-permute-start | bytes 1572872 | tf_op jit(solution)/shard_map/ppermute | solution.py:19
  91.4 25.6 %collective-permute-start.53 = (bf16[4,32,2048]{2,1,0:T(8,128)(2,1)}, bf16[4,32,2048]{2,1,0:T(8,128)(2,1)}, u32[]{:S(2)}, u32[]{:S(2)}) collective-permute-start(bf16[4,32,2048]{2,1,0:T(8,128)(2,1)} %get-tuple-element.53), channel_id=1, source_target_pairs={{0,2},{1,3},{2,0},{3,1},{4,6},{5,7},{6,4},{7,5},{8,10},{9,11},{10,... | collective-permute-start | bytes 1572872 | tf_op jit(solution)/shard_map/ppermute | solution.py:19
  92.4 30.6 %collective-permute-start.52 = (bf16[4,32,2048]{2,1,0:T(8,128)(2,1)}, bf16[4,32,2048]{2,1,0:T(8,128)(2,1)}, u32[]{:S(2)}, u32[]{:S(2)}) collective-permute-start(bf16[4,32,2048]{2,1,0:T(8,128)(2,1)} %get-tuple-element.53), channel_id=1, source_target_pairs={{0,1},{1,0},{2,3},{3,2},{4,5},{5,4},{6,7},{7,6},{8,9},{9,8},{10,11... | collective-permute-start | bytes 1572872 | tf_op jit(solution)/shard_map/ppermute | solution.py:19
  94.4 40.8 %collective-permute-start.39 = (bf16[4,32,2048]{2,1,0:T(8,128)(2,1)}, bf16[4,32,2048]{2,1,0:T(8,128)(2,1)}, u32[]{:S(2)}, u32[]{:S(2)}) collective-permute-start(bf16[4,32,2048]{2,1,0:T(8,128)(2,1)} %get-tuple-element.63), channel_id=1, source_target_pairs={{0,3},{1,2},{2,1},{3,0},{4,7},{5,6},{6,5},{7,4},{8,11},{9,10},{10,... | collective-permute-start | bytes 1572872 | tf_op jit(solution)/shard_map/ppermute | solution.py:19
  100.5 39.1 %collective-permute-start.38 = (bf16[4,32,2048]{2,1,0:T(8,128)(2,1)}, bf16[4,32,2048]{2,1,0:T(8,128)(2,1)S(1)}, u32[]{:S(2)}, u32[]{:S(2)}) collective-permute-start(bf16[4,32,2048]{2,1,0:T(8,128)(2,1)} %get-tuple-element.63), channel_id=1, source_target_pairs={{0,2},{1,3},{2,0},{3,1},{4,6},{5,7},{6,4},{7,5},{8,10},{9,11},{10,... | collective-permute-start | bytes 1572872 | tf_op jit(solution)/shard_map/ppermute | solution.py:19
  112.7 32.7 %collective-permute-start.37 = (bf16[4,32,2048]{2,1,0:T(8,128)(2,1)}, bf16[4,32,2048]{2,1,0:T(8,128)(2,1)S(1)}, u32[]{:S(2)}, u32[]{:S(2)}) collective-permute-start(bf16[4,32,2048]{2,1,0:T(8,128)(2,1)} %get-tuple-element.63), channel_id=1, source_target_pairs={{0,1},{1,0},{2,3},{3,2},{4,5},{5,4},{6,7},{7,6},{8,9},{9,8},{10,11... | collective-permute-start | bytes 1572872 | tf_op jit(solution)/shard_map/ppermute | solution.py:19
  117.0 40.6 %collective-permute-start.8 = (bf16[4,32,2048]{2,1,0:T(8,128)(2,1)S(1)}, bf16[4,32,2048]{2,1,0:T(8,128)(2,1)S(1)}, u32[]{:S(2)}, u32[]{:S(2)}) collective-permute-start(bf16[4,32,2048]{2,1,0:T(8,128)(2,1)S(1)} %get-tuple-element.83), channel_id=1, source_target_pairs={{0,3},{1,2},{2,1},{3,0},{4,7},{5,6},{6,5},{7,4},{8,11},{9,10},{10,... | collective-permute-start | bytes 1572872 | tf_op jit(solution)/shard_map/ppermute | solution.py:19
  123.0 36.2 %collective-permute-start.7 = (bf16[4,32,2048]{2,1,0:T(8,128)(2,1)S(1)}, bf16[4,32,2048]{2,1,0:T(8,128)(2,1)S(1)}, u32[]{:S(2)}, u32[]{:S(2)}) collective-permute-start(bf16[4,32,2048]{2,1,0:T(8,128)(2,1)S(1)} %get-tuple-element.83), channel_id=1, source_target_pairs={{0,2},{1,3},{2,0},{3,1},{4,6},{5,7},{6,4},{7,5},{8,10},{9,11},{10,... | collective-permute-start | bytes 1572872 | tf_op jit(solution)/shard_map/ppermute | solution.py:19
  135.3 32.7 %collective-permute-start.6 = (bf16[4,32,2048]{2,1,0:T(8,128)(2,1)S(1)}, bf16[4,32,2048]{2,1,0:T(8,128)(2,1)S(1)}, u32[]{:S(2)}, u32[]{:S(2)}) collective-permute-start(bf16[4,32,2048]{2,1,0:T(8,128)(2,1)S(1)} %get-tuple-element.83), channel_id=1, source_target_pairs={{0,1},{1,0},{2,3},{3,2},{4,5},{5,4},{6,7},{7,6},{8,9},{9,8},{10,11... | collective-permute-start | bytes 1572872 | tf_op jit(solution)/shard_map/ppermute | solution.py:19
  180.9 40.2 %collective-permute-start.9 = (bf16[128,3072]{1,0:T(8,128)(2,1)}, bf16[128,3072]{1,0:T(8,128)(2,1)}, u32[]{:S(2)}, u32[]{:S(2)}) collective-permute-start(bf16[128,3072]{1,0:T(8,128)(2,1)} %get-tuple-element.29), channel_id=1, source_target_pairs={{0,8},{4,12},{1,9},{5,13},{2,10},{6,14},{3,11},{7,15}} | collective-permute-start | bytes 2359304 | tf_op jit(solution)/shard_map/ppermute | solution.py:23
  183.4 66.4 %collective-permute-start.12 = (bf16[128,3072]{1,0:T(8,128)(2,1)}, bf16[128,3072]{1,0:T(8,128)(2,1)S(1)}, u32[]{:S(2)}, u32[]{:S(2)}) collective-permute-start(bf16[128,3072]{1,0:T(8,128)(2,1)} %get-tuple-element.30), channel_id=1, source_target_pairs={{24,16},{28,20},{25,17},{29,21},{26,18},{30,22},{27,19},{31,23}} | collective-permute-start | bytes 2359304 | tf_op jit(solution)/shard_map/ppermute | solution.py:23
  195.0 29.0 %collective-permute-start.25 = (bf16[128,3072]{1,0:T(8,128)(2,1)}, bf16[128,3072]{1,0:T(8,128)(2,1)}, u32[]{:S(2)}, u32[]{:S(2)}) collective-permute-start(bf16[128,3072]{1,0:T(8,128)(2,1)} %get-tuple-element.25), channel_id=1, source_target_pairs={{0,8},{4,12},{1,9},{5,13},{2,10},{6,14},{3,11},{7,15}} | collective-permute-start | bytes 2359304 | tf_op jit(solution)/shard_map/ppermute | solution.py:23
  197.2 73.1 %collective-permute-start.28 = (bf16[128,3072]{1,0:T(8,128)(2,1)}, bf16[128,3072]{1,0:T(8,128)(2,1)S(1)}, u32[]{:S(2)}, u32[]{:S(2)}) collective-permute-start(bf16[128,3072]{1,0:T(8,128)(2,1)} %get-tuple-element.26), channel_id=1, source_target_pairs={{24,16},{28,20},{25,17},{29,21},{26,18},{30,22},{27,19},{31,23}} | collective-permute-start | bytes 2359304 | tf_op jit(solution)/shard_map/ppermute | solution.py:23
  221.1 62.6 %collective-permute-start.58 = (bf16[128,3072]{1,0:T(8,128)(2,1)}, bf16[128,3072]{1,0:T(8,128)(2,1)S(1)}, u32[]{:S(2)}, u32[]{:S(2)}) collective-permute-start(bf16[128,3072]{1,0:T(8,128)(2,1)} %get-tuple-element.18), channel_id=1, source_target_pairs={{24,16},{28,20},{25,17},{29,21},{26,18},{30,22},{27,19},{31,23}} | collective-permute-start | bytes 2359304 | tf_op jit(solution)/shard_map/ppermute | solution.py:23
  224.0 24.9 %collective-permute-start.40 = (bf16[128,3072]{1,0:T(8,128)(2,1)S(1)}, bf16[128,3072]{1,0:T(8,128)(2,1)S(1)}, u32[]{:S(2)}, u32[]{:S(2)}) collective-permute-start(bf16[128,3072]{1,0:T(8,128)(2,1)S(1)} %get-tuple-element.21), channel_id=1, source_target_pairs={{0,8},{4,12},{1,9},{5,13},{2,10},{6,14},{3,11},{7,15}} | collective-permute-start | bytes 2359304 | tf_op jit(solution)/shard_map/ppermute | solution.py:23
  232.1 33.6 %collective-permute-start.10 = (bf16[128,3072]{1,0:T(8,128)(2,1)S(1)}, bf16[128,3072]{1,0:T(8,128)(2,1)S(1)}, u32[]{:S(2)}, u32[]{:S(2)}) collective-permute-start(bf16[128,3072]{1,0:T(8,128)(2,1)S(1)} %add_convert_fusion.15), channel_id=1, source_target_pairs={{0,8},{4,12},{8,16},{12,20},{1,9},{5,13},{9,17},{13,21},{2,10},{6,... | collective-permute-start | bytes 2359304 | tf_op jit(solution)/shard_map/ppermute | solution.py:23
  248.8 51.8 %collective-permute-start.43 = (bf16[128,3072]{1,0:T(8,128)(2,1)S(1)}, bf16[128,3072]{1,0:T(8,128)(2,1)S(1)}, u32[]{:S(2)}, u32[]{:S(2)}) collective-permute-start(bf16[128,3072]{1,0:T(8,128)(2,1)S(1)} %get-tuple-element.22), channel_id=1, source_target_pairs={{24,16},{28,20},{25,17},{29,21},{26,18},{30,22},{27,19},{31,23}} | collective-permute-start | bytes 2359304 | tf_op jit(solution)/shard_map/ppermute | solution.py:23
  249.8 32.8 %collective-permute-start.26 = (bf16[128,3072]{1,0:T(8,128)(2,1)S(1)}, bf16[128,3072]{1,0:T(8,128)(2,1)S(1)}, u32[]{:S(2)}, u32[]{:S(2)}) collective-permute-start(bf16[128,3072]{1,0:T(8,128)(2,1)S(1)} %add_convert_fusion.11), channel_id=1, source_target_pairs={{0,8},{4,12},{8,16},{12,20},{1,9},{5,13},{9,17},{13,21},{2,10},{6,... | collective-permute-start | bytes 2359304 | tf_op jit(solution)/shard_map/ppermute | solution.py:23
  265.7 33.7 %collective-permute-start.56 = (bf16[128,3072]{1,0:T(8,128)(2,1)S(1)}, bf16[128,3072]{1,0:T(8,128)(2,1)S(1)}, u32[]{:S(2)}, u32[]{:S(2)}) collective-permute-start(bf16[128,3072]{1,0:T(8,128)(2,1)S(1)} %add_convert_fusion.3), channel_id=1, source_target_pairs={{0,8},{4,12},{8,16},{12,20},{1,9},{5,13},{9,17},{13,21},{2,10},{6,... | collective-permute-start | bytes 2359304 | tf_op jit(solution)/shard_map/ppermute | solution.py:23
  270.3 45.9 %collective-permute-start.41 = (bf16[128,3072]{1,0:T(8,128)(2,1)S(1)}, bf16[128,3072]{1,0:T(8,128)(2,1)S(1)}, u32[]{:S(2)}, u32[]{:S(2)}) collective-permute-start(bf16[128,3072]{1,0:T(8,128)(2,1)S(1)} %add_convert_fusion.7), channel_id=1, source_target_pairs={{0,8},{4,12},{8,16},{12,20},{1,9},{5,13},{9,17},{13,21},{2,10},{6,... | collective-permute-start | bytes 2359304 | tf_op jit(solution)/shard_map/ppermute | solution.py:23
  282.5 34.9 %collective-permute-start.13 = (bf16[128,3072]{1,0:T(8,128)(2,1)S(1)}, bf16[128,3072]{1,0:T(8,128)(2,1)S(1)}, u32[]{:S(2)}, u32[]{:S(2)}) collective-permute-start(bf16[128,3072]{1,0:T(8,128)(2,1)S(1)} %get-tuple-element.28), channel_id=1, source_target_pairs={{16,8},{20,12},{24,16},{28,20},{17,9},{21,13},{25,17},{29,21},{18,... | collective-permute-start | bytes 2359304 | tf_op jit(solution)/shard_map/ppermute | solution.py:23
  283.7 70.7 %collective-permute-start.11 = (bf16[128,3072]{1,0:T(8,128)(2,1)S(1)}, bf16[128,3072]{1,0:T(8,128)(2,1)S(1)}, u32[]{:S(2)}, u32[]{:S(2)}) collective-permute-start(bf16[128,3072]{1,0:T(8,128)(2,1)S(1)} %get-tuple-element.27), channel_id=1, source_target_pairs={{0,8},{4,12},{8,16},{12,20},{16,24},{20,28},{1,9},{5,13},{9,17},{1... | collective-permute-start | bytes 2359304 | tf_op jit(solution)/shard_map/ppermute | solution.py:23
  300.6 56.7 %collective-permute-start.27 = (bf16[128,3072]{1,0:T(8,128)(2,1)S(1)}, bf16[128,3072]{1,0:T(8,128)(2,1)S(1)}, u32[]{:S(2)}, u32[]{:S(2)}) collective-permute-start(bf16[128,3072]{1,0:T(8,128)(2,1)S(1)} %get-tuple-element.23), channel_id=1, source_target_pairs={{0,8},{4,12},{8,16},{12,20},{16,24},{20,28},{1,9},{5,13},{9,17},{1... | collective-permute-start | bytes 2359304 | tf_op jit(solution)/shard_map/ppermute | solution.py:23
  317.5 79.9 %collective-permute-start.57 = (bf16[128,3072]{1,0:T(8,128)(2,1)S(1)}, bf16[128,3072]{1,0:T(8,128)(2,1)S(1)}, u32[]{:S(2)}, u32[]{:S(2)}) collective-permute-start(bf16[128,3072]{1,0:T(8,128)(2,1)S(1)} %get-tuple-element.15), channel_id=1, source_target_pairs={{0,8},{4,12},{8,16},{12,20},{16,24},{20,28},{1,9},{5,13},{9,17},{1... | collective-permute-start | bytes 2359304 | tf_op jit(solution)/shard_map/ppermute | solution.py:23
  323.3 32.4 %collective-permute-start.14 = (bf16[128,3072]{1,0:T(8,128)(2,1)S(1)}, bf16[128,3072]{1,0:T(8,128)(2,1)S(1)}, u32[]{:S(2)}, u32[]{:S(2)}) collective-permute-start(bf16[128,3072]{1,0:T(8,128)(2,1)S(1)} %add_convert_fusion.12), channel_id=1, source_target_pairs={{8,0},{12,4},{16,8},{20,12},{24,16},{28,20},{9,1},{13,5},{17,9},{2... | collective-permute-start | bytes 2359304 | tf_op jit(solution)/shard_map/ppermute | solution.py:23
  325.1 73.4 %collective-permute-start.42 = (bf16[128,3072]{1,0:T(8,128)(2,1)S(1)}, bf16[128,3072]{1,0:T(8,128)(2,1)S(1)}, u32[]{:S(2)}, u32[]{:S(2)}) collective-permute-start(bf16[128,3072]{1,0:T(8,128)(2,1)S(1)} %get-tuple-element.19), channel_id=1, source_target_pairs={{0,8},{4,12},{8,16},{12,20},{16,24},{20,28},{1,9},{5,13},{9,17},{1... | collective-permute-start | bytes 2359304 | tf_op jit(solution)/shard_map/ppermute | solution.py:23
  355.7 41.7 %collective-permute-start.60 = (bf16[128,3072]{1,0:T(8,128)(2,1)S(1)}, bf16[128,3072]{1,0:T(8,128)(2,1)S(1)}, u32[]{:S(2)}, u32[]{:S(2)}) collective-permute-start(bf16[128,3072]{1,0:T(8,128)(2,1)S(1)} %add_convert_fusion), channel_id=1, source_target_pairs={{8,0},{12,4},{16,8},{20,12},{24,16},{28,20},{9,1},{13,5},{17,9},{2... | collective-permute-start | bytes 2359304 | tf_op jit(solution)/shard_map/ppermute | solution.py:23
  357.3 48.7 %collective-permute-start.45 = (bf16[128,3072]{1,0:T(8,128)(2,1)S(1)}, bf16[128,3072]{1,0:T(8,128)(2,1)S(1)}, u32[]{:S(2)}, u32[]{:S(2)}) collective-permute-start(bf16[128,3072]{1,0:T(8,128)(2,1)S(1)} %add_convert_fusion.4), channel_id=1, source_target_pairs={{8,0},{12,4},{16,8},{20,12},{24,16},{28,20},{9,1},{13,5},{17,9},{2... | collective-permute-start | bytes 2359304 | tf_op jit(solution)/shard_map/ppermute | solution.py:23
  367.1 64.0 %collective-permute-start.15 = (bf16[2,3072]{1,0:T(2,128)(2,1)S(1)}, bf16[2,3072]{1,0:T(2,128)(2,1)S(1)}, u32[]{:S(2)}, u32[]{:S(2)}) collective-permute-start(bf16[2,3072]{1,0:T(2,128)(2,1)S(1)} %fusion.51), channel_id=1, source_target_pairs={{0,4},{4,8},{8,12},{12,16},{16,20},{20,24},{24,28},{1,5},{5,9},{9,... | collective-permute-start | bytes 36872 | tf_op jit(solution)/shard_map/ppermute | solution.py:134
  410.8 72.5 %collective-permute-start.61 = (bf16[128,1024]{1,0:T(8,128)(2,1)}, bf16[128,1024]{1,0:T(8,128)(2,1)}, u32[]{:S(2)}, u32[]{:S(2)}) collective-permute-start(bf16[128,1024]{1,0:T(8,128)(2,1)} %fusion.48), channel_id=1, source_target_pairs={{0,4},{4,8},{8,12},{12,16},{16,20},{20,24},{24,28},{1,5},{5,9},{9,... | collective-permute-start | bytes 786440 | tf_op jit(solution)/shard_map/ppermute | solution.py:135
  (50 other events, 605.0 us)
Sparse Core Ops, SparseCore 0:
  15.5 27.3 all-gather.1

commit v2 on v0

v2 whole, which is shorter than its diff:
```python
import jax
import jax.numpy as jnp
import numpy as np
from jax import lax
from jax.experimental import pallas as pl
from jax.experimental.pallas import tpu as pltpu
from jax.sharding import PartitionSpec as P

CORES = 2
EPS = 1e-06
STAGES = (3, 5)
ROUNDS = (((0, 0), (1, 1), (2, 2), (3, 3), 4), ((1, 1), (2, 3), (4, 4), (5, 5), 6))
LANES = 128


def pick(stack, index):
    return lax.dynamic_index_in_dim(stack, index, 0, keepdims=False)


def swap(value, count, bits):
    if bits == 0:
        return value
    return lax.ppermute(value, "fsdp", [(j, j ^ bits) for j in range(count)])


def plane_shift(value, edges):
    return lax.ppermute(
        value, "ctx", [(a * CORES + c, b * CORES + c) for a, b in edges for c in range(CORES)]
    )


def dft_matrices(length, taps):
    bins = length // 2 + 1
    room = -(-bins // 8) * 8
    k = np.arange(bins)[:, None]
    angle = 2.0 * np.pi * ((k * np.arange(length)[None, :]) % length) / length
    weight = np.where((k == 0) | (k == length // 2), 1.0, 2.0) / length
    analysis = np.zeros((2, room, length))
    synthesis = np.zeros((2, room, length))
    analysis[:, :bins] = np.stack([np.cos(angle), -np.sin(angle)])
    synthesis[:, :bins] = np.stack([weight * np.cos(angle), -weight * np.sin(angle)])
    return (
        analysis.reshape(2 * room, length).astype(np.float32),
        synthesis.reshape(2 * room, length)[:, taps:].T.astype(np.float32),
    )


def tile(*extents):
    return 2 * LANES if all(e % (2 * LANES) == 0 for e in extents) else LANES


def halves(value):
    high = value.astype(jnp.bfloat16)
    return high, (value - high.astype(jnp.float32)).astype(jnp.bfloat16)


def dot(a, b):
    return jnp.dot(a, b, preferred_element_type=jnp.float32)


def finish_kernel(
    query, key, value, query_rim, key_rim, value_rim, gated_rim, short, long,
    analysis_high, analysis_low, synthesis_high, synthesis_low, out, extended, signal,
):
    row_count = out.shape[0]
    taps = long.shape[0]
    room = analysis_high.shape[0] // 2
    reach = short.shape[0]
    for b, (body, rim) in enumerate(((query, query_rim), (key, key_rim), (value, value_rim))):
        extended[b, :8] = rim[rim.shape[0] - 8 :].astype(jnp.float32)
        extended[b, 8:] = body[...].astype(jnp.float32)

    def featurized(b, start, count):
        result = None
        for s in range(reach):
            term = short[s, b : b + 1, :] * extended[b, 8 + start - s : 8 + start - s + count]
            result = term if result is None else result + term
        return result

    signal[:taps] = gated_rim[...]
    for start in range(0, row_count, taps):
        gated = featurized(1, start, taps) * featurized(2, start, taps)
        signal[taps + start : 2 * taps + start] = gated.astype(jnp.bfloat16)

    long_high, long_low = halves(long[...])
    tones = (
        dot(analysis_high[:, :taps], long_high)
        + dot(analysis_high[:, :taps], long_low)
        + dot(analysis_low[:, :taps], long_high)
    )
    for start in range(0, row_count, taps):
        block = signal[start : start + 2 * taps]
        spectrum = dot(analysis_high[...], block) + dot(analysis_low[...], block)
        real = spectrum[:room] * tones[:room] - spectrum[room:] * tones[room:]
        imag = spectrum[:room] * tones[room:] + spectrum[room:] * tones[:room]
        high, low = halves(jnp.concatenate([real, imag], axis=0))
        response = (
            dot(synthesis_high[...], high)
            + dot(synthesis_high[...], low)
            + dot(synthesis_low[...], high)
        )
        out[start : start + taps] = (featurized(0, start, taps) * response).astype(out.dtype)


def finish(projected, rim, gated_rim, short_filter, long_filter):
    row_count = projected.shape[0]
    taps, channels = long_filter.shape
    width = tile(channels)
    count = channels // width
    analysis, synthesis = (jnp.asarray(m) for m in dft_matrices(2 * taps, taps))
    constants = (*halves(analysis), *halves(synthesis))

    def branch(rows, b):
        return pl.BlockSpec((rows, width), lambda i, b=b: (0, b * count + i))

    operands = [*[projected] * 3, *[rim] * 3, gated_rim, short_filter, long_filter, *constants]
    specs = (
        [branch(row_count, b) for b in range(3)]
        + [branch(rim.shape[0], b) for b in range(3)]
        + [
            pl.BlockSpec((taps, width), lambda i: (0, i)),
            pl.BlockSpec((short_filter.shape[0], 3, width), lambda i: (0, 0, i)),
            pl.BlockSpec((taps, width), lambda i: (0, i)),
        ]
        + [pl.BlockSpec(m.shape, lambda i: (0, 0)) for m in constants]
    )
    return pl.pallas_call(
        finish_kernel,
        out_shape=jax.ShapeDtypeStruct((row_count, channels), jnp.bfloat16),
        grid=(count,),
        in_specs=specs,
        out_specs=pl.BlockSpec((row_count, width), lambda i: (0, i)),
        scratch_shapes=[
            pltpu.VMEM((3, 8 + row_count, width), jnp.float32),
            pltpu.VMEM((taps + row_count, width), jnp.bfloat16),
        ],
        compiler_params=pltpu.CompilerParams(vmem_limit_bytes=32 * 1024 * 1024),
        cost_estimate=pl.CostEstimate(
            flops=row_count * channels * 5000, bytes_accessed=row_count * channels * 10, transcendentals=0
        ),
    )(*operands)


def passed_along(value):
    count = lax.axis_size("ctx")
    return lax.ppermute(value, "ctx", [(i, i + 1) for i in range(count - 1)])


def rims(last_rows, short_filter, long_count):
    reach = short_filter.shape[0]
    channels = short_filter.shape[2]
    total = last_rows.shape[0]
    mixed = []
    for b in (1, 2):
        rows = last_rows[:, b * channels : (b + 1) * channels].astype(jnp.float32)
        mixed.append(
            sum(
                short_filter[s, b] * rows[total - long_count - s : total - s] for s in range(reach)
            )
        )
    gated = (mixed[0] * mixed[1]).astype(jnp.bfloat16)
    return passed_along(last_rows[total - 16 :]), passed_along(gated)


def together(values):
    leaves, tree = jax.tree.flatten(values)
    anywhere = pl.BlockSpec(memory_space=pl.ANY)
    leaves = pl.pallas_call(
        lambda *refs: None,
        out_shape=[jax.ShapeDtypeStruct(leaf.shape, leaf.dtype) for leaf in leaves],
        in_specs=[anywhere] * len(leaves),
        out_specs=[anywhere] * len(leaves),
        input_output_aliases={at: at for at in range(len(leaves))},
    )(*leaves)
    return jax.tree.unflatten(tree, leaves)


def spread_near(value, columns):
    if columns != 4:
        return [swap(value, columns, t) for t in range(1, columns)]
    return [swap(value, columns, 1), swap(value, columns, 2)]


def spread_far(near, columns):
    if columns != 4:
        return []
    half = near[0].shape[-1] // 2
    return [swap(near[1][..., :half], columns, 1), swap(near[0][..., half:], columns, 2)]


def spread_all(value, near, far):
    return [value, *near] + ([jnp.concatenate(far, axis=-1)] if far else [])


def partial_kernel(column, *refs):
    *lefts, own, other, out, joined = refs
    planes, columns, share, depth = joined.shape

    @pl.when(pl.program_id(0) == 0)
    def _():
        for t, left in enumerate(lefts):
            joined[:, column[0] ^ t] = left[...]

    rows = joined[...].reshape(planes * columns * share, depth)
    half = depth // 2
    out[...] = dot(rows[:, :half], own[0]) + dot(rows[:, half:], other[0])


def partial_sums(column, lefts, part, parts, own, other):
    planes, share, depth = lefts[0].shape
    planes = planes // parts
    columns = len(lefts)
    late = own.shape[2]
    rows = planes * columns * share
    weights = pl.BlockSpec((1, own.shape[1], late), lambda b, _: (b, 0, 0))
    return pl.pallas_call(
        partial_kernel,
        out_shape=jax.ShapeDtypeStruct((rows, 3 * late), jnp.float32),
        grid_spec=pltpu.PrefetchScalarGridSpec(
            num_scalar_prefetch=1,
            grid=(3,),
            in_specs=[pl.BlockSpec((planes, share, depth), lambda b, _: (part, 0, 0))] * columns
            + [weights, weights],
            out_specs=pl.BlockSpec((rows, late), lambda b, _: (0, b)),
            scratch_shapes=[pltpu.VMEM((planes, columns, share, depth), jnp.bfloat16)],
        ),
        compiler_params=pltpu.CompilerParams(vmem_limit_bytes=48 * 1024 * 1024),
        cost_estimate=pl.CostEstimate(
            flops=2 * rows * depth * 3 * late,
            bytes_accessed=2 * rows * depth + 6 * depth * late + 12 * rows * late,
            transcendentals=0,
        ),
    )(column, *lefts, own, other).reshape(planes, columns * share, 3 * late)


def on_device(tokens, gain, in_weight, short_filter, long_filter):
    planes = lax.axis_size("ctx") // CORES
    columns = lax.axis_size("fsdp")
    plane = lax.axis_index("ctx") // CORES
    core = lax.axis_index("ctx") % CORES
    column = lax.axis_index("fsdp")
    place = jnp.stack([column, plane]).astype(jnp.int32)
    row_count, width = tokens.shape
    long_count = long_filter.shape[0]

    parts = STAGES
    if row_count % (sum(parts) * columns * 16):
        parts = (1, 1)
    unit = row_count // sum(parts)
    sizes = [unit * part for part in parts]
    stages = [(row_count - sizes[0], sizes[0]), (0, sizes[1])]

    own_weight = jnp.transpose(in_weight, (1, 0, 2))
    other_weight = lax.ppermute(
        own_weight,
        "ctx",
        [(p * CORES + c, p * CORES + 1 - c) for p in range(planes) for c in range(CORES)],
    )
    gains = gain.reshape(columns, width)
    gain_here = jnp.stack([pick(gains, column ^ t) for t in range(columns)])[:, None, :]

    def to_trade(stage):
        start, size = stages[stage]
        own = tokens[start : start + size].reshape(columns, -1, width)
        return [pick(own, column ^ t) for t in range(columns)]

    def trade(pieces):
        return [swap(piece, columns, t) for t, piece in enumerate(pieces)]

    def normalize(wide):
        wide = jnp.stack(wide).astype(jnp.float32)
        mean_square = jnp.sum(wide * wide, axis=(0, 2), keepdims=True) / (columns * width)
        return (wide * lax.rsqrt(mean_square + EPS) * gain_here).astype(jnp.bfloat16)

    def turned(normed):
        return jnp.where(core == 0, normed, jnp.roll(normed, width // 2, axis=2))

    def to_planes(normed):
        rows_of = [None] * planes
        for d in range(planes):
            piece = pick(normed, column ^ ((plane + d) % planes))
            if d > 0:
                piece = plane_shift(piece, [(p, (p + d) % planes) for p in range(planes)])
            rows_of[(planes - d) % planes] = piece
        return rows_of

    def send_weights(step, right, left):
        return (
            plane_shift(right, [(p, p + 1) for p in range(planes - 1) if p >= step - 1]),
            plane_shift(left, [(p, p - 1) for p in range(1, planes) if p <= planes - step]),
        )

    def onward(term, arrived):
        if arrived is not None:
            term = term + arrived.astype(jnp.float32)
        return term.astype(jnp.bfloat16)

    def send_sums(step, terms, sums):
        right, left = sums
        return (
            plane_shift(
                onward(terms[planes - step], right),
                [(p, p + 1) for p in range(planes - 1) if p < step],
            ),
            plane_shift(
                onward(terms[step], left),
                [(p, p - 1) for p in range(1, planes) if p >= planes - step],
            ),
        )

    count, steps = len(stages), planes - 1
    order = [m for k in range(1, planes // 2) for m in (planes - k, k)] + [planes // 2, 0]
    last = max(at[4] for at in ROUNDS) + steps - 1
    live = {f"pieces{stage}": to_trade(stage) for stage in range(count)}
    own, normed, terms, totals, flying = {}, {}, {}, {}, {}

    for now in range(last + 1):
        for stage, (to_shares, across, near, far, first) in enumerate(ROUNDS):
            if now == to_shares[0]:
                flying[f"trade{stage}"] = to_shares[1], trade(live.pop(f"pieces{stage}"))
            if now == across[0]:
                normed[stage] = turned(normalize(live.pop(f"trade{stage}")))
                flying[f"planes{stage}"] = across[1], to_planes(normed[stage])
            if now == near[0]:
                pieces = live.pop(f"planes{stage}")
                own[stage] = jnp.stack([pieces[m] for m in order])
                flying[f"near{stage}"] = near[1], spread_near(own[stage], columns)
            if now == far[0]:
                flying[f"far{stage}"] = far[1], spread_far(live[f"near{stage}"], columns)
            if now == first:
                lefts = spread_all(
                    own[stage], live.pop(f"near{stage}"), live.pop(f"far{stage}")
                )
                products = [
                    product[m]
                    for half in range(2)
                    for product in [
                        partial_sums(place, lefts, half, 2, own_weight, other_weight)
                    ]
                    for m in range(planes // 2)
                ]
                terms[stage] = [products[order.index(m)] for m in range(planes)]
                live[f"sums{stage}"] = (None, None)
            if first <= now < first + steps:
                sums = live.pop(f"sums{stage}")
                flying[f"sums{stage}"] = now, send_sums(now - first + 1, terms[stage], sums)
        for name in [name for name, (end, _) in flying.items() if end == now]:
            live[name] = flying.pop(name)[1]
        live = together(live) if now < last else live
        for stage in range(count):
            if now == ROUNDS[stage][4] + steps - 1:
                right, left = live.pop(f"sums{stage}")
                total = terms[stage][0] + right.astype(jnp.float32) + left.astype(jnp.float32)
                totals[stage] = total.astype(jnp.bfloat16)

    rim, gated_rim = rims(totals[0], short_filter, long_count)
    projected = jnp.concatenate([totals[1], totals[0]], axis=0)
    return finish(projected, rim, gated_rim, short_filter, long_filter)


def solution(mesh):
    return jax.shard_map(
        on_device,
        mesh=mesh,
        in_specs=(
            P("ctx", "fsdp"),
            P(),
            P("ctx", None, "fsdp"),
            P(None, None, "fsdp"),
            P(None, "fsdp"),
        ),
        out_specs=P("ctx", "fsdp"),
        check_vma=False,
    )
```

time: 666 us -> 379 us (0.57)
  waiting for transfers between devices: 510 us -> 192 us
  starting transfers between devices: 4.43 us -> 75.4 us
  Pallas kernels: 0 us -> 55.6 us
  other arithmetic: 76.1 us -> 29.3 us
  matrix products: 33.9 us -> 0 us
  between operations: 13.5 us -> 0.84 us
    all_gather x2 -> x0, waiting for transfers between devices: 508 us -> none  [the longest x1 424 us: on_device(): panel_rows = lax.all_gather(in_weight, 'ctx', axis=0, tiled=True)]
    ppermute x2 -> x35, waiting for transfers between devices: 1.84 us -> 192 us  [the longest x18 156 us: plane_shift(): lax.ppermute(value, 'ctx', [(a * CORES + c, b * CORES + c) for a, b in ed...]
    ppermute x2 -> x35, starting transfers between devices: 4.39 us -> 75.4 us  [the longest x18 51.7 us: plane_shift(): lax.ppermute(value, 'ctx', [(a * CORES + c, b * CORES + c) for a, b in ed...]
    add x9 -> x0, other arithmetic: 62.8 us -> none  [the longest x8 60.9 us: group_step(): accumulated = accumulated + tap_weights * window_rows]
    pallas_call x0 -> x13, Pallas kernels: none -> 55.6 us  [the longest x4 48.1 us: partial_sums(): pl.pallas_call(partial_kernel, out_shape=jax.ShapeDtypeStruct((rows, 3 *...]
    dot_general x1 -> x0, matrix products: 33.9 us -> none  [on_device(): jnp.dot(normed, panel_rows.reshape(panel_rows.shape[0], 3 * channels), pr...]
    convert_element_type x4 -> x10, other arithmetic: 8.21 us -> 21.8 us  [the longest x4 17.9 us: onward(): return term.astype(jnp.bfloat16)]
    dynamic_slice x8 -> x1, local copies, waits for them, and re-layouts: 10.3 us -> 0.04 us  [pick(): return lax.dynamic_index_in_dim(stack, index, 0, keepdims=False)]
  transfers between devices with their start and end apart: 4 -> 35, of which waited for: 4 -> 18; matrix products, arithmetic and copies ran while one was open for 2% -> 6% of each run, Pallas kernels for 0% -> 9%
where the time goes in v2:
time: 379 us; the launch traced here: 378 us
  waiting for transfers between devices  192 us (51%)
  starting transfers between devices  75.4 us (20%)
  Pallas kernels  55.6 us (15%)
  other arithmetic  29.3 us (8%)
  local copies, waits for them, and re-layouts  25 us (7%)
    ppermute x18, waiting for transfers between devices, plane_shift(): lax.ppermute(value, 'ctx', [(a * CORES + c, b * CORES + c) for a, b in ed...  156 us
    ppermute x18, starting transfers between devices, plane_shift(): lax.ppermute(value, 'ctx', [(a * CORES + c, b * CORES + c) for a, b in ed...  51.7 us
    pallas_call x4, Pallas kernels, partial_sums(): pl.pallas_call(partial_kernel, out_shape=jax.ShapeDtypeStruct((rows, 3 *...  48.1 us
    ppermute x14, waiting for transfers between devices, swap(): return lax.ppermute(value, 'fsdp', [(j, j ^ bits) for j in range(count)])  36.1 us
    convert_element_type x4, other arithmetic, onward(): return term.astype(jnp.bfloat16)  17.9 us
    ppermute x14, starting transfers between devices, swap(): return lax.ppermute(value, 'fsdp', [(j, j ^ bits) for j in range(count)])  16.2 us
    unnamed x126, local copies, waits for them, and re-layouts  9.1 us
    slice x2, local copies, waits for them, and re-layouts, on_device(): product[m]  7.95 us
  transfers between devices with their start and end apart: 35, of which 18 were waited for; matrix products, arithmetic and copies ran while one was open for 6% of the time, Pallas kernels for 9%

profile of v2, /device:TPU:0, one launch (start us, length us, event | category | flops | bytes accessed | tf_op | source)
XLA Modules:
  0.0 378.2 jit_solution(17985002748810712411)
XLA Ops:
  1.9 3.9 %collective-permute-start.2 = (bf16[48,2048]{1,0:T(8,128)(2,1)S(1)}, bf16[48,2048]{1,0:T(8,128)(2,1)S(1)}, u32[]{:S(2)}, u32[]{:S(2)}) collective-permute-start(bf16[48,2048]{1,0:T(8,128)(2,1)S(1)} %get-tuple-element.119), channel_id=1, source_target_pairs={{0,3},{1,2},{2,1},{3,0},{4,7},{5,6},{6,5},{7,4},{8,11},{9,10},{10,... | collective-permute-start | bytes 589832 | tf_op jit(solution)/shard_map/ppermute | solution.py:23
  7.6 4.0 %collective-permute-done.2.refs_7_ = bf16[48,2048]{1,0:T(8,128)(2,1)S(1)} collective-permute-done((bf16[48,2048]{1,0:T(8,128)(2,1)S(1)}, bf16[48,2048]{1,0:T(8,128)(2,1)S(1)}, u32[]{:S(2)}, u32[]{:S(2)}) %collective-permute-start.2) | collective-permute-done | bytes 196640 | tf_op jit(solution)/shard_map/ppermute | solution.py:23
  11.6 3.3 collective-permute-done.1.refs_6_
  26.7 3.2 collective-permute-done.5.refs_3_
  31.5 5.8 %collective-permute-done.4.refs_2_ = bf16[48,2048]{1,0:T(8,128)(2,1)S(1)} collective-permute-done((bf16[48,2048]{1,0:T(8,128)(2,1)S(1)}, bf16[48,2048]{1,0:T(8,128)(2,1)S(1)}, u32[]{:S(2)}, u32[]{:S(2)}) %collective-permute-start.4) | collective-permute-done | bytes 196640 | tf_op jit(solution)/shard_map/ppermute | solution.py:27
  39.0 5.2 %collective-permute-done.3.refs_1_ = bf16[48,2048]{1,0:T(8,128)(2,1)S(1)} collective-permute-done((bf16[48,2048]{1,0:T(8,128)(2,1)S(1)}, bf16[48,2048]{1,0:T(8,128)(2,1)S(1)}, u32[]{:S(2)}, u32[]{:S(2)}) %collective-permute-start.3) | collective-permute-done | bytes 196640 | tf_op jit(solution)/shard_map/ppermute | solution.py:27
  52.1 13.1 %collective-permute-done.10.refs_1_ = bf16[4,48,2048]{2,1,0:T(8,128)(2,1)S(1)} collective-permute-done((bf16[4,48,2048]{2,1,0:T(8,128)(2,1)S(1)}, bf16[4,48,2048]{2,1,0:T(8,128)(2,1)S(1)}, u32[]{:S(2)}, u32[]{:S(2)}) %collective-permute-start.10) | collective-permute-done | bytes 786464 | tf_op jit(solution)/shard_map/ppermute | solution.py:23
  73.5 12.6 %collective-permute-done.14.refs_6_ = bf16[80,2048]{1,0:T(8,128)(2,1)S(1)} collective-permute-done((bf16[80,2048]{1,0:T(8,128)(2,1)S(1)}, bf16[80,2048]{1,0:T(8,128)(2,1)S(1)}, u32[]{:S(2)}, u32[]{:S(2)}) %collective-permute-start.14) | collective-permute-done | bytes 327712 | tf_op jit(solution)/shard_map/ppermute | solution.py:27
  91.1 10.5 %shard_map.77 = f32[384,3072]{1,0:T(8,128)} custom-call(s32[2]{0:T(128)S(1)} %pad_add_fusion.column, bf16[4,48,2048]{2,1,0:T(8,128)(2,1)S(1)} %pad_maximum_fusion.4.refs_0_, bf16[4,48,2048]{2,1,0:T(8,128)(2,1)S(1)} %copy-done.3, bf16[4,48,2048]{2,1,0:T(8,128)(2,1)S(1)} %copy-done.1, bf16[4,48,2048]{2,1,0:T(8,128)(2,1)S(1)} %constant_dynamic-update-slice_fusion.refs_3_, ...), custom_call_target="tpu_custom_call" | custom-call | flops 4831838208 | bytes 18874368 | tf_op jit(solution)/shard_map/pallas_call | solution.py:216
  106.0 9.8 %collective-permute-start.19 = (bf16[192,3072]{1,0:T(8,128)(2,1)S(1)}, bf16[192,3072]{1,0:T(8,128)(2,1)}, u32[]{:S(2)}, u32[]{:S(2)}) collective-permute-start(bf16[192,3072]{1,0:T(8,128)(2,1)S(1)} %get-tuple-element.100), channel_id=1, source_target_pairs={{0,8},{4,12},{1,9},{5,13},{2,10},{6,14},{3,11},{7,15}} | collective-permute-start | bytes 3538952 | tf_op jit(solution)/shard_map/ppermute | solution.py:27
  115.7 10.4 %shard_map.79 = f32[384,3072]{1,0:T(8,128)} custom-call(s32[2]{0:T(128)S(1)} %pad_add_fusion.column, bf16[4,48,2048]{2,1,0:T(8,128)(2,1)S(1)} %pad_maximum_fusion.4.refs_0_, bf16[4,48,2048]{2,1,0:T(8,128)(2,1)S(1)} %copy-done.3, bf16[4,48,2048]{2,1,0:T(8,128)(2,1)S(1)} %copy-done.1, bf16[4,48,2048]{2,1,0:T(8,128)(2,1)S(1)} %constant_dynamic-update-slice_fusion.refs_3_, ...), custom_call_target="tpu_custom_call" | custom-call | flops 4831838208 | bytes 18874368 | tf_op jit(solution)/shard_map/pallas_call | solution.py:216
  126.2 13.0 %collective-permute-done.19.refs_2_ = bf16[192,3072]{1,0:T(8,128)(2,1)} collective-permute-done((bf16[192,3072]{1,0:T(8,128)(2,1)S(1)}, bf16[192,3072]{1,0:T(8,128)(2,1)}, u32[]{:S(2)}, u32[]{:S(2)}) %collective-permute-start.19) | collective-permute-done | bytes 1179680 | tf_op jit(solution)/shard_map/ppermute | solution.py:27
  139.2 3.1 add_convert_fusion.6
  143.1 6.1 %collective-permute-start.23 = (bf16[192,3072]{1,0:T(8,128)(2,1)S(1)}, bf16[192,3072]{1,0:T(8,128)(2,1)}, u32[]{:S(2)}, u32[]{:S(2)}) collective-permute-start(bf16[192,3072]{1,0:T(8,128)(2,1)S(1)} %get-tuple-element.98), channel_id=1, source_target_pairs={{0,8},{4,12},{8,16},{12,20},{1,9},{5,13},{9,17},{13,21},{2,10},{6,... | collective-permute-start | bytes 3538952 | tf_op jit(solution)/shard_map/ppermute | solution.py:27
  151.4 12.6 %collective-permute-done.22.refs_1_ = bf16[4,80,1024]{2,1,0:T(8,128)(2,1)S(1)} collective-permute-done((bf16[4,80,1024]{2,1,0:T(8,128)(2,1)S(1)}, bf16[4,80,1024]{2,1,0:T(8,128)(2,1)S(1)}, u32[]{:S(2)}, u32[]{:S(2)}) %collective-permute-start.22) | collective-permute-done | bytes 655392 | tf_op jit(solution)/shard_map/ppermute | solution.py:23
  166.3 5.4 %collective-permute-done.23.refs_4_ = bf16[192,3072]{1,0:T(8,128)(2,1)} collective-permute-done((bf16[192,3072]{1,0:T(8,128)(2,1)S(1)}, bf16[192,3072]{1,0:T(8,128)(2,1)}, u32[]{:S(2)}, u32[]{:S(2)}) %collective-permute-start.23) | collective-permute-done | bytes 1179680 | tf_op jit(solution)/shard_map/ppermute | solution.py:27
  174.3 13.8 %shard_map.82 = f32[640,3072]{1,0:T(8,128)} custom-call(s32[2]{0:T(128)S(1)} %pad_add_fusion.column, bf16[4,80,2048]{2,1,0:T(8,128)(2,1)S(1)} %copy-done.11, bf16[4,80,2048]{2,1,0:T(8,128)(2,1)S(1)} %copy-done.9, bf16[4,80,2048]{2,1,0:T(8,128)(2,1)S(1)} %copy-done.6, bf16[4,80,2048]{2,1,0:T(8,128)(2,1)S(1)} %constant_dynamic-update-slice_fusion.2.refs_3_, ...), custom_call_target="tpu_custom_call" | custom-call | flops 8053063680 | bytes 23068672 | tf_op jit(solution)/shard_map/pallas_call | solution.py:216
  188.1 5.2 %fusion.16 = (bf16[320,3072]{1,0:T(8,128)(2,1)}, bf16[320,3072]{1,0:T(8,128)(2,1)S(1)}) fusion(f32[640,3072]{1,0:T(8,128)} %shard_map.82), kind=kLoop, calls=%fused_computation.77 | loop fusion | bytes 7864320 | tf_op jit(solution)/shard_map/slice | solution.py:335
  194.1 5.9 %collective-permute-start.27 = (bf16[320,3072]{1,0:T(8,128)(2,1)S(1)}, bf16[320,3072]{1,0:T(8,128)(2,1)}, u32[]{:S(2)}, u32[]{:S(2)}) collective-permute-start(bf16[320,3072]{1,0:T(8,128)(2,1)S(1)} %get-tuple-element.94), channel_id=1, source_target_pairs={{0,8},{4,12},{1,9},{5,13},{2,10},{6,14},{3,11},{7,15}} | collective-permute-start | bytes 5898248 | tf_op jit(solution)/shard_map/ppermute | solution.py:27
  200.0 3.0 add_convert_fusion.4
  204.3 4.6 %collective-permute-start.25 = (bf16[192,3072]{1,0:T(8,128)(2,1)S(1)}, bf16[192,3072]{1,0:T(8,128)(2,1)S(1)}, u32[]{:S(2)}, u32[]{:S(2)}) collective-permute-start(bf16[192,3072]{1,0:T(8,128)(2,1)S(1)} %get-tuple-element.96), channel_id=1, source_target_pairs={{0,8},{4,12},{8,16},{12,20},{16,24},{20,28},{1,9},{5,13},{9,17},{1... | collective-permute-start | bytes 3538952 | tf_op jit(solution)/shard_map/ppermute | solution.py:27
  209.0 13.4 %shard_map.81 = f32[640,3072]{1,0:T(8,128)} custom-call(s32[2]{0:T(128)S(1)} %pad_add_fusion.column, bf16[4,80,2048]{2,1,0:T(8,128)(2,1)S(1)} %copy-done.11, bf16[4,80,2048]{2,1,0:T(8,128)(2,1)S(1)} %copy-done.9, bf16[4,80,2048]{2,1,0:T(8,128)(2,1)S(1)} %copy-done.6, bf16[4,80,2048]{2,1,0:T(8,128)(2,1)S(1)} %constant_dynamic-update-slice_fusion.2.refs_3_, ...), custom_call_target="tpu_custom_call" | custom-call | flops 8053063680 | bytes 23068672 | tf_op jit(solution)/shard_map/pallas_call | solution.py:216
  222.4 7.6 %collective-permute-done.26.refs_1_ = bf16[192,3072]{1,0:T(8,128)(2,1)S(1)} collective-permute-done((bf16[192,3072]{1,0:T(8,128)(2,1)}, bf16[192,3072]{1,0:T(8,128)(2,1)S(1)}, u32[]{:S(2)}, u32[]{:S(2)}) %collective-permute-start.26) | collective-permute-done | bytes 1179680 | tf_op jit(solution)/shard_map/ppermute | solution.py:27
  230.0 33.4 %collective-permute-done.25.refs_0_ = bf16[192,3072]{1,0:T(8,128)(2,1)S(1)} collective-permute-done((bf16[192,3072]{1,0:T(8,128)(2,1)S(1)}, bf16[192,3072]{1,0:T(8,128)(2,1)S(1)}, u32[]{:S(2)}, u32[]{:S(2)}) %collective-permute-start.25) | collective-permute-done | bytes 1179680 | tf_op jit(solution)/shard_map/ppermute | solution.py:27
  265.7 4.5 %add_convert_fusion.2 = (bf16[320,3072]{1,0:T(8,128)(2,1)S(1)}, bf16[320,3072]{1,0:T(8,128)(2,1)S(1)}) fusion(bf16[320,3072]{1,0:T(8,128)(2,1)} %get-tuple-element.84, f32[640,3072]{1,0:T(8,128)} %shard_map.81, bf16[320,3072]{1,0:T(8,128)(2,1)} %get-tuple-element.83), kind=kLoop, calls=%fused_computation.5 | loop fusion | flops 5898240 | bytes 11796480 | tf_op jit(solution)/shard_map/convert_element_type | solution.py:296
  271.1 6.2 %collective-permute-start.29 = (bf16[320,3072]{1,0:T(8,128)(2,1)S(1)}, bf16[320,3072]{1,0:T(8,128)(2,1)}, u32[]{:S(2)}, u32[]{:S(2)}) collective-permute-start(bf16[320,3072]{1,0:T(8,128)(2,1)S(1)} %get-tuple-element.92), channel_id=1, source_target_pairs={{0,8},{4,12},{8,16},{12,20},{1,9},{5,13},{9,17},{13,21},{2,10},{6,... | collective-permute-start | bytes 5898248 | tf_op jit(solution)/shard_map/ppermute | solution.py:27
  277.2 37.3 %collective-permute-done.29.refs_0_ = bf16[320,3072]{1,0:T(8,128)(2,1)} collective-permute-done((bf16[320,3072]{1,0:T(8,128)(2,1)S(1)}, bf16[320,3072]{1,0:T(8,128)(2,1)}, u32[]{:S(2)}, u32[]{:S(2)}) %collective-permute-start.29) | collective-permute-done | bytes 1966112 | tf_op jit(solution)/shard_map/ppermute | solution.py:27
  314.6 7.3 %add_convert_fusion.1 = (bf16[320,3072]{1,0:T(8,128)(2,1)}, bf16[320,3072]{1,0:T(8,128)(2,1)S(1)}) fusion(bf16[320,3072]{1,0:T(8,128)(2,1)} %get-tuple-element.85, f32[640,3072]{1,0:T(8,128)} %shard_map.82, bf16[320,3072]{1,0:T(8,128)(2,1)} %get-tuple-element.86), kind=kLoop, calls=%fused_computation.4 | loop fusion | flops 5898240 | bytes 15728640 | tf_op jit(solution)/shard_map/convert_element_type | solution.py:296
  321.8 4.9 %collective-permute-start.31 = (bf16[320,3072]{1,0:T(8,128)(2,1)}, bf16[320,3072]{1,0:T(8,128)(2,1)S(1)}, u32[]{:S(2)}, u32[]{:S(2)}) collective-permute-start(bf16[320,3072]{1,0:T(8,128)(2,1)} %get-tuple-element.89), channel_id=1, source_target_pairs={{0,8},{4,12},{8,16},{12,20},{16,24},{20,28},{1,9},{5,13},{9,17},{1... | collective-permute-start | bytes 5898248 | tf_op jit(solution)/shard_map/ppermute | solution.py:27
  330.5 5.7 %collective-permute-start.34 = (bf16[128,1024]{1,0:T(8,128)(2,1)S(1)}, bf16[128,1024]{1,0:T(8,128)(2,1)S(1)}, u32[]{:S(2)}, u32[]{:S(2)}) collective-permute-start(bf16[128,1024]{1,0:T(8,128)(2,1)S(1)} %fusion.12), channel_id=1, source_target_pairs={{0,4},{4,8},{8,12},{12,16},{16,20},{20,24},{24,28},{1,5},{5,9},{9,... | collective-permute-start | bytes 786440 | tf_op jit(solution)/shard_map/ppermute | solution.py:146
  336.2 32.2 %collective-permute-done.31 = bf16[320,3072]{1,0:T(8,128)(2,1)S(1)} collective-permute-done((bf16[320,3072]{1,0:T(8,128)(2,1)}, bf16[320,3072]{1,0:T(8,128)(2,1)S(1)}, u32[]{:S(2)}, u32[]{:S(2)}) %collective-permute-start.31) | collective-permute-done | bytes 1966112 | tf_op jit(solution)/shard_map/ppermute | solution.py:27
  370.8 7.4 %shard_map.85 = bf16[512,1024]{1,0:T(8,128)(2,1)} custom-call(bf16[512,3072]{1,0:T(8,128)(2,1)S(1)} %pad_maximum_fusion.query.key.value, bf16[512,3072]{1,0:T(8,128)(2,1)S(1)} %pad_maximum_fusion.query.key.value, bf16[512,3072]{1,0:T(8,128)(2,1)S(1)} %pad_maximum_fusion.query.key.value, ...), custom_call_target="tpu_custom_call" | custom-call | flops 2621440000 | bytes 5242880 | tf_op jit(solution)/shard_map/pallas_call | solution.py:127
  (223 shorter events, 62.9 us)
Async XLA Ops:
  0.0 91.0 %collective-permute-start.18 = (bf16[3,1024,1024]{2,1,0:T(8,128)(2,1)}, bf16[3,1024,1024]{2,1,0:T(8,128)(2,1)}, u32[]{:S(2)}, u32[]{:S(2)}) collective-permute-start(bf16[3,1024,1024]{2,1,0:T(8,128)(2,1)} %bitcast.61), channel_id=1, source_target_pairs={{0,4},{4,0},{8,12},{12,8},{16,20},{20,16},{24,28},{28,24},{1,5},{5... | collective-permute-start | bytes 18874376 | tf_op jit(solution)/shard_map/ppermute | solution.py:254
  1.9 9.7 %collective-permute-start.2 = (bf16[48,2048]{1,0:T(8,128)(2,1)S(1)}, bf16[48,2048]{1,0:T(8,128)(2,1)S(1)}, u32[]{:S(2)}, u32[]{:S(2)}) collective-permute-start(bf16[48,2048]{1,0:T(8,128)(2,1)S(1)} %get-tuple-element.119), channel_id=1, source_target_pairs={{0,3},{1,2},{2,1},{3,0},{4,7},{5,6},{6,5},{7,4},{8,11},{9,10},{10,... | collective-permute-start | bytes 589832 | tf_op jit(solution)/shard_map/ppermute | solution.py:23
  5.8 9.1 %collective-permute-start.1 = (bf16[48,2048]{1,0:T(8,128)(2,1)S(1)}, bf16[48,2048]{1,0:T(8,128)(2,1)S(1)}, u32[]{:S(2)}, u32[]{:S(2)}) collective-permute-start(bf16[48,2048]{1,0:T(8,128)(2,1)S(1)} %get-tuple-element.120), channel_id=1, source_target_pairs={{0,2},{1,3},{2,0},{3,1},{4,6},{5,7},{6,4},{7,5},{8,10},{9,11},{10,... | collective-permute-start | bytes 589832 | tf_op jit(solution)/shard_map/ppermute | solution.py:23
  20.2 9.7 %collective-permute-start.5 = (bf16[48,2048]{1,0:T(8,128)(2,1)S(1)}, bf16[48,2048]{1,0:T(8,128)(2,1)S(1)}, u32[]{:S(2)}, u32[]{:S(2)}) collective-permute-start(bf16[48,2048]{1,0:T(8,128)(2,1)S(1)} %get-tuple-element.113), channel_id=1, source_target_pairs={{0,8},{4,12},{8,16},{12,20},{16,24},{20,28},{24,0},{28,4},{1,9},{5... | collective-permute-start | bytes 589832 | tf_op jit(solution)/shard_map/ppermute | solution.py:27
  21.8 15.5 %collective-permute-start.4 = (bf16[48,2048]{1,0:T(8,128)(2,1)S(1)}, bf16[48,2048]{1,0:T(8,128)(2,1)S(1)}, u32[]{:S(2)}, u32[]{:S(2)}) collective-permute-start(bf16[48,2048]{1,0:T(8,128)(2,1)S(1)} %get-tuple-element.114), channel_id=1, source_target_pairs={{0,16},{4,20},{8,24},{12,28},{16,0},{20,4},{24,8},{28,12},{1,17},{... | collective-permute-start | bytes 589832 | tf_op jit(solution)/shard_map/ppermute | solution.py:27
  24.4 19.8 %collective-permute-start.6 = (bf16[80,2048]{1,0:T(8,128)(2,1)S(1)}, bf16[80,2048]{1,0:T(8,128)(2,1)S(1)}, u32[]{:S(2)}, u32[]{:S(2)}) collective-permute-start(bf16[80,2048]{1,0:T(8,128)(2,1)S(1)} %copy-done.51), channel_id=1, source_target_pairs={{0,1},{1,0},{2,3},{3,2},{4,5},{5,4},{6,7},{7,6},{8,9},{9,8},{10,11... | collective-permute-start | bytes 983048 | tf_op jit(solution)/shard_map/ppermute | solution.py:23
  25.9 18.3 %collective-permute-start.7 = (bf16[80,2048]{1,0:T(8,128)(2,1)S(1)}, bf16[80,2048]{1,0:T(8,128)(2,1)S(1)}, u32[]{:S(2)}, u32[]{:S(2)}) collective-permute-start(bf16[80,2048]{1,0:T(8,128)(2,1)S(1)} %copy-done.50), channel_id=1, source_target_pairs={{0,2},{1,3},{2,0},{3,1},{4,6},{5,7},{6,4},{7,5},{8,10},{9,11},{10,... | collective-permute-start | bytes 983048 | tf_op jit(solution)/shard_map/ppermute | solution.py:23
  29.9 14.3 %collective-permute-start.8 = (bf16[80,2048]{1,0:T(8,128)(2,1)S(1)}, bf16[80,2048]{1,0:T(8,128)(2,1)S(1)}, u32[]{:S(2)}, u32[]{:S(2)}) collective-permute-start(bf16[80,2048]{1,0:T(8,128)(2,1)S(1)} %copy-done.49), channel_id=1, source_target_pairs={{0,3},{1,2},{2,1},{3,0},{4,7},{5,6},{6,5},{7,4},{8,11},{9,10},{10,... | collective-permute-start | bytes 983048 | tf_op jit(solution)/shard_map/ppermute | solution.py:23
  46.6 18.7 %collective-permute-start.10 = (bf16[4,48,2048]{2,1,0:T(8,128)(2,1)S(1)}, bf16[4,48,2048]{2,1,0:T(8,128)(2,1)S(1)}, u32[]{:S(2)}, u32[]{:S(2)}) collective-permute-start(bf16[4,48,2048]{2,1,0:T(8,128)(2,1)S(1)} %pad_maximum_fusion.4.refs_0_), channel_id=1, source_target_pairs={{0,2},{1,3},{2,0},{3,1},{4,6},{5,7},{6,4},{7,5},{8,10},{9,11},{10,... | collective-permute-start | bytes 2359304 | tf_op jit(solution)/shard_map/ppermute | solution.py:23
  48.2 18.3 %collective-permute-start.9 = (bf16[4,48,2048]{2,1,0:T(8,128)(2,1)S(1)}, bf16[4,48,2048]{2,1,0:T(8,128)(2,1)S(1)}, u32[]{:S(2)}, u32[]{:S(2)}) collective-permute-start(bf16[4,48,2048]{2,1,0:T(8,128)(2,1)S(1)} %pad_maximum_fusion.4.refs_0_), channel_id=1, source_target_pairs={{0,1},{1,0},{2,3},{3,2},{4,5},{5,4},{6,7},{7,6},{8,9},{9,8},{10,11... | collective-permute-start | bytes 2359304 | tf_op jit(solution)/shard_map/ppermute | solution.py:23
  52.1 19.4 %collective-permute-start.15 = (bf16[80,2048]{1,0:T(8,128)(2,1)}, bf16[80,2048]{1,0:T(8,128)(2,1)S(1)}, u32[]{:S(2)}, u32[]{:S(2)}) collective-permute-start(bf16[80,2048]{1,0:T(8,128)(2,1)} %get-tuple-element.101), channel_id=1, source_target_pairs={{0,8},{4,12},{8,16},{12,20},{16,24},{20,28},{24,0},{28,4},{1,9},{5... | collective-permute-start | bytes 983048 | tf_op jit(solution)/shard_map/ppermute | solution.py:27
  69.4 16.7 %collective-permute-start.12 = (bf16[4,48,1024]{2,1,0:T(8,128)(2,1)S(1)}, bf16[4,48,1024]{2,1,0:T(8,128)(2,1)S(1)}, u32[]{:S(2)}, u32[]{:S(2)}) collective-permute-start(bf16[4,48,1024]{2,1,0:T(8,128)(2,1)S(1)} %slice.116), channel_id=1, source_target_pairs={{0,2},{1,3},{2,0},{3,1},{4,6},{5,7},{6,4},{7,5},{8,10},{9,11},{10,... | collective-permute-start | bytes 1179656 | tf_op jit(solution)/shard_map/ppermute | solution.py:23
  70.7 15.4 %collective-permute-start.11 = (bf16[4,48,1024]{2,1,0:T(8,128)(2,1)S(1)}, bf16[4,48,1024]{2,1,0:T(8,128)(2,1)S(1)}, u32[]{:S(2)}, u32[]{:S(2)}) collective-permute-start(bf16[4,48,1024]{2,1,0:T(8,128)(2,1)S(1)} %slice.115), channel_id=1, source_target_pairs={{0,1},{1,0},{2,3},{3,2},{4,5},{5,4},{6,7},{7,6},{8,9},{9,8},{10,11... | collective-permute-start | bytes 1179656 | tf_op jit(solution)/shard_map/ppermute | solution.py:23
  71.5 14.6 %collective-permute-start.14 = (bf16[80,2048]{1,0:T(8,128)(2,1)S(1)}, bf16[80,2048]{1,0:T(8,128)(2,1)S(1)}, u32[]{:S(2)}, u32[]{:S(2)}) collective-permute-start(bf16[80,2048]{1,0:T(8,128)(2,1)S(1)} %get-tuple-element.102), channel_id=1, source_target_pairs={{0,16},{4,20},{8,24},{12,28},{16,0},{20,4},{24,8},{28,12},{1,17},{... | collective-permute-start | bytes 983048 | tf_op jit(solution)/shard_map/ppermute | solution.py:27
  71.5 14.6 %collective-permute-start.13 = (bf16[80,2048]{1,0:T(8,128)(2,1)S(1)}, bf16[80,2048]{1,0:T(8,128)(2,1)S(1)}, u32[]{:S(2)}, u32[]{:S(2)}) collective-permute-start(bf16[80,2048]{1,0:T(8,128)(2,1)S(1)} %get-tuple-element.103), channel_id=1, source_target_pairs={{0,24},{4,28},{8,0},{12,4},{16,8},{20,12},{24,16},{28,20},{1,25},{... | collective-permute-start | bytes 983048 | tf_op jit(solution)/shard_map/ppermute | solution.py:27
  88.8 37.3 %collective-permute-start.17 = (bf16[4,80,2048]{2,1,0:T(8,128)(2,1)S(1)}, bf16[4,80,2048]{2,1,0:T(8,128)(2,1)S(1)}, u32[]{:S(2)}, u32[]{:S(2)}) collective-permute-start(bf16[4,80,2048]{2,1,0:T(8,128)(2,1)S(1)} %pad_maximum_fusion.2.refs_0_), channel_id=1, source_target_pairs={{0,2},{1,3},{2,0},{3,1},{4,6},{5,7},{6,4},{7,5},{8,10},{9,11},{10,... | collective-permute-start | bytes 3932168 | tf_op jit(solution)/shard_map/ppermute | solution.py:23
  90.1 36.1 %collective-permute-start.16 = (bf16[4,80,2048]{2,1,0:T(8,128)(2,1)S(1)}, bf16[4,80,2048]{2,1,0:T(8,128)(2,1)S(1)}, u32[]{:S(2)}, u32[]{:S(2)}) collective-permute-start(bf16[4,80,2048]{2,1,0:T(8,128)(2,1)S(1)} %pad_maximum_fusion.2.refs_0_), channel_id=1, source_target_pairs={{0,1},{1,0},{2,3},{3,2},{4,5},{5,4},{6,7},{7,6},{8,9},{9,8},{10,11... | collective-permute-start | bytes 3932168 | tf_op jit(solution)/shard_map/ppermute | solution.py:23
  104.3 21.9 %collective-permute-start.20 = (bf16[192,3072]{1,0:T(8,128)(2,1)S(1)}, bf16[192,3072]{1,0:T(8,128)(2,1)}, u32[]{:S(2)}, u32[]{:S(2)}) collective-permute-start(bf16[192,3072]{1,0:T(8,128)(2,1)S(1)} %get-tuple-element.99), channel_id=1, source_target_pairs={{24,16},{28,20},{25,17},{29,21},{26,18},{30,22},{27,19},{31,23}} | collective-permute-start | bytes 3538952 | tf_op jit(solution)/shard_map/ppermute | solution.py:27
  106.0 33.2 %collective-permute-start.19 = (bf16[192,3072]{1,0:T(8,128)(2,1)S(1)}, bf16[192,3072]{1,0:T(8,128)(2,1)}, u32[]{:S(2)}, u32[]{:S(2)}) collective-permute-start(bf16[192,3072]{1,0:T(8,128)(2,1)S(1)} %get-tuple-element.100), channel_id=1, source_target_pairs={{0,8},{4,12},{1,9},{5,13},{2,10},{6,14},{3,11},{7,15}} | collective-permute-start | bytes 3538952 | tf_op jit(solution)/shard_map/ppermute | solution.py:27
  142.4 23.1 %collective-permute-start.24 = (bf16[192,3072]{1,0:T(8,128)(2,1)S(1)}, bf16[192,3072]{1,0:T(8,128)(2,1)S(1)}, u32[]{:S(2)}, u32[]{:S(2)}) collective-permute-start(bf16[192,3072]{1,0:T(8,128)(2,1)S(1)} %get-tuple-element.97), channel_id=1, source_target_pairs={{16,8},{20,12},{24,16},{28,20},{17,9},{21,13},{25,17},{29,21},{18,... | collective-permute-start | bytes 3538952 | tf_op jit(solution)/shard_map/ppermute | solution.py:27
  143.1 28.6 %collective-permute-start.23 = (bf16[192,3072]{1,0:T(8,128)(2,1)S(1)}, bf16[192,3072]{1,0:T(8,128)(2,1)}, u32[]{:S(2)}, u32[]{:S(2)}) collective-permute-start(bf16[192,3072]{1,0:T(8,128)(2,1)S(1)} %get-tuple-element.98), channel_id=1, source_target_pairs={{0,8},{4,12},{8,16},{12,20},{1,9},{5,13},{9,17},{13,21},{2,10},{6,... | collective-permute-start | bytes 3538952 | tf_op jit(solution)/shard_map/ppermute | solution.py:27
  149.3 14.7 %collective-permute-start.22 = (bf16[4,80,1024]{2,1,0:T(8,128)(2,1)S(1)}, bf16[4,80,1024]{2,1,0:T(8,128)(2,1)S(1)}, u32[]{:S(2)}, u32[]{:S(2)}) collective-permute-start(bf16[4,80,1024]{2,1,0:T(8,128)(2,1)S(1)} %slice.122), channel_id=1, source_target_pairs={{0,2},{1,3},{2,0},{3,1},{4,6},{5,7},{6,4},{7,5},{8,10},{9,11},{10,... | collective-permute-start | bytes 1966088 | tf_op jit(solution)/shard_map/ppermute | solution.py:23
  151.1 14.4 %collective-permute-start.21 = (bf16[4,80,1024]{2,1,0:T(8,128)(2,1)S(1)}, bf16[4,80,1024]{2,1,0:T(8,128)(2,1)S(1)}, u32[]{:S(2)}, u32[]{:S(2)}) collective-permute-start(bf16[4,80,1024]{2,1,0:T(8,128)(2,1)S(1)} %slice.121), channel_id=1, source_target_pairs={{0,1},{1,0},{2,3},{3,2},{4,5},{5,4},{6,7},{7,6},{8,9},{9,8},{10,11... | collective-permute-start | bytes 1966088 | tf_op jit(solution)/shard_map/ppermute | solution.py:23
  193.3 70.1 %collective-permute-start.28 = (bf16[320,3072]{1,0:T(8,128)(2,1)}, bf16[320,3072]{1,0:T(8,128)(2,1)S(1)}, u32[]{:S(2)}, u32[]{:S(2)}) collective-permute-start(bf16[320,3072]{1,0:T(8,128)(2,1)} %get-tuple-element.93), channel_id=1, source_target_pairs={{24,16},{28,20},{25,17},{29,21},{26,18},{30,22},{27,19},{31,23}} | collective-permute-start | bytes 5898248 | tf_op jit(solution)/shard_map/ppermute | solution.py:27
  194.1 70.3 %collective-permute-start.27 = (bf16[320,3072]{1,0:T(8,128)(2,1)S(1)}, bf16[320,3072]{1,0:T(8,128)(2,1)}, u32[]{:S(2)}, u32[]{:S(2)}) collective-permute-start(bf16[320,3072]{1,0:T(8,128)(2,1)S(1)} %get-tuple-element.94), channel_id=1, source_target_pairs={{0,8},{4,12},{1,9},{5,13},{2,10},{6,14},{3,11},{7,15}} | collective-permute-start | bytes 5898248 | tf_op jit(solution)/shard_map/ppermute | solution.py:27
  203.1 26.9 %collective-permute-start.26 = (bf16[192,3072]{1,0:T(8,128)(2,1)}, bf16[192,3072]{1,0:T(8,128)(2,1)S(1)}, u32[]{:S(2)}, u32[]{:S(2)}) collective-permute-start(bf16[192,3072]{1,0:T(8,128)(2,1)} %get-tuple-element.95), channel_id=1, source_target_pairs={{8,0},{12,4},{16,8},{20,12},{24,16},{28,20},{9,1},{13,5},{17,9},{2... | collective-permute-start | bytes 3538952 | tf_op jit(solution)/shard_map/ppermute | solution.py:27
  204.3 59.1 %collective-permute-start.25 = (bf16[192,3072]{1,0:T(8,128)(2,1)S(1)}, bf16[192,3072]{1,0:T(8,128)(2,1)S(1)}, u32[]{:S(2)}, u32[]{:S(2)}) collective-permute-start(bf16[192,3072]{1,0:T(8,128)(2,1)S(1)} %get-tuple-element.96), channel_id=1, source_target_pairs={{0,8},{4,12},{8,16},{12,20},{16,24},{20,28},{1,9},{5,13},{9,17},{1... | collective-permute-start | bytes 3538952 | tf_op jit(solution)/shard_map/ppermute | solution.py:27
  271.1 43.5 %collective-permute-start.29 = (bf16[320,3072]{1,0:T(8,128)(2,1)S(1)}, bf16[320,3072]{1,0:T(8,128)(2,1)}, u32[]{:S(2)}, u32[]{:S(2)}) collective-permute-start(bf16[320,3072]{1,0:T(8,128)(2,1)S(1)} %get-tuple-element.92), channel_id=1, source_target_pairs={{0,8},{4,12},{8,16},{12,20},{1,9},{5,13},{9,17},{13,21},{2,10},{6,... | collective-permute-start | bytes 5898248 | tf_op jit(solution)/shard_map/ppermute | solution.py:27
  321.8 46.6 %collective-permute-start.31 = (bf16[320,3072]{1,0:T(8,128)(2,1)}, bf16[320,3072]{1,0:T(8,128)(2,1)S(1)}, u32[]{:S(2)}, u32[]{:S(2)}) collective-permute-start(bf16[320,3072]{1,0:T(8,128)(2,1)} %get-tuple-element.89), channel_id=1, source_target_pairs={{0,8},{4,12},{8,16},{12,20},{16,24},{20,28},{1,9},{5,13},{9,17},{1... | collective-permute-start | bytes 5898248 | tf_op jit(solution)/shard_map/ppermute | solution.py:27
  326.7 42.0 %collective-permute-start.32 = (bf16[320,3072]{1,0:T(8,128)(2,1)S(1)}, bf16[320,3072]{1,0:T(8,128)(2,1)S(1)}, u32[]{:S(2)}, u32[]{:S(2)}) collective-permute-start(bf16[320,3072]{1,0:T(8,128)(2,1)S(1)} %get-tuple-element.90), channel_id=1, source_target_pairs={{8,0},{12,4},{16,8},{20,12},{24,16},{28,20},{9,1},{13,5},{17,9},{2... | collective-permute-start | bytes 5898248 | tf_op jit(solution)/shard_map/ppermute | solution.py:27
  328.6 41.2 %collective-permute-start.33 = (bf16[16,3072]{1,0:T(8,128)(2,1)S(1)}, bf16[16,3072]{1,0:T(8,128)(2,1)S(1)}, u32[]{:S(2)}, u32[]{:S(2)}) collective-permute-start(bf16[16,3072]{1,0:T(8,128)(2,1)S(1)} %slice.156), channel_id=1, source_target_pairs={{0,4},{4,8},{8,12},{12,16},{16,20},{20,24},{24,28},{1,5},{5,9},{9,... | collective-permute-start | bytes 294920 | tf_op jit(solution)/shard_map/ppermute | solution.py:146
  330.5 39.4 %collective-permute-start.34 = (bf16[128,1024]{1,0:T(8,128)(2,1)S(1)}, bf16[128,1024]{1,0:T(8,128)(2,1)S(1)}, u32[]{:S(2)}, u32[]{:S(2)}) collective-permute-start(bf16[128,1024]{1,0:T(8,128)(2,1)S(1)} %fusion.12), channel_id=1, source_target_pairs={{0,4},{4,8},{8,12},{12,16},{16,20},{20,24},{24,28},{1,5},{5,9},{9,... | collective-permute-start | bytes 786440 | tf_op jit(solution)/shard_map/ppermute | solution.py:146
  (67 other events, 552.2 us)

commit v3 on v2

--- a/solution.py
+++ b/solution.py
@@ -9,7 +9,8 @@
 CORES = 2
 EPS = 1e-06
 STAGES = (3, 5)
-ROUNDS = (((0, 0), (1, 1), (2, 2), (3, 3), 4), ((1, 1), (2, 3), (4, 4), (5, 5), 6))
+ROUNDS = ((0, (1, 1), 2, 3, 4, 4), (1, (2, 3), 4, 5, 6, 7))
+CHAINS = (1, 2)
 LANES = 128
 
 
@@ -193,8 +194,9 @@
 
 
 def partial_kernel(column, *refs):
-    *lefts, own, other, out, joined = refs
+    own, other, out, joined = refs[-4:]
     planes, columns, share, depth = joined.shape
+    lefts = refs[:columns]
 
     @pl.when(pl.program_id(0) == 0)
     def _():
@@ -203,7 +205,8 @@
 
     rows = joined[...].reshape(planes * columns * share, depth)
     half = depth // 2
-    out[...] = dot(rows[:, :half], own[0]) + dot(rows[:, half:], other[0])
+    total = dot(rows[:, :half], own[0]) + dot(rows[:, half:], other[0])
+    out[...] = total.astype(out.dtype)
 
 
 def partial_sums(column, lefts, part, parts, own, other):
@@ -215,7 +218,7 @@
     weights = pl.BlockSpec((1, own.shape[1], late), lambda b, _: (b, 0, 0))
     return pl.pallas_call(
         partial_kernel,
-        out_shape=jax.ShapeDtypeStruct((rows, 3 * late), jnp.float32),
+        out_shape=jax.ShapeDtypeStruct((rows, 3 * late), jnp.bfloat16),
         grid_spec=pltpu.PrefetchScalarGridSpec(
             num_scalar_prefetch=1,
             grid=(3,),
@@ -227,7 +230,7 @@
         compiler_params=pltpu.CompilerParams(vmem_limit_bytes=48 * 1024 * 1024),
         cost_estimate=pl.CostEstimate(
             flops=2 * rows * depth * 3 * late,
-            bytes_accessed=2 * rows * depth + 6 * depth * late + 12 * rows * late,
+            bytes_accessed=2 * rows * depth + 6 * depth * late + 6 * rows * late,
             transcendentals=0,
         ),
     )(column, *lefts, own, other).reshape(planes, columns * share, 3 * late)
@@ -275,86 +278,105 @@
     def turned(normed):
         return jnp.where(core == 0, normed, jnp.roll(normed, width // 2, axis=2))
 
-    def to_planes(normed):
-        rows_of = [None] * planes
-        for d in range(planes):
+    def to_planes(normed, distances):
+        rows_of = {}
+        for d in distances:
             piece = pick(normed, column ^ ((plane + d) % planes))
-            if d > 0:
-                piece = plane_shift(piece, [(p, (p + d) % planes) for p in range(planes)])
-            rows_of[(planes - d) % planes] = piece
+            rows_of[planes - d] = plane_shift(piece, [(p, (p + d) % planes) for p in range(planes)])
         return rows_of
 
-    def send_weights(step, right, left):
+    def onward(step, terms, sums):
+        sent = terms[planes - step], terms[step]
+        if sums is None:
+            return sent
+        return [
+            (term.astype(jnp.float32) + arrived.astype(jnp.float32)).astype(jnp.bfloat16)
+            for term, arrived in zip(sent, sums)
+        ]
+
+    def send_sums(step, right, left):
         return (
-            plane_shift(right, [(p, p + 1) for p in range(planes - 1) if p >= step - 1]),
-            plane_shift(left, [(p, p - 1) for p in range(1, planes) if p <= planes - step]),
-        )
-
-    def onward(term, arrived):
-        if arrived is not None:
-            term = term + arrived.astype(jnp.float32)
-        return term.astype(jnp.bfloat16)
-
-    def send_sums(step, terms, sums):
-        right, left = sums
-        return (
-            plane_shift(
-                onward(terms[planes - step], right),
-                [(p, p + 1) for p in range(planes - 1) if p < step],
-            ),
-            plane_shift(
-                onward(terms[step], left),
-                [(p, p - 1) for p in range(1, planes) if p >= planes - step],
-            ),
+            plane_shift(right, [(p, p + 1) for p in range(planes - 1) if p < step]),
+            plane_shift(left, [(p, p - 1) for p in range(1, planes) if p >= planes - step]),
         )
 
     count, steps = len(stages), planes - 1
     order = [m for k in range(1, planes // 2) for m in (planes - k, k)] + [planes // 2, 0]
-    last = max(at[4] for at in ROUNDS) + steps - 1
+    around = [planes // 2], [d for d in range(1, planes) if d != planes // 2]
     live = {f"pieces{stage}": to_trade(stage) for stage in range(count)}
-    own, normed, terms, totals, flying = {}, {}, {}, {}, {}
-
-    for now in range(last + 1):
-        for stage, (to_shares, across, near, far, first) in enumerate(ROUNDS):
-            if now == to_shares[0]:
-                flying[f"trade{stage}"] = to_shares[1], trade(live.pop(f"pieces{stage}"))
+    own, normed, rows_of, sums = {}, {}, {}, {}
+
+    chains = {}
+
+    def split(stage, halves_of_terms):
+        terms = [half[m] for half in halves_of_terms for m in range(planes // 2)]
+        parts = CHAINS[stage]
+        rows = stages[stage][1] // parts
+        chains[stage] = [
+            [terms[order.index(m)][part * rows : (part + 1) * rows] for m in range(planes)]
+            for part in range(parts)
+        ]
+        sums[stage] = [None] * parts
+
+    def next_sums(stage, step):
+        sent = [
+            onward(step, terms, arrived) for terms, arrived in zip(chains[stage], sums[stage])
+        ]
+        return [send_sums(step, *pair) for pair in sent]
+
+    for now in range(ROUNDS[-1][-1]):
+        fresh = {"weight": other_weight} if now == 0 else {}
+        for stage, (to_shares, across, near, far, product, first) in enumerate(ROUNDS):
+            if now < to_shares:
+                fresh[f"pieces{stage}"] = live[f"pieces{stage}"]
+            if now == to_shares:
+                fresh[f"trade{stage}"] = trade(live[f"pieces{stage}"])
             if now == across[0]:
-                normed[stage] = turned(normalize(live.pop(f"trade{stage}")))
-                flying[f"planes{stage}"] = across[1], to_planes(normed[stage])
-            if now == near[0]:
-                pieces = live.pop(f"planes{stage}")
-                own[stage] = jnp.stack([pieces[m] for m in order])
-                flying[f"near{stage}"] = near[1], spread_near(own[stage], columns)
-            if now == far[0]:
-                flying[f"far{stage}"] = far[1], spread_far(live[f"near{stage}"], columns)
-            if now == first:
-                lefts = spread_all(
-                    own[stage], live.pop(f"near{stage}"), live.pop(f"far{stage}")
-                )
-                products = [
-                    product[m]
+                normed[stage] = turned(normalize(live[f"trade{stage}"]))
+                rows_of[stage] = {0: pick(normed[stage], column ^ plane)}
+            for at, distances in zip(across, around):
+                if now == at:
+                    fresh[f"planes{stage}{distances[0]}"] = to_planes(normed[stage], distances)
+            if now == near:
+                own[stage] = jnp.stack([rows_of[stage][m] for m in order])
+                fresh[f"near{stage}"] = spread_near(own[stage], columns)
+            if now == far:
+                fresh[f"near{stage}"] = live[f"near{stage}"]
+                fresh[f"far{stage}"] = spread_far(live[f"near{stage}"], columns)
+            if now == product:
+                lefts = spread_all(own[stage], live[f"near{stage}"], live[f"far{stage}"])
+                fresh[f"terms{stage}"] = [
+                    partial_sums(place, lefts, half, 2, own_weight, other_weight)
                     for half in range(2)
-                    for product in [
-                        partial_sums(place, lefts, half, 2, own_weight, other_weight)
-                    ]
-                    for m in range(planes // 2)
                 ]
-                terms[stage] = [products[order.index(m)] for m in range(planes)]
-                live[f"sums{stage}"] = (None, None)
+                if now == first:
+                    split(stage, fresh.pop(f"terms{stage}"))
             if first <= now < first + steps:
-                sums = live.pop(f"sums{stage}")
-                flying[f"sums{stage}"] = now, send_sums(now - first + 1, terms[stage], sums)
-        for name in [name for name, (end, _) in flying.items() if end == now]:
-            live[name] = flying.pop(name)[1]
-        live = together(live) if now < last else live
+                fresh[f"sums{stage}"] = next_sums(stage, now - first + 1)
+        live = together(fresh)
+        other_weight = live.pop("weight", other_weight)
         for stage in range(count):
-            if now == ROUNDS[stage][4] + steps - 1:
-                right, left = live.pop(f"sums{stage}")
-                total = terms[stage][0] + right.astype(jnp.float32) + left.astype(jnp.float32)
-                totals[stage] = total.astype(jnp.bfloat16)
-
+            for distances in around:
+                rows_of.get(stage, {}).update(live.pop(f"planes{stage}{distances[0]}", {}))
+            if f"sums{stage}" in live:
+                sums[stage] = live.pop(f"sums{stage}")
+            if f"terms{stage}" in live:
+                split(stage, live.pop(f"terms{stage}"))
+    for step in range(1, planes):
+        sums[count - 1] = next_sums(count - 1, step)
+
+    def summed(stage):
+        parts = []
+        for terms, (right, left) in zip(chains[stage], sums[stage]):
+            total = terms[0].astype(jnp.float32)
+            total = total + right.astype(jnp.float32) + left.astype(jnp.float32)
+            parts.append(total.astype(jnp.bfloat16))
+        return parts
+
+    totals = {stage: summed(stage) for stage in range(count)}
+    totals[0] = jnp.concatenate(totals[0], axis=0)
     rim, gated_rim = rims(totals[0], short_filter, long_count)
-    projected = jnp.concatenate([totals[1], totals[0]], axis=0)
+    projected = jnp.concatenate([*totals[1], totals[0]], axis=0)
     return finish(projected, rim, gated_rim, short_filter, long_filter)
 
 

time: 379 us -> 348 us (0.918)
  waiting for transfers between devices: 192 us -> 167 us
  starting transfers between devices: 75.4 us -> 88.3 us
  other arithmetic: 29.3 us -> 17.6 us
  Pallas kernels: 55.6 us -> 51.1 us
    ppermute x14, waiting for transfers between devices: 36.1 us -> 19.3 us  [swap(): return lax.ppermute(value, 'fsdp', [(j, j ^ bits) for j in range(count)])]
    ppermute x18 -> x24, starting transfers between devices: 51.7 us -> 65.5 us  [plane_shift(): lax.ppermute(value, 'ctx', [(a * CORES + c, b * CORES + c) for a, b in ed...]
    convert_element_type x6 -> x8, other arithmetic: 19.4 us -> 9.33 us  [the longest x5 7.16 us: onward(): (term.astype(jnp.float32) + arrived.astype(jnp.float32)).astype(jnp.bfloa...]
    ppermute x18 -> x24, waiting for transfers between devices: 156 us -> 147 us  [plane_shift(): lax.ppermute(value, 'ctx', [(a * CORES + c, b * CORES + c) for a, b in ed...]
    slice x2, local copies, waits for them, and re-layouts: 7.95 us -> 2.75 us  [the longest x1 2.6 us: split(): terms[order.index(m)][part * rows:(part + 1) * rows]]
    pallas_call x4, Pallas kernels: 48.1 us -> 43.7 us  [partial_sums(): pl.pallas_call(partial_kernel, out_shape=jax.ShapeDtypeStruct((rows, 3 *...]
    unnamed x126 -> x108, local copies, waits for them, and re-layouts: 9.1 us -> 10.6 us
  transfers between devices with their start and end apart: 35 -> 41, of which waited for: 18 -> 18; matrix products, arithmetic and copies ran while one was open for 6% -> 3% of each run, Pallas kernels for 9% -> 13%
where the time goes in v3:
time: 348 us; the launch traced here: 347 us
  waiting for transfers between devices  167 us (48%)
  starting transfers between devices  88.3 us (25%)
  Pallas kernels  51.1 us (15%)
  local copies, waits for them, and re-layouts  22.7 us (7%)
  other arithmetic  17.6 us (5%)
    ppermute x24, waiting for transfers between devices, plane_shift(): lax.ppermute(value, 'ctx', [(a * CORES + c, b * CORES + c) for a, b in ed...  147 us
    ppermute x24, starting transfers between devices, plane_shift(): lax.ppermute(value, 'ctx', [(a * CORES + c, b * CORES + c) for a, b in ed...  65.5 us
    pallas_call x4, Pallas kernels, partial_sums(): pl.pallas_call(partial_kernel, out_shape=jax.ShapeDtypeStruct((rows, 3 *...  43.7 us
    ppermute x14, waiting for transfers between devices, swap(): return lax.ppermute(value, 'fsdp', [(j, j ^ bits) for j in range(count)])  19.3 us
    ppermute x14, starting transfers between devices, swap(): return lax.ppermute(value, 'fsdp', [(j, j ^ bits) for j in range(count)])  16.4 us
    unnamed x108, local copies, waits for them, and re-layouts  10.6 us
    pallas_call x1, Pallas kernels, finish(): pl.pallas_call(finish_kernel, out_shape=jax.ShapeDtypeStruct((row_count,...  7.45 us
    convert_element_type x5, other arithmetic, onward(): (term.astype(jnp.float32) + arrived.astype(jnp.float32)).astype(jnp.bfloa...  7.16 us
  transfers between devices with their start and end apart: 41, of which 18 were waited for; matrix products, arithmetic and copies ran while one was open for 3% of the time, Pallas kernels for 13%

profile of v3, /device:TPU:0, one launch (start us, length us, event | category | flops | bytes accessed | tf_op | source)
XLA Modules:
  0.0 347.4 jit_solution(18444936151366703647)
XLA Ops:
  7.6 2.9 collective-permute-done.refs_5_
  10.6 4.8 %collective-permute-done.1.refs_6_ = bf16[48,2048]{1,0:T(8,128)(2,1)S(1)} collective-permute-done((bf16[48,2048]{1,0:T(8,128)(2,1)S(1)}, bf16[48,2048]{1,0:T(8,128)(2,1)S(1)}, u32[]{:S(2)}, u32[]{:S(2)}) %collective-permute-start.1) | collective-permute-done | bytes 196640 | tf_op jit(solution)/shard_map/ppermute | solution.py:24
  19.8 3.7 %collective-permute-start.4 = (bf16[48,2048]{1,0:T(8,128)(2,1)S(1)}, bf16[48,2048]{1,0:T(8,128)(2,1)S(1)}, u32[]{:S(2)}, u32[]{:S(2)}) collective-permute-start(bf16[48,2048]{1,0:T(8,128)(2,1)S(1)} %get-tuple-element.117), channel_id=1, source_target_pairs={{0,24},{4,28},{8,0},{12,4},{16,8},{20,12},{24,16},{28,20},{1,25},{... | collective-permute-start | bytes 589832 | tf_op jit(solution)/shard_map/ppermute | solution.py:28
  28.5 6.9 %collective-permute-done.5.refs_1_ = bf16[48,2048]{1,0:T(8,128)(2,1)S(1)} collective-permute-done((bf16[48,2048]{1,0:T(8,128)(2,1)S(1)}, bf16[48,2048]{1,0:T(8,128)(2,1)S(1)}, u32[]{:S(2)}, u32[]{:S(2)}) %collective-permute-start.5) | collective-permute-done | bytes 196640 | tf_op jit(solution)/shard_map/ppermute | solution.py:28
  35.4 5.4 %collective-permute-done.6.refs_2_ = bf16[48,2048]{1,0:T(8,128)(2,1)S(1)} collective-permute-done((bf16[48,2048]{1,0:T(8,128)(2,1)S(1)}, bf16[48,2048]{1,0:T(8,128)(2,1)S(1)}, u32[]{:S(2)}, u32[]{:S(2)}) %collective-permute-start.6) | collective-permute-done | bytes 196640 | tf_op jit(solution)/shard_map/ppermute | solution.py:28
  47.8 16.1 %collective-permute-done.12.refs_2_ = bf16[80,2048]{1,0:T(8,128)(2,1)S(1)} collective-permute-done((bf16[80,2048]{1,0:T(8,128)(2,1)S(1)}, bf16[80,2048]{1,0:T(8,128)(2,1)S(1)}, u32[]{:S(2)}, u32[]{:S(2)}) %collective-permute-start.12) | collective-permute-done | bytes 327712 | tf_op jit(solution)/shard_map/ppermute | solution.py:28
  72.1 14.2 %collective-permute-done.15.refs_4_ = bf16[80,2048]{1,0:T(8,128)(2,1)S(1)} collective-permute-done((bf16[80,2048]{1,0:T(8,128)(2,1)}, bf16[80,2048]{1,0:T(8,128)(2,1)S(1)}, u32[]{:S(2)}, u32[]{:S(2)}) %collective-permute-start.15) | collective-permute-done | bytes 327712 | tf_op jit(solution)/shard_map/ppermute | solution.py:28
  91.7 8.8 %shard_map.77 = bf16[384,3072]{1,0:T(8,128)(2,1)S(1)} custom-call(s32[2]{0:T(128)S(1)} %pad_add_fusion.column, bf16[4,48,2048]{2,1,0:T(8,128)(2,1)S(1)} %pad_maximum_fusion.4.refs_0_, bf16[4,48,2048]{2,1,0:T(8,128)(2,1)S(1)} %copy-done.1, bf16[4,48,2048]{2,1,0:T(8,128)(2,1)S(1)} %copy-done.3, ...), custom_call_target="tpu_custom_call" | custom-call | flops 4831838208 | bytes 16515072 | tf_op jit(solution)/shard_map/pallas_call | solution.py:219
  100.6 3.1 collective-permute-start.19
  104.5 8.8 %shard_map.79 = bf16[384,3072]{1,0:T(8,128)(2,1)S(1)} custom-call(s32[2]{0:T(128)S(1)} %pad_add_fusion.column, bf16[4,48,2048]{2,1,0:T(8,128)(2,1)S(1)} %pad_maximum_fusion.4.refs_0_, bf16[4,48,2048]{2,1,0:T(8,128)(2,1)S(1)} %copy-done.1, bf16[4,48,2048]{2,1,0:T(8,128)(2,1)S(1)} %copy-done.3, ...), custom_call_target="tpu_custom_call" | custom-call | flops 4831838208 | bytes 16515072 | tf_op jit(solution)/shard_map/pallas_call | solution.py:219
  114.7 12.4 %collective-permute-done.19.refs_2_ = bf16[192,3072]{1,0:T(8,128)(2,1)S(1)} collective-permute-done((bf16[192,3072]{1,0:T(8,128)(2,1)S(1)}, bf16[192,3072]{1,0:T(8,128)(2,1)S(1)}, u32[]{:S(2)}, u32[]{:S(2)}) %collective-permute-start.19) | collective-permute-done | bytes 1179680 | tf_op jit(solution)/shard_map/ppermute | solution.py:28
  131.2 5.4 %collective-permute-start.23 = (bf16[192,3072]{1,0:T(8,128)(2,1)S(1)}, bf16[192,3072]{1,0:T(8,128)(2,1)}, u32[]{:S(2)}, u32[]{:S(2)}) collective-permute-start(bf16[192,3072]{1,0:T(8,128)(2,1)S(1)} %get-tuple-element.99), channel_id=1, source_target_pairs={{0,8},{4,12},{8,16},{12,20},{1,9},{5,13},{9,17},{13,21},{2,10},{6,... | collective-permute-start | bytes 3538952 | tf_op jit(solution)/shard_map/ppermute | solution.py:28
  142.7 10.2 %collective-permute-done.21.refs_0_ = bf16[4,80,1024]{2,1,0:T(8,128)(2,1)S(1)} collective-permute-done((bf16[4,80,1024]{2,1,0:T(8,128)(2,1)S(1)}, bf16[4,80,1024]{2,1,0:T(8,128)(2,1)S(1)}, u32[]{:S(2)}, u32[]{:S(2)}) %collective-permute-start.21) | collective-permute-done | bytes 655392 | tf_op jit(solution)/shard_map/ppermute | solution.py:24
  154.3 3.8 %collective-permute-done.23.refs_4_ = bf16[192,3072]{1,0:T(8,128)(2,1)} collective-permute-done((bf16[192,3072]{1,0:T(8,128)(2,1)S(1)}, bf16[192,3072]{1,0:T(8,128)(2,1)}, u32[]{:S(2)}, u32[]{:S(2)}) %collective-permute-start.23) | collective-permute-done | bytes 1179680 | tf_op jit(solution)/shard_map/ppermute | solution.py:28
  160.6 8.9 %collective-permute-start.25 = (bf16[192,3072]{1,0:T(8,128)(2,1)S(1)}, bf16[192,3072]{1,0:T(8,128)(2,1)S(1)}, u32[]{:S(2)}, u32[]{:S(2)}) collective-permute-start(bf16[192,3072]{1,0:T(8,128)(2,1)S(1)} %get-tuple-element.97), channel_id=1, source_target_pairs={{0,8},{4,12},{8,16},{12,20},{16,24},{20,28},{1,9},{5,13},{9,17},{1... | collective-permute-start | bytes 3538952 | tf_op jit(solution)/shard_map/ppermute | solution.py:28
  172.2 13.1 %shard_map.81 = bf16[640,3072]{1,0:T(8,128)(2,1)} custom-call(s32[2]{0:T(128)S(1)} %pad_add_fusion.column, bf16[4,80,2048]{2,1,0:T(8,128)(2,1)S(1)} %copy-done.7, bf16[4,80,2048]{2,1,0:T(8,128)(2,1)} %get-tuple-element.75.refs_1_, bf16[4,80,2048]{2,1,0:T(8,128)(2,1)} %get-tuple-element.76.refs_2_, ...), custom_call_target="tpu_custom_call" | custom-call | flops 8053063680 | bytes 19136512 | tf_op jit(solution)/shard_map/pallas_call | solution.py:219
  185.3 13.1 %shard_map.82 = bf16[640,3072]{1,0:T(8,128)(2,1)} custom-call(s32[2]{0:T(128)S(1)} %pad_add_fusion.column, bf16[4,80,2048]{2,1,0:T(8,128)(2,1)S(1)} %copy-done.7, bf16[4,80,2048]{2,1,0:T(8,128)(2,1)} %get-tuple-element.75.refs_1_, bf16[4,80,2048]{2,1,0:T(8,128)(2,1)} %get-tuple-element.76.refs_2_, ...), custom_call_target="tpu_custom_call" | custom-call | flops 8053063680 | bytes 19136512 | tf_op jit(solution)/shard_map/pallas_call | solution.py:219
  202.3 4.6 %collective-permute-start.27 = (bf16[160,3072]{1,0:T(8,128)(2,1)S(1)}, bf16[160,3072]{1,0:T(8,128)(2,1)S(1)}, u32[]{:S(2)}, u32[]{:S(2)}) collective-permute-start(bf16[160,3072]{1,0:T(8,128)(2,1)S(1)} %get-tuple-element.90), channel_id=1, source_target_pairs={{0,8},{4,12},{1,9},{5,13},{2,10},{6,14},{3,11},{7,15}} | collective-permute-start | bytes 2949128 | tf_op jit(solution)/shard_map/ppermute | solution.py:28
  207.6 16.4 %collective-permute-done.27 = bf16[160,3072]{1,0:T(8,128)(2,1)S(1)} collective-permute-done((bf16[160,3072]{1,0:T(8,128)(2,1)S(1)}, bf16[160,3072]{1,0:T(8,128)(2,1)S(1)}, u32[]{:S(2)}, u32[]{:S(2)}) %collective-permute-start.27) | collective-permute-done | bytes 983072 | tf_op jit(solution)/shard_map/ppermute | solution.py:28
  224.7 4.6 %collective-permute-start.28 = (bf16[160,3072]{1,0:T(8,128)(2,1)S(1)}, bf16[160,3072]{1,0:T(8,128)(2,1)S(1)}, u32[]{:S(2)}, u32[]{:S(2)}) collective-permute-start(bf16[160,3072]{1,0:T(8,128)(2,1)S(1)} %get-tuple-element.88), channel_id=1, source_target_pairs={{0,8},{4,12},{8,16},{12,20},{1,9},{5,13},{9,17},{13,21},{2,10},{6,... | collective-permute-start | bytes 2949128 | tf_op jit(solution)/shard_map/ppermute | solution.py:28
  230.8 3.4 collective-permute-start.33
  234.2 17.2 %collective-permute-done.28 = bf16[160,3072]{1,0:T(8,128)(2,1)S(1)} collective-permute-done((bf16[160,3072]{1,0:T(8,128)(2,1)S(1)}, bf16[160,3072]{1,0:T(8,128)(2,1)S(1)}, u32[]{:S(2)}, u32[]{:S(2)}) %collective-permute-start.28) | collective-permute-done | bytes 983072 | tf_op jit(solution)/shard_map/ppermute | solution.py:28
  253.4 5.2 %collective-permute-start.29 = (bf16[160,3072]{1,0:T(8,128)(2,1)S(1)}, bf16[160,3072]{1,0:T(8,128)(2,1)S(1)}, u32[]{:S(2)}, u32[]{:S(2)}) collective-permute-start(bf16[160,3072]{1,0:T(8,128)(2,1)S(1)} %get-tuple-element.86), channel_id=1, source_target_pairs={{0,8},{4,12},{8,16},{12,20},{16,24},{20,28},{1,9},{5,13},{9,17},{1... | collective-permute-start | bytes 2949128 | tf_op jit(solution)/shard_map/ppermute | solution.py:28
  258.6 13.9 %collective-permute-done.33 = bf16[160,3072]{1,0:T(8,128)(2,1)S(1)} collective-permute-done((bf16[160,3072]{1,0:T(8,128)(2,1)S(1)}, bf16[160,3072]{1,0:T(8,128)(2,1)S(1)}, u32[]{:S(2)}, u32[]{:S(2)}) %collective-permute-start.33) | collective-permute-done | bytes 983072 | tf_op jit(solution)/shard_map/ppermute | solution.py:28
  272.5 15.3 %collective-permute-done.29 = bf16[160,3072]{1,0:T(8,128)(2,1)S(1)} collective-permute-done((bf16[160,3072]{1,0:T(8,128)(2,1)S(1)}, bf16[160,3072]{1,0:T(8,128)(2,1)S(1)}, u32[]{:S(2)}, u32[]{:S(2)}) %collective-permute-start.29) | collective-permute-done | bytes 983072 | tf_op jit(solution)/shard_map/ppermute | solution.py:28
  288.9 4.4 %collective-permute-start.34 = (bf16[160,3072]{1,0:T(8,128)(2,1)S(1)}, bf16[160,3072]{1,0:T(8,128)(2,1)S(1)}, u32[]{:S(2)}, u32[]{:S(2)}) collective-permute-start(bf16[160,3072]{1,0:T(8,128)(2,1)S(1)} %get-tuple-element.85), channel_id=1, source_target_pairs={{0,8},{4,12},{8,16},{12,20},{1,9},{5,13},{9,17},{13,21},{2,10},{6,... | collective-permute-start | bytes 2949128 | tf_op jit(solution)/shard_map/ppermute | solution.py:28
  294.1 14.6 %collective-permute-done.34 = bf16[160,3072]{1,0:T(8,128)(2,1)S(1)} collective-permute-done((bf16[160,3072]{1,0:T(8,128)(2,1)S(1)}, bf16[160,3072]{1,0:T(8,128)(2,1)S(1)}, u32[]{:S(2)}, u32[]{:S(2)}) %collective-permute-start.34) | collective-permute-done | bytes 983072 | tf_op jit(solution)/shard_map/ppermute | solution.py:28
  310.7 10.8 %collective-permute-start.35 = (bf16[160,3072]{1,0:T(8,128)(2,1)S(1)}, bf16[160,3072]{1,0:T(8,128)(2,1)S(1)}, u32[]{:S(2)}, u32[]{:S(2)}) collective-permute-start(bf16[160,3072]{1,0:T(8,128)(2,1)S(1)} %get-tuple-element.94), channel_id=1, source_target_pairs={{0,8},{4,12},{8,16},{12,20},{16,24},{20,28},{1,9},{5,13},{9,17},{1... | collective-permute-start | bytes 2949128 | tf_op jit(solution)/shard_map/ppermute | solution.py:28
  323.9 4.6 %collective-permute-start.40 = (bf16[128,1024]{1,0:T(8,128)(2,1)S(1)}, bf16[128,1024]{1,0:T(8,128)(2,1)S(1)}, u32[]{:S(2)}, u32[]{:S(2)}) collective-permute-start(bf16[128,1024]{1,0:T(8,128)(2,1)S(1)} %fusion.18), channel_id=1, source_target_pairs={{0,4},{4,8},{8,12},{12,16},{16,20},{20,24},{24,28},{1,5},{5,9},{9,... | collective-permute-start | bytes 786440 | tf_op jit(solution)/shard_map/ppermute | solution.py:147
  328.5 4.7 %collective-permute-done.38 = bf16[160,3072]{1,0:T(8,128)(2,1)S(1)} collective-permute-done((bf16[160,3072]{1,0:T(8,128)(2,1)S(1)}, bf16[160,3072]{1,0:T(8,128)(2,1)S(1)}, u32[]{:S(2)}, u32[]{:S(2)}) %collective-permute-start.38) | collective-permute-done | bytes 983072 | tf_op jit(solution)/shard_map/ppermute | solution.py:28
  333.3 5.0 %collective-permute-done.35 = bf16[160,3072]{1,0:T(8,128)(2,1)S(1)} collective-permute-done((bf16[160,3072]{1,0:T(8,128)(2,1)S(1)}, bf16[160,3072]{1,0:T(8,128)(2,1)S(1)}, u32[]{:S(2)}, u32[]{:S(2)}) %collective-permute-start.35) | collective-permute-done | bytes 983072 | tf_op jit(solution)/shard_map/ppermute | solution.py:28
  340.0 7.4 %shard_map.84 = bf16[512,1024]{1,0:T(8,128)(2,1)} custom-call(bf16[512,3072]{1,0:T(8,128)(2,1)S(1)} %pad_maximum_fusion.query.key.value, bf16[512,3072]{1,0:T(8,128)(2,1)S(1)} %pad_maximum_fusion.query.key.value, bf16[512,3072]{1,0:T(8,128)(2,1)S(1)} %pad_maximum_fusion.query.key.value, ...), custom_call_target="tpu_custom_call" | custom-call | flops 2621440000 | bytes 5242880 | tf_op jit(solution)/shard_map/pallas_call | solution.py:128
  (215 shorter events, 72.8 us)
Async XLA Ops:
  0.0 15.4 %collective-permute-start.3 = (bf16[3,1024,1024]{2,1,0:T(8,128)(2,1)}, bf16[3,1024,1024]{2,1,0:T(8,128)(2,1)}, u32[]{:S(2)}, u32[]{:S(2)}) collective-permute-start(bf16[3,1024,1024]{2,1,0:T(8,128)(2,1)} %bitcast.86), channel_id=1, source_target_pairs={{0,4},{4,0},{8,12},{12,8},{16,20},{20,16},{24,28},{28,24},{1,5},{5... | collective-permute-start | bytes 18874376 | tf_op jit(solution)/shard_map/ppermute | solution.py:257
  23.5 17.3 %collective-permute-start.7 = (bf16[80,2048]{1,0:T(8,128)(2,1)S(1)}, bf16[80,2048]{1,0:T(8,128)(2,1)S(1)}, u32[]{:S(2)}, u32[]{:S(2)}) collective-permute-start(bf16[80,2048]{1,0:T(8,128)(2,1)S(1)} %copy-done.44), channel_id=1, source_target_pairs={{0,1},{1,0},{2,3},{3,2},{4,5},{5,4},{6,7},{7,6},{8,9},{9,8},{10,11... | collective-permute-start | bytes 983048 | tf_op jit(solution)/shard_map/ppermute | solution.py:24
  24.7 16.1 %collective-permute-start.8 = (bf16[80,2048]{1,0:T(8,128)(2,1)S(1)}, bf16[80,2048]{1,0:T(8,128)(2,1)S(1)}, u32[]{:S(2)}, u32[]{:S(2)}) collective-permute-start(bf16[80,2048]{1,0:T(8,128)(2,1)S(1)} %copy-done.43), channel_id=1, source_target_pairs={{0,2},{1,3},{2,0},{3,1},{4,6},{5,7},{6,4},{7,5},{8,10},{9,11},{10,... | collective-permute-start | bytes 983048 | tf_op jit(solution)/shard_map/ppermute | solution.py:24
  25.6 15.2 %collective-permute-start.9 = (bf16[80,2048]{1,0:T(8,128)(2,1)S(1)}, bf16[80,2048]{1,0:T(8,128)(2,1)S(1)}, u32[]{:S(2)}, u32[]{:S(2)}) collective-permute-start(bf16[80,2048]{1,0:T(8,128)(2,1)S(1)} %copy-done.42), channel_id=1, source_target_pairs={{0,3},{1,2},{2,1},{3,0},{4,7},{5,6},{6,5},{7,4},{8,11},{9,10},{10,... | collective-permute-start | bytes 983048 | tf_op jit(solution)/shard_map/ppermute | solution.py:24
  43.2 20.7 %collective-permute-start.10 = (bf16[4,48,2048]{2,1,0:T(8,128)(2,1)S(1)}, bf16[4,48,2048]{2,1,0:T(8,128)(2,1)S(1)}, u32[]{:S(2)}, u32[]{:S(2)}) collective-permute-start(bf16[4,48,2048]{2,1,0:T(8,128)(2,1)S(1)} %pad_maximum_fusion.4.refs_0_), channel_id=1, source_target_pairs={{0,1},{1,0},{2,3},{3,2},{4,5},{5,4},{6,7},{7,6},{8,9},{9,8},{10,11... | collective-permute-start | bytes 2359304 | tf_op jit(solution)/shard_map/ppermute | solution.py:24
  44.7 19.2 %collective-permute-start.11 = (bf16[4,48,2048]{2,1,0:T(8,128)(2,1)S(1)}, bf16[4,48,2048]{2,1,0:T(8,128)(2,1)S(1)}, u32[]{:S(2)}, u32[]{:S(2)}) collective-permute-start(bf16[4,48,2048]{2,1,0:T(8,128)(2,1)S(1)} %pad_maximum_fusion.4.refs_0_), channel_id=1, source_target_pairs={{0,2},{1,3},{2,0},{3,1},{4,6},{5,7},{6,4},{7,5},{8,10},{9,11},{10,... | collective-permute-start | bytes 2359304 | tf_op jit(solution)/shard_map/ppermute | solution.py:24
  47.8 16.1 %collective-permute-start.12 = (bf16[80,2048]{1,0:T(8,128)(2,1)S(1)}, bf16[80,2048]{1,0:T(8,128)(2,1)S(1)}, u32[]{:S(2)}, u32[]{:S(2)}) collective-permute-start(bf16[80,2048]{1,0:T(8,128)(2,1)S(1)} %get-tuple-element.105), channel_id=1, source_target_pairs={{0,16},{4,20},{8,24},{12,28},{16,0},{20,4},{24,8},{28,12},{1,17},{... | collective-permute-start | bytes 983048 | tf_op jit(solution)/shard_map/ppermute | solution.py:28
  66.8 19.6 %collective-permute-start.13 = (bf16[4,48,1024]{2,1,0:T(8,128)(2,1)S(1)}, bf16[4,48,1024]{2,1,0:T(8,128)(2,1)S(1)}, u32[]{:S(2)}, u32[]{:S(2)}) collective-permute-start(bf16[4,48,1024]{2,1,0:T(8,128)(2,1)S(1)} %slice.153), channel_id=1, source_target_pairs={{0,1},{1,0},{2,3},{3,2},{4,5},{5,4},{6,7},{7,6},{8,9},{9,8},{10,11... | collective-permute-start | bytes 1179656 | tf_op jit(solution)/shard_map/ppermute | solution.py:24
  68.3 18.1 %collective-permute-start.14 = (bf16[4,48,1024]{2,1,0:T(8,128)(2,1)S(1)}, bf16[4,48,1024]{2,1,0:T(8,128)(2,1)S(1)}, u32[]{:S(2)}, u32[]{:S(2)}) collective-permute-start(bf16[4,48,1024]{2,1,0:T(8,128)(2,1)S(1)} %slice.154), channel_id=1, source_target_pairs={{0,2},{1,3},{2,0},{3,1},{4,6},{5,7},{6,4},{7,5},{8,10},{9,11},{10,... | collective-permute-start | bytes 1179656 | tf_op jit(solution)/shard_map/ppermute | solution.py:24
  70.0 16.3 %collective-permute-start.15 = (bf16[80,2048]{1,0:T(8,128)(2,1)}, bf16[80,2048]{1,0:T(8,128)(2,1)S(1)}, u32[]{:S(2)}, u32[]{:S(2)}) collective-permute-start(bf16[80,2048]{1,0:T(8,128)(2,1)} %get-tuple-element.104), channel_id=1, source_target_pairs={{0,24},{4,28},{8,0},{12,4},{16,8},{20,12},{24,16},{28,20},{1,25},{... | collective-permute-start | bytes 983048 | tf_op jit(solution)/shard_map/ppermute | solution.py:28
  89.5 37.5 %collective-permute-start.17 = (bf16[4,80,2048]{2,1,0:T(8,128)(2,1)S(1)}, bf16[4,80,2048]{2,1,0:T(8,128)(2,1)}, u32[]{:S(2)}, u32[]{:S(2)}) collective-permute-start(bf16[4,80,2048]{2,1,0:T(8,128)(2,1)S(1)} %pad_maximum_fusion.2.refs_0_), channel_id=1, source_target_pairs={{0,1},{1,0},{2,3},{3,2},{4,5},{5,4},{6,7},{7,6},{8,9},{9,8},{10,11... | collective-permute-start | bytes 3932168 | tf_op jit(solution)/shard_map/ppermute | solution.py:24
  90.8 37.6 %collective-permute-start.18 = (bf16[4,80,2048]{2,1,0:T(8,128)(2,1)S(1)}, bf16[4,80,2048]{2,1,0:T(8,128)(2,1)}, u32[]{:S(2)}, u32[]{:S(2)}) collective-permute-start(bf16[4,80,2048]{2,1,0:T(8,128)(2,1)S(1)} %pad_maximum_fusion.2.refs_0_), channel_id=1, source_target_pairs={{0,2},{1,3},{2,0},{3,1},{4,6},{5,7},{6,4},{7,5},{8,10},{9,11},{10,... | collective-permute-start | bytes 3932168 | tf_op jit(solution)/shard_map/ppermute | solution.py:24
  100.6 26.4 %collective-permute-start.19 = (bf16[192,3072]{1,0:T(8,128)(2,1)S(1)}, bf16[192,3072]{1,0:T(8,128)(2,1)S(1)}, u32[]{:S(2)}, u32[]{:S(2)}) collective-permute-start(bf16[192,3072]{1,0:T(8,128)(2,1)S(1)} %get-tuple-element.101), channel_id=1, source_target_pairs={{0,8},{4,12},{1,9},{5,13},{2,10},{6,14},{3,11},{7,15}} | collective-permute-start | bytes 3538952 | tf_op jit(solution)/shard_map/ppermute | solution.py:28
  103.7 23.3 %collective-permute-start.20 = (bf16[192,3072]{1,0:T(8,128)(2,1)S(1)}, bf16[192,3072]{1,0:T(8,128)(2,1)S(1)}, u32[]{:S(2)}, u32[]{:S(2)}) collective-permute-start(bf16[192,3072]{1,0:T(8,128)(2,1)S(1)} %get-tuple-element.100), channel_id=1, source_target_pairs={{24,16},{28,20},{25,17},{29,21},{26,18},{30,22},{27,19},{31,23}} | collective-permute-start | bytes 3538952 | tf_op jit(solution)/shard_map/ppermute | solution.py:28
  131.2 26.9 %collective-permute-start.23 = (bf16[192,3072]{1,0:T(8,128)(2,1)S(1)}, bf16[192,3072]{1,0:T(8,128)(2,1)}, u32[]{:S(2)}, u32[]{:S(2)}) collective-permute-start(bf16[192,3072]{1,0:T(8,128)(2,1)S(1)} %get-tuple-element.99), channel_id=1, source_target_pairs={{0,8},{4,12},{8,16},{12,20},{1,9},{5,13},{9,17},{13,21},{2,10},{6,... | collective-permute-start | bytes 3538952 | tf_op jit(solution)/shard_map/ppermute | solution.py:28
  136.6 21.5 %collective-permute-start.24 = (bf16[192,3072]{1,0:T(8,128)(2,1)S(1)}, bf16[192,3072]{1,0:T(8,128)(2,1)}, u32[]{:S(2)}, u32[]{:S(2)}) collective-permute-start(bf16[192,3072]{1,0:T(8,128)(2,1)S(1)} %get-tuple-element.98), channel_id=1, source_target_pairs={{16,8},{20,12},{24,16},{28,20},{17,9},{21,13},{25,17},{29,21},{18,... | collective-permute-start | bytes 3538952 | tf_op jit(solution)/shard_map/ppermute | solution.py:28
  160.6 37.8 %collective-permute-start.25 = (bf16[192,3072]{1,0:T(8,128)(2,1)S(1)}, bf16[192,3072]{1,0:T(8,128)(2,1)S(1)}, u32[]{:S(2)}, u32[]{:S(2)}) collective-permute-start(bf16[192,3072]{1,0:T(8,128)(2,1)S(1)} %get-tuple-element.97), channel_id=1, source_target_pairs={{0,8},{4,12},{8,16},{12,20},{16,24},{20,28},{1,9},{5,13},{9,17},{1... | collective-permute-start | bytes 3538952 | tf_op jit(solution)/shard_map/ppermute | solution.py:28
  169.5 28.8 %collective-permute-start.26 = (bf16[192,3072]{1,0:T(8,128)(2,1)S(1)}, bf16[192,3072]{1,0:T(8,128)(2,1)S(1)}, u32[]{:S(2)}, u32[]{:S(2)}) collective-permute-start(bf16[192,3072]{1,0:T(8,128)(2,1)S(1)} %get-tuple-element.96), channel_id=1, source_target_pairs={{8,0},{12,4},{16,8},{20,12},{24,16},{28,20},{9,1},{13,5},{17,9},{2... | collective-permute-start | bytes 3538952 | tf_op jit(solution)/shard_map/ppermute | solution.py:28
  202.3 21.8 %collective-permute-start.27 = (bf16[160,3072]{1,0:T(8,128)(2,1)S(1)}, bf16[160,3072]{1,0:T(8,128)(2,1)S(1)}, u32[]{:S(2)}, u32[]{:S(2)}) collective-permute-start(bf16[160,3072]{1,0:T(8,128)(2,1)S(1)} %get-tuple-element.90), channel_id=1, source_target_pairs={{0,8},{4,12},{1,9},{5,13},{2,10},{6,14},{3,11},{7,15}} | collective-permute-start | bytes 2949128 | tf_op jit(solution)/shard_map/ppermute | solution.py:28
  206.9 17.2 %collective-permute-start.30 = (bf16[160,3072]{1,0:T(8,128)(2,1)S(1)}, bf16[160,3072]{1,0:T(8,128)(2,1)S(1)}, u32[]{:S(2)}, u32[]{:S(2)}) collective-permute-start(bf16[160,3072]{1,0:T(8,128)(2,1)S(1)} %get-tuple-element.93), channel_id=1, source_target_pairs={{24,16},{28,20},{25,17},{29,21},{26,18},{30,22},{27,19},{31,23}} | collective-permute-start | bytes 2949128 | tf_op jit(solution)/shard_map/ppermute | solution.py:28
  224.7 26.7 %collective-permute-start.28 = (bf16[160,3072]{1,0:T(8,128)(2,1)S(1)}, bf16[160,3072]{1,0:T(8,128)(2,1)S(1)}, u32[]{:S(2)}, u32[]{:S(2)}) collective-permute-start(bf16[160,3072]{1,0:T(8,128)(2,1)S(1)} %get-tuple-element.88), channel_id=1, source_target_pairs={{0,8},{4,12},{8,16},{12,20},{1,9},{5,13},{9,17},{13,21},{2,10},{6,... | collective-permute-start | bytes 2949128 | tf_op jit(solution)/shard_map/ppermute | solution.py:28
  229.3 22.1 %collective-permute-start.31 = (bf16[160,3072]{1,0:T(8,128)(2,1)S(1)}, bf16[160,3072]{1,0:T(8,128)(2,1)S(1)}, u32[]{:S(2)}, u32[]{:S(2)}) collective-permute-start(bf16[160,3072]{1,0:T(8,128)(2,1)S(1)} %get-tuple-element.89), channel_id=1, source_target_pairs={{16,8},{20,12},{24,16},{28,20},{17,9},{21,13},{25,17},{29,21},{18,... | collective-permute-start | bytes 2949128 | tf_op jit(solution)/shard_map/ppermute | solution.py:28
  230.0 28.6 %collective-permute-start.36 = (bf16[160,3072]{1,0:T(8,128)(2,1)S(1)}, bf16[160,3072]{1,0:T(8,128)(2,1)S(1)}, u32[]{:S(2)}, u32[]{:S(2)}) collective-permute-start(bf16[160,3072]{1,0:T(8,128)(2,1)S(1)} %get-tuple-element.92), channel_id=1, source_target_pairs={{24,16},{28,20},{25,17},{29,21},{26,18},{30,22},{27,19},{31,23}} | collective-permute-start | bytes 2949128 | tf_op jit(solution)/shard_map/ppermute | solution.py:28
  230.8 41.7 %collective-permute-start.33 = (bf16[160,3072]{1,0:T(8,128)(2,1)S(1)}, bf16[160,3072]{1,0:T(8,128)(2,1)S(1)}, u32[]{:S(2)}, u32[]{:S(2)}) collective-permute-start(bf16[160,3072]{1,0:T(8,128)(2,1)S(1)} %get-tuple-element.91), channel_id=1, source_target_pairs={{0,8},{4,12},{1,9},{5,13},{2,10},{6,14},{3,11},{7,15}} | collective-permute-start | bytes 2949128 | tf_op jit(solution)/shard_map/ppermute | solution.py:28
  252.1 20.4 %collective-permute-start.32 = (bf16[160,3072]{1,0:T(8,128)(2,1)S(1)}, bf16[160,3072]{1,0:T(8,128)(2,1)S(1)}, u32[]{:S(2)}, u32[]{:S(2)}) collective-permute-start(bf16[160,3072]{1,0:T(8,128)(2,1)S(1)} %get-tuple-element.87), channel_id=1, source_target_pairs={{8,0},{12,4},{16,8},{20,12},{24,16},{28,20},{9,1},{13,5},{17,9},{2... | collective-permute-start | bytes 2949128 | tf_op jit(solution)/shard_map/ppermute | solution.py:28
  253.4 34.4 %collective-permute-start.29 = (bf16[160,3072]{1,0:T(8,128)(2,1)S(1)}, bf16[160,3072]{1,0:T(8,128)(2,1)S(1)}, u32[]{:S(2)}, u32[]{:S(2)}) collective-permute-start(bf16[160,3072]{1,0:T(8,128)(2,1)S(1)} %get-tuple-element.86), channel_id=1, source_target_pairs={{0,8},{4,12},{8,16},{12,20},{16,24},{20,28},{1,9},{5,13},{9,17},{1... | collective-permute-start | bytes 2949128 | tf_op jit(solution)/shard_map/ppermute | solution.py:28
  288.9 19.8 %collective-permute-start.34 = (bf16[160,3072]{1,0:T(8,128)(2,1)S(1)}, bf16[160,3072]{1,0:T(8,128)(2,1)S(1)}, u32[]{:S(2)}, u32[]{:S(2)}) collective-permute-start(bf16[160,3072]{1,0:T(8,128)(2,1)S(1)} %get-tuple-element.85), channel_id=1, source_target_pairs={{0,8},{4,12},{8,16},{12,20},{1,9},{5,13},{9,17},{13,21},{2,10},{6,... | collective-permute-start | bytes 2949128 | tf_op jit(solution)/shard_map/ppermute | solution.py:28
  293.3 15.4 %collective-permute-start.37 = (bf16[160,3072]{1,0:T(8,128)(2,1)S(1)}, bf16[160,3072]{1,0:T(8,128)(2,1)S(1)}, u32[]{:S(2)}, u32[]{:S(2)}) collective-permute-start(bf16[160,3072]{1,0:T(8,128)(2,1)S(1)} %get-tuple-element.84), channel_id=1, source_target_pairs={{16,8},{20,12},{24,16},{28,20},{17,9},{21,13},{25,17},{29,21},{18,... | collective-permute-start | bytes 2949128 | tf_op jit(solution)/shard_map/ppermute | solution.py:28
  309.4 23.8 %collective-permute-start.38 = (bf16[160,3072]{1,0:T(8,128)(2,1)S(1)}, bf16[160,3072]{1,0:T(8,128)(2,1)S(1)}, u32[]{:S(2)}, u32[]{:S(2)}) collective-permute-start(bf16[160,3072]{1,0:T(8,128)(2,1)S(1)} %get-tuple-element.95), channel_id=1, source_target_pairs={{8,0},{12,4},{16,8},{20,12},{24,16},{28,20},{9,1},{13,5},{17,9},{2... | collective-permute-start | bytes 2949128 | tf_op jit(solution)/shard_map/ppermute | solution.py:28
  310.7 27.6 %collective-permute-start.35 = (bf16[160,3072]{1,0:T(8,128)(2,1)S(1)}, bf16[160,3072]{1,0:T(8,128)(2,1)S(1)}, u32[]{:S(2)}, u32[]{:S(2)}) collective-permute-start(bf16[160,3072]{1,0:T(8,128)(2,1)S(1)} %get-tuple-element.94), channel_id=1, source_target_pairs={{0,8},{4,12},{8,16},{12,20},{16,24},{20,28},{1,9},{5,13},{9,17},{1... | collective-permute-start | bytes 2949128 | tf_op jit(solution)/shard_map/ppermute | solution.py:28
  322.2 16.9 %collective-permute-start.39 = (bf16[16,3072]{1,0:T(8,128)(2,1)S(1)}, bf16[16,3072]{1,0:T(8,128)(2,1)S(1)}, u32[]{:S(2)}, u32[]{:S(2)}) collective-permute-start(bf16[16,3072]{1,0:T(8,128)(2,1)S(1)} %slice.196), channel_id=1, source_target_pairs={{0,4},{4,8},{8,12},{12,16},{16,20},{20,24},{24,28},{1,5},{5,9},{9,... | collective-permute-start | bytes 294920 | tf_op jit(solution)/shard_map/ppermute | solution.py:147
  323.9 15.2 %collective-permute-start.40 = (bf16[128,1024]{1,0:T(8,128)(2,1)S(1)}, bf16[128,1024]{1,0:T(8,128)(2,1)S(1)}, u32[]{:S(2)}, u32[]{:S(2)}) collective-permute-start(bf16[128,1024]{1,0:T(8,128)(2,1)S(1)} %fusion.18), channel_id=1, source_target_pairs={{0,4},{4,8},{8,12},{12,16},{16,20},{20,24},{24,28},{1,5},{5,9},{9,... | collective-permute-start | bytes 786440 | tf_op jit(solution)/shard_map/ppermute | solution.py:147
  (64 other events, 439.9 us)

commit v4 on v3

v4 whole, which is shorter than its diff:
```python
import jax
import jax.numpy as jnp
import numpy as np
from jax import lax
from jax.experimental import pallas as pl
from jax.experimental.pallas import tpu as pltpu
from jax.sharding import PartitionSpec as P

CORES = 2
EPS = 1e-06
STAGES = (3, 5)
ROUNDS = ((0, (1, 1), 2, 3, 4, 4), (1, (2, 3), 4, 5, 6, 7))
CHAINS = (1, 2)
LANES = 128
RIM = 16


def pick(stack, index):
    return lax.dynamic_index_in_dim(stack, index, 0, keepdims=False)


def swap(value, count, bits):
    if bits == 0:
        return value
    return lax.ppermute(value, "fsdp", [(j, j ^ bits) for j in range(count)])


def plane_shift(value, edges):
    return lax.ppermute(
        value, "ctx", [(a * CORES + c, b * CORES + c) for a, b in edges for c in range(CORES)]
    )


def dft_matrices(length, taps):
    bins = length // 2 + 1
    room = -(-bins // 8) * 8
    k = np.arange(bins)[:, None]
    angle = 2.0 * np.pi * ((k * np.arange(length)[None, :]) % length) / length
    weight = np.where((k == 0) | (k == length // 2), 1.0, 2.0) / length
    analysis = np.zeros((2, room, length))
    synthesis = np.zeros((2, room, length))
    analysis[:, :bins] = np.stack([np.cos(angle), -np.sin(angle)])
    synthesis[:, :bins] = np.stack([weight * np.cos(angle), -weight * np.sin(angle)])
    return (
        analysis.reshape(2 * room, length).astype(np.float32),
        synthesis.reshape(2 * room, length)[:, taps:].T.astype(np.float32),
    )


def tile(*extents):
    return 2 * LANES if all(e % (2 * LANES) == 0 for e in extents) else LANES


def halves(value):
    high = value.astype(jnp.bfloat16)
    return high, (value - high.astype(jnp.float32)).astype(jnp.bfloat16)


def dot(a, b):
    return jnp.dot(a, b, preferred_element_type=jnp.float32)


def finish_kernel(
    query, key, value, rims, short, long,
    analysis_high, analysis_low, synthesis_high, synthesis_low, out, extended, signal,
):
    row_count = out.shape[0]
    taps = long.shape[0]
    room = analysis_high.shape[0] // 2
    reach = short.shape[0]
    for b, body in enumerate((query, key, value)):
        extended[b, :8] = rims[taps + RIM * b : taps + RIM * (b + 1)].astype(jnp.float32)[RIM - 8 :]
        extended[b, 8:] = body[...].astype(jnp.float32)

    def featurized(b, start, count):
        result = None
        for s in range(reach):
            term = short[s, b : b + 1, :] * extended[b, 8 + start - s : 8 + start - s + count]
            result = term if result is None else result + term
        return result

    signal[:taps] = rims[:taps]
    for start in range(0, row_count, taps):
        gated = featurized(1, start, taps) * featurized(2, start, taps)
        signal[taps + start : 2 * taps + start] = gated.astype(jnp.bfloat16)

    long_high, long_low = halves(long[...])
    tones = (
        dot(analysis_high[:, :taps], long_high)
        + dot(analysis_high[:, :taps], long_low)
        + dot(analysis_low[:, :taps], long_high)
    )
    for start in range(0, row_count, taps):
        block = signal[start : start + 2 * taps]
        spectrum = dot(analysis_high[...], block) + dot(analysis_low[...], block)
        real = spectrum[:room] * tones[:room] - spectrum[room:] * tones[room:]
        imag = spectrum[:room] * tones[room:] + spectrum[room:] * tones[:room]
        high, low = halves(jnp.concatenate([real, imag], axis=0))
        response = (
            dot(synthesis_high[...], high)
            + dot(synthesis_high[...], low)
            + dot(synthesis_low[...], high)
        )
        out[start : start + taps] = (featurized(0, start, taps) * response).astype(out.dtype)


def finish(projected, rims, short_filter, long_filter):
    row_count = projected.shape[0]
    taps, channels = long_filter.shape
    width = tile(channels)
    count = channels // width
    analysis, synthesis = (jnp.asarray(m) for m in dft_matrices(2 * taps, taps))
    constants = (*halves(analysis), *halves(synthesis))

    def branch(b):
        return pl.BlockSpec((row_count, width), lambda i: (0, b * count + i))

    operands = [*[projected] * 3, rims, short_filter, long_filter, *constants]
    specs = (
        [branch(b) for b in range(3)]
        + [
            pl.BlockSpec((rims.shape[0], width), lambda i: (0, i)),
            pl.BlockSpec((short_filter.shape[0], 3, width), lambda i: (0, 0, i)),
            pl.BlockSpec((taps, width), lambda i: (0, i)),
        ]
        + [pl.BlockSpec(m.shape, lambda i: (0, 0)) for m in constants]
    )
    return pl.pallas_call(
        finish_kernel,
        out_shape=jax.ShapeDtypeStruct((row_count, channels), jnp.bfloat16),
        grid=(count,),
        in_specs=specs,
        out_specs=pl.BlockSpec((row_count, width), lambda i: (0, i)),
        scratch_shapes=[
            pltpu.VMEM((3, 8 + row_count, width), jnp.float32),
            pltpu.VMEM((taps + row_count, width), jnp.bfloat16),
        ],
        compiler_params=pltpu.CompilerParams(vmem_limit_bytes=32 * 1024 * 1024),
        cost_estimate=pl.CostEstimate(
            flops=row_count * channels * 5000, bytes_accessed=row_count * channels * 10, transcendentals=0
        ),
    )(*operands)


def passed_rims(last_rows, short_filter, long_count):
    reach = short_filter.shape[0]
    channels = short_filter.shape[2]
    total = last_rows.shape[0]
    branches = [last_rows[:, b * channels : (b + 1) * channels] for b in range(3)]
    mixed = []
    for b in (1, 2):
        rows = branches[b].astype(jnp.float32)
        mixed.append(
            sum(
                short_filter[s, b] * rows[total - long_count - s : total - s] for s in range(reach)
            )
        )
    gated = (mixed[0] * mixed[1]).astype(jnp.bfloat16)
    packed = jnp.concatenate([gated] + [rows[total - RIM :] for rows in branches], axis=0)
    count = lax.axis_size("ctx")
    return lax.ppermute(packed, "ctx", [(i, i + 1) for i in range(count - 1)])


def together(values):
    leaves, tree = jax.tree.flatten(values)
    anywhere = pl.BlockSpec(memory_space=pl.ANY)
    leaves = pl.pallas_call(
        lambda *refs: None,
        out_shape=[jax.ShapeDtypeStruct(leaf.shape, leaf.dtype) for leaf in leaves],
        in_specs=[anywhere] * len(leaves),
        out_specs=[anywhere] * len(leaves),
        input_output_aliases={at: at for at in range(len(leaves))},
    )(*leaves)
    return jax.tree.unflatten(tree, leaves)


def spread_near(value, columns):
    if columns != 4:
        return [swap(value, columns, t) for t in range(1, columns)]
    return [swap(value, columns, 1), swap(value, columns, 2)]


def spread_far(near, columns):
    if columns != 4:
        return []
    half = near[0].shape[-1] // 2
    return [swap(near[1][..., :half], columns, 1), swap(near[0][..., half:], columns, 2)]


def spread_all(value, near, far):
    return [value, *near] + ([jnp.concatenate(far, axis=-1)] if far else [])


def partial_kernel(place, *refs):
    *lefts, own, other, out, joined = refs
    planes, columns, share, depth = joined.shape

    @pl.when(pl.program_id(0) == 0)
    def _():
        for t, left in enumerate(lefts):
            joined[:, place[0] ^ t] = left[...]

    rows = joined[...].reshape(planes * columns * share, depth)
    half = depth // 2
    total = dot(rows[:, :half], own[0]) + dot(rows[:, half:], other[0])
    out[...] = total.astype(out.dtype)


def partial_sums(place, lefts, own, other, size, at):
    _, share, depth = lefts[0].shape
    columns = len(lefts)
    channels = own.shape[2]
    rows = size * columns * share
    weights = pl.BlockSpec((1, own.shape[1], channels), lambda b, _: (b, 0, 0))
    left = pl.BlockSpec(
        (size, share, depth), lambda b, place: (place[1] if at is None else at, 0, 0)
    )
    return pl.pallas_call(
        partial_kernel,
        out_shape=jax.ShapeDtypeStruct((rows, 3 * channels), jnp.bfloat16),
        grid_spec=pltpu.PrefetchScalarGridSpec(
            num_scalar_prefetch=1,
            grid=(3,),
            in_specs=[left] * columns + [weights, weights],
            out_specs=pl.BlockSpec((rows, channels), lambda b, _: (0, b)),
            scratch_shapes=[pltpu.VMEM((size, columns, share, depth), jnp.bfloat16)],
        ),
        compiler_params=pltpu.CompilerParams(vmem_limit_bytes=56 * 1024 * 1024),
        cost_estimate=pl.CostEstimate(
            flops=2 * rows * depth * 3 * channels,
            bytes_accessed=2 * rows * depth + 6 * depth * channels + 6 * rows * channels,
            transcendentals=0,
        ),
    )(place, *lefts, own, other).reshape(size, columns * share, 3 * channels)


def on_device(tokens, gain, in_weight, short_filter, long_filter):
    planes = lax.axis_size("ctx") // CORES
    columns = lax.axis_size("fsdp")
    plane = lax.axis_index("ctx") // CORES
    core = lax.axis_index("ctx") % CORES
    column = lax.axis_index("fsdp")
    early_half = plane < planes // 2
    place = jnp.stack([column, jnp.where(early_half, 0, 1)]).astype(jnp.int32)
    row_count, width = tokens.shape
    long_count = long_filter.shape[0]

    parts = STAGES
    if row_count % (sum(parts) * columns * RIM):
        parts = (1, 1)
    unit = row_count // sum(parts)
    sizes = [unit * part for part in parts]
    stages = [(row_count - sizes[0], sizes[0]), (0, sizes[1])]

    weight = jnp.transpose(in_weight, (1, 0, 2))
    other_weight = lax.ppermute(
        weight,
        "ctx",
        [(p * CORES + c, p * CORES + 1 - c) for p in range(planes) for c in range(CORES)],
    )

    gains = gain.reshape(columns, width)
    gain_here = jnp.stack([pick(gains, column ^ t) for t in range(columns)])[:, None, :]

    def to_trade(stage):
        start, size = stages[stage]
        rows = tokens[start : start + size].reshape(columns, -1, width)
        return [pick(rows, column ^ t) for t in range(columns)]

    def trade(pieces):
        return [swap(piece, columns, t) for t, piece in enumerate(pieces)]

    def normalize(wide):
        wide = jnp.stack(wide).astype(jnp.float32)
        mean_square = jnp.sum(wide * wide, axis=(0, 2), keepdims=True) / (columns * width)
        normed = (wide * lax.rsqrt(mean_square + EPS) * gain_here).astype(jnp.bfloat16)
        return jnp.where(core == 0, normed, jnp.roll(normed, width // 2, axis=2))

    def to_planes(normed, distances):
        rows_of = {}
        for d in distances:
            piece = pick(normed, column ^ ((plane + d) % planes))
            rows_of[planes - d] = plane_shift(piece, [(p, (p + d) % planes) for p in range(planes)])
        return rows_of

    def send_sums(step, terms, arrived, sent=None):
        def onward(term, came):
            if came is None:
                return term
            return (term.astype(jnp.float32) + came.astype(jnp.float32)).astype(jnp.bfloat16)

        right = [(p, p + 1) for p in range(planes - 1) if p < step]
        left = [(p, p - 1) for p in range(1, planes) if p >= planes - step]
        if 2 * step < planes:
            if sent is None:
                sent = jnp.where(early_half, terms[planes - step], terms[step])
            return [plane_shift(onward(sent, arrived[0]), right + left)]
        return [
            plane_shift(onward(terms[planes - step], arrived[0]), right),
            plane_shift(onward(terms[step], arrived[-1]), left),
        ]

    count, steps = len(stages), planes - 1
    order = [m for k in range(1, planes // 2) for m in (planes - k, k)] + [planes // 2, 0]
    around = [planes // 2], [d for d in range(1, planes) if d != planes // 2]
    chains, sums = {}, {}
    normed, rows_of, own, lefts = {}, {}, {}, {}

    def product(stage, size, at):
        return partial_sums(place, lefts[stage], weight, other_weight, size, at)

    def split(stage, blocks):
        terms = [block for part in blocks for block in part]
        rows = stages[stage][1] // CHAINS[stage]
        chains[stage] = [
            [terms[order.index(m)][part * rows : (part + 1) * rows] for m in range(planes)]
            for part in range(CHAINS[stage])
        ]
        sums[stage] = [[None]] * CHAINS[stage]

    live = {f"pieces{stage}": to_trade(stage) for stage in range(count)}
    for now in range(ROUNDS[-1][-1]):
        fresh = {"weight": other_weight} if now == 0 else {}
        for stage, (to_shares, across, near, far, ready, first) in enumerate(ROUNDS):
            if now < to_shares:
                fresh[f"pieces{stage}"] = live[f"pieces{stage}"]
            if now == to_shares:
                fresh[f"trade{stage}"] = trade(live[f"pieces{stage}"])
            if now == across[0]:
                normed[stage] = normalize(live[f"trade{stage}"])
                rows_of[stage] = {0: pick(normed[stage], column ^ plane)}
            for at, distances in zip(across, around):
                if now == at:
                    fresh[f"planes{stage}{distances[0]}"] = to_planes(normed[stage], distances)
            if now == near:
                own[stage] = jnp.stack([rows_of[stage][m] for m in order])
                fresh[f"near{stage}"] = spread_near(own[stage], columns)
            if now == far:
                fresh[f"near{stage}"] = live[f"near{stage}"]
                fresh[f"far{stage}"] = spread_far(live[f"near{stage}"], columns)
            if now == ready:
                lefts[stage] = spread_all(own[stage], live[f"near{stage}"], live[f"far{stage}"])
                if now == first:
                    lead = product(stage, 1, None)[0]
                    split(stage, [product(stage, planes, 0)])
                    fresh[f"sums{stage}"] = [send_sums(1, chains[stage][0], [None], lead)]
                else:
                    fresh[f"lead{stage}"] = product(stage, planes // 2, 0)
            if first < now < first + steps:
                fresh[f"sums{stage}"] = [
                    send_sums(now - first + 1, terms, arrived)
                    for terms, arrived in zip(chains[stage], sums[stage])
                ]
        live = together(fresh)
        other_weight = live.pop("weight", other_weight)
        for stage in range(count):
            for distances in around:
                rows_of.get(stage, {}).update(live.pop(f"planes{stage}{distances[0]}", {}))
            if f"sums{stage}" in live:
                sums[stage] = live.pop(f"sums{stage}")

    last = count - 1
    split(last, [live[f"lead{last}"], product(last, planes // 2, 1)])
    for step in range(1, planes):
        sums[last] = [
            send_sums(step, terms, arrived) for terms, arrived in zip(chains[last], sums[last])
        ]

    def summed(stage):
        parts = []
        for terms, arrived in zip(chains[stage], sums[stage]):
            total = terms[0].astype(jnp.float32)
            total = total + arrived[0].astype(jnp.float32) + arrived[-1].astype(jnp.float32)
            parts.append(total.astype(jnp.bfloat16))
        return parts

    (last_rows,) = summed(0)
    rims = passed_rims(last_rows, short_filter, long_count)
    projected = jnp.concatenate([*summed(1), last_rows], axis=0)
    return finish(projected, rims, short_filter, long_filter)


def solution(mesh):
    return jax.shard_map(
        on_device,
        mesh=mesh,
        in_specs=(
            P("ctx", "fsdp"),
            P(),
            P("ctx", None, "fsdp"),
            P(None, None, "fsdp"),
            P(None, "fsdp"),
        ),
        out_specs=P("ctx", "fsdp"),
        check_vma=False,
    )
```

time: 348 us -> 337 us (0.968)
  starting transfers between devices: 88.3 us -> 76.4 us
  waiting for transfers between devices: 167 us -> 158 us
  Pallas kernels: 51.1 us -> 59 us
  other arithmetic: 17.6 us -> 22.7 us
  local copies, waits for them, and re-layouts: 22.7 us -> 18.6 us
    ppermute x24 -> x21, waiting for transfers between devices: 147 us -> 138 us  [plane_shift(): lax.ppermute(value, 'ctx', [(a * CORES + c, b * CORES + c) for a, b in ed...]
    pallas_call x4, Pallas kernels: 43.7 us -> 51.6 us  [partial_sums(): pl.pallas_call(partial_kernel, out_shape=jax.ShapeDtypeStruct((rows, 3 *...]
    ppermute x24 -> x21, starting transfers between devices: 65.5 us -> 58 us  [plane_shift(): lax.ppermute(value, 'ctx', [(a * CORES + c, b * CORES + c) for a, b in ed...]
    ppermute x3 -> x2, starting transfers between devices: 6.35 us -> 1.76 us  [the longest x1 1.31 us: passed_rims(): return lax.ppermute(packed, 'ctx', [(i, i + 1) for i in range(count - 1)])]
    unnamed x108 -> x114, local copies, waits for them, and re-layouts: 10.6 us -> 12.6 us
  transfers between devices with their start and end apart: 41 -> 37, of which waited for: 18 -> 20; matrix products, arithmetic and copies ran while one was open for 3% -> 3% of each run, Pallas kernels for 13% -> 15%
where the time goes in v4:
time: 337 us; the launch traced here: 336 us
  waiting for transfers between devices  158 us (47%)
  starting transfers between devices  76.4 us (23%)
  Pallas kernels  59 us (18%)
  other arithmetic  22.7 us (7%)
  local copies, waits for them, and re-layouts  18.6 us (6%)
    ppermute x21, waiting for transfers between devices, plane_shift(): lax.ppermute(value, 'ctx', [(a * CORES + c, b * CORES + c) for a, b in ed...  138 us
    ppermute x21, starting transfers between devices, plane_shift(): lax.ppermute(value, 'ctx', [(a * CORES + c, b * CORES + c) for a, b in ed...  58 us
    pallas_call x4, Pallas kernels, partial_sums(): pl.pallas_call(partial_kernel, out_shape=jax.ShapeDtypeStruct((rows, 3 *...  51.6 us
    ppermute x14, waiting for transfers between devices, swap(): return lax.ppermute(value, 'fsdp', [(j, j ^ bits) for j in range(count)])  20 us
    ppermute x14, starting transfers between devices, swap(): return lax.ppermute(value, 'fsdp', [(j, j ^ bits) for j in range(count)])  16.6 us
    unnamed x114, local copies, waits for them, and re-layouts  12.6 us
    convert_element_type x5, other arithmetic, onward(): (term.astype(jnp.float32) + came.astype(jnp.float32)).astype(jnp.bfloat16)  8.36 us
    pallas_call x1, Pallas kernels, finish(): pl.pallas_call(finish_kernel, out_shape=jax.ShapeDtypeStruct((row_count,...  7.35 us
  transfers between devices with their start and end apart: 37, of which 20 were waited for; matrix products, arithmetic and copies ran while one was open for 3% of the time, Pallas kernels for 15%

profile of v4, /device:TPU:0, one launch (start us, length us, event | category | flops | bytes accessed | tf_op | source)
XLA Modules:
  0.0 335.7 jit_solution(2086209914895897569)
XLA Ops:
  1.9 3.9 %collective-permute-start.2 = (bf16[48,2048]{1,0:T(8,128)(2,1)S(1)}, bf16[48,2048]{1,0:T(8,128)(2,1)S(1)}, u32[]{:S(2)}, u32[]{:S(2)}) collective-permute-start(bf16[48,2048]{1,0:T(8,128)(2,1)S(1)} %get-tuple-element.110), channel_id=1, source_target_pairs={{0,3},{1,2},{2,1},{3,0},{4,7},{5,6},{6,5},{7,4},{8,11},{9,10},{10,... | collective-permute-start | bytes 589832 | tf_op jit(solution)/shard_map/ppermute | solution.py:25
  7.6 4.0 %collective-permute-done.2.refs_7_ = bf16[48,2048]{1,0:T(8,128)(2,1)S(1)} collective-permute-done((bf16[48,2048]{1,0:T(8,128)(2,1)S(1)}, bf16[48,2048]{1,0:T(8,128)(2,1)S(1)}, u32[]{:S(2)}, u32[]{:S(2)}) %collective-permute-start.2) | collective-permute-done | bytes 196640 | tf_op jit(solution)/shard_map/ppermute | solution.py:25
  11.6 3.3 collective-permute-done.1.refs_6_
  27.3 8.9 %collective-permute-done.6.refs_2_ = bf16[48,2048]{1,0:T(8,128)(2,1)S(1)} collective-permute-done((bf16[48,2048]{1,0:T(8,128)(2,1)S(1)}, bf16[48,2048]{1,0:T(8,128)(2,1)S(1)}, u32[]{:S(2)}, u32[]{:S(2)}) %collective-permute-start.6) | collective-permute-done | bytes 196640 | tf_op jit(solution)/shard_map/ppermute | solution.py:29
  36.2 5.7 %collective-permute-done.4.refs_0_ = bf16[48,2048]{1,0:T(8,128)(2,1)S(1)} collective-permute-done((bf16[48,2048]{1,0:T(8,128)(2,1)S(1)}, bf16[48,2048]{1,0:T(8,128)(2,1)S(1)}, u32[]{:S(2)}, u32[]{:S(2)}) %collective-permute-start.4) | collective-permute-done | bytes 196640 | tf_op jit(solution)/shard_map/ppermute | solution.py:29
  48.7 14.4 %collective-permute-done.12.refs_2_ = bf16[80,2048]{1,0:T(8,128)(2,1)S(1)} collective-permute-done((bf16[80,2048]{1,0:T(8,128)(2,1)S(1)}, bf16[80,2048]{1,0:T(8,128)(2,1)S(1)}, u32[]{:S(2)}, u32[]{:S(2)}) %collective-permute-start.12) | collective-permute-done | bytes 327712 | tf_op jit(solution)/shard_map/ppermute | solution.py:29
  69.3 3.8 %collective-permute-start.15 = (bf16[80,2048]{1,0:T(8,128)(2,1)}, bf16[80,2048]{1,0:T(8,128)(2,1)S(1)}, u32[]{:S(2)}, u32[]{:S(2)}) collective-permute-start(bf16[80,2048]{1,0:T(8,128)(2,1)} %get-tuple-element.91), channel_id=1, source_target_pairs={{0,24},{4,28},{8,0},{12,4},{16,8},{20,12},{24,16},{28,20},{1,25},{... | collective-permute-start | bytes 983048 | tf_op jit(solution)/shard_map/ppermute | solution.py:29
  73.8 8.2 %collective-permute-done.16.refs_5_ = bf16[80,2048]{1,0:T(8,128)(2,1)S(1)} collective-permute-done((bf16[80,2048]{1,0:T(8,128)(2,1)}, bf16[80,2048]{1,0:T(8,128)(2,1)S(1)}, u32[]{:S(2)}, u32[]{:S(2)}) %collective-permute-start.16) | collective-permute-done | bytes 327712 | tf_op jit(solution)/shard_map/ppermute | solution.py:29
  82.0 3.6 %collective-permute-done.15.refs_4_ = bf16[80,2048]{1,0:T(8,128)(2,1)S(1)} collective-permute-done((bf16[80,2048]{1,0:T(8,128)(2,1)}, bf16[80,2048]{1,0:T(8,128)(2,1)S(1)}, u32[]{:S(2)}, u32[]{:S(2)}) %collective-permute-start.15) | collective-permute-done | bytes 327712 | tf_op jit(solution)/shard_map/ppermute | solution.py:29
  91.7 8.5 %shard_map.77 = bf16[192,3072]{1,0:T(8,128)(2,1)} custom-call(s32[2]{0:T(128)} %pad_add_fusion.place, bf16[4,48,2048]{2,1,0:T(8,128)(2,1)} %copy-done.27, bf16[4,48,2048]{2,1,0:T(8,128)(2,1)} %get-tuple-element.62.refs_1_, bf16[4,48,2048]{2,1,0:T(8,128)(2,1)} %get-tuple-element.63.refs_2_, bf16[4,48,2048]{2,1,0:T(8,128)(2,1)} %copy-done.38, ...), custom_call_target="tpu_custom_call" | custom-call | flops 2415919104 | bytes 14548992 | tf_op jit(solution)/shard_map/pallas_call | solution.py:218
  102.5 15.5 %shard_map.79 = bf16[768,3072]{1,0:T(8,128)(2,1)} custom-call(s32[2]{0:T(128)} %pad_add_fusion.place, bf16[4,48,2048]{2,1,0:T(8,128)(2,1)} %copy-done.27, bf16[4,48,2048]{2,1,0:T(8,128)(2,1)} %get-tuple-element.62.refs_1_, bf16[4,48,2048]{2,1,0:T(8,128)(2,1)} %get-tuple-element.63.refs_2_, bf16[4,48,2048]{2,1,0:T(8,128)(2,1)} %copy-done.38, ...), custom_call_target="tpu_custom_call" | custom-call | flops 9663676416 | bytes 20447232 | tf_op jit(solution)/shard_map/pallas_call | solution.py:218
  118.0 8.1 %collective-permute-done.19.refs_2_ = bf16[192,3072]{1,0:T(8,128)(2,1)S(1)} collective-permute-done((bf16[192,3072]{1,0:T(8,128)(2,1)}, bf16[192,3072]{1,0:T(8,128)(2,1)S(1)}, u32[]{:S(2)}, u32[]{:S(2)}) %collective-permute-start.19) | collective-permute-done | bytes 1179680 | tf_op jit(solution)/shard_map/ppermute | solution.py:29
  133.3 4.9 %collective-permute-start.22 = (bf16[192,3072]{1,0:T(8,128)(2,1)S(1)}, bf16[192,3072]{1,0:T(8,128)(2,1)}, u32[]{:S(2)}, u32[]{:S(2)}) collective-permute-start(bf16[192,3072]{1,0:T(8,128)(2,1)S(1)} %add_convert_fusion.3), channel_id=1, source_target_pairs={{0,8},{4,12},{8,16},{12,20},{1,9},{5,13},{9,17},{13,21},{2,10},{6,... | collective-permute-start | bytes 3538952 | tf_op jit(solution)/shard_map/ppermute | solution.py:29
  140.7 11.0 %collective-permute-done.21.refs_1_ = bf16[4,80,1024]{2,1,0:T(8,128)(2,1)S(1)} collective-permute-done((bf16[4,80,1024]{2,1,0:T(8,128)(2,1)S(1)}, bf16[4,80,1024]{2,1,0:T(8,128)(2,1)S(1)}, u32[]{:S(2)}, u32[]{:S(2)}) %collective-permute-start.21) | collective-permute-done | bytes 655392 | tf_op jit(solution)/shard_map/ppermute | solution.py:25
  153.2 6.4 %collective-permute-done.22.refs_4_ = bf16[192,3072]{1,0:T(8,128)(2,1)} collective-permute-done((bf16[192,3072]{1,0:T(8,128)(2,1)S(1)}, bf16[192,3072]{1,0:T(8,128)(2,1)}, u32[]{:S(2)}, u32[]{:S(2)}) %collective-permute-start.22) | collective-permute-done | bytes 1179680 | tf_op jit(solution)/shard_map/ppermute | solution.py:29
  159.6 3.3 add_convert_fusion.1
  164.3 6.1 %collective-permute-start.24 = (bf16[192,3072]{1,0:T(8,128)(2,1)S(1)}, bf16[192,3072]{1,0:T(8,128)(2,1)S(1)}, u32[]{:S(2)}, u32[]{:S(2)}) collective-permute-start(bf16[192,3072]{1,0:T(8,128)(2,1)S(1)} %get-tuple-element.80), channel_id=1, source_target_pairs={{0,8},{4,12},{8,16},{12,20},{16,24},{20,28},{1,9},{5,13},{9,17},{1... | collective-permute-start | bytes 3538952 | tf_op jit(solution)/shard_map/ppermute | solution.py:29
  171.6 13.6 %shard_map.82 = bf16[640,3072]{1,0:T(8,128)(2,1)} custom-call(s32[2]{0:T(128)} %pad_add_fusion.place, bf16[4,80,2048]{2,1,0:T(8,128)(2,1)} %copy-done.48, bf16[4,80,2048]{2,1,0:T(8,128)(2,1)} %get-tuple-element.70.refs_1_, bf16[4,80,2048]{2,1,0:T(8,128)(2,1)} %get-tuple-element.71.refs_2_, bf16[4,80,2048]{2,1,0:T(8,128)(2,1)} %copy-done.54, ...), custom_call_target="tpu_custom_call" | custom-call | flops 8053063680 | bytes 19136512 | tf_op jit(solution)/shard_map/pallas_call | solution.py:218
  185.2 5.3 %collective-permute-done.25.refs_2_ = bf16[192,3072]{1,0:T(8,128)(2,1)S(1)} collective-permute-done((bf16[192,3072]{1,0:T(8,128)(2,1)S(1)}, bf16[192,3072]{1,0:T(8,128)(2,1)S(1)}, u32[]{:S(2)}, u32[]{:S(2)}) %collective-permute-start.25) | collective-permute-done | bytes 1179680 | tf_op jit(solution)/shard_map/ppermute | solution.py:29
  195.0 4.6 %collective-permute-start.26 = (bf16[160,3072]{1,0:T(8,128)(2,1)S(1)}, bf16[160,3072]{1,0:T(8,128)(2,1)S(1)}, u32[]{:S(2)}, u32[]{:S(2)}) collective-permute-start(bf16[160,3072]{1,0:T(8,128)(2,1)S(1)} %get-tuple-element.85), channel_id=1, source_target_pairs={{0,8},{4,12},{24,16},{28,20},{1,9},{5,13},{25,17},{29,21},{2,10},{... | collective-permute-start | bytes 2949128 | tf_op jit(solution)/shard_map/ppermute | solution.py:29
  199.5 14.1 %shard_map.81 = bf16[640,3072]{1,0:T(8,128)(2,1)} custom-call(s32[2]{0:T(128)} %pad_add_fusion.place, bf16[4,80,2048]{2,1,0:T(8,128)(2,1)} %copy-done.48, bf16[4,80,2048]{2,1,0:T(8,128)(2,1)} %get-tuple-element.70.refs_1_, bf16[4,80,2048]{2,1,0:T(8,128)(2,1)} %get-tuple-element.71.refs_2_, bf16[4,80,2048]{2,1,0:T(8,128)(2,1)} %copy-done.54, ...), custom_call_target="tpu_custom_call" | custom-call | flops 8053063680 | bytes 19136512 | tf_op jit(solution)/shard_map/pallas_call | solution.py:218
  218.1 5.0 %collective-permute-start.27 = (bf16[160,3072]{1,0:T(8,128)(2,1)S(1)}, bf16[160,3072]{1,0:T(8,128)(2,1)S(1)}, u32[]{:S(2)}, u32[]{:S(2)}) collective-permute-start(bf16[160,3072]{1,0:T(8,128)(2,1)S(1)} %add_convert_fusion.7), channel_id=1, source_target_pairs={{0,8},{4,12},{8,16},{12,20},{1,9},{5,13},{9,17},{13,21},{2,10},{6,... | collective-permute-start | bytes 2949128 | tf_op jit(solution)/shard_map/ppermute | solution.py:29
  223.2 5.3 %collective-permute-start.31 = (bf16[160,3072]{1,0:T(8,128)(2,1)S(1)}, bf16[160,3072]{1,0:T(8,128)(2,1)S(1)}, u32[]{:S(2)}, u32[]{:S(2)}) collective-permute-start(bf16[160,3072]{1,0:T(8,128)(2,1)S(1)} %get-tuple-element.86), channel_id=1, source_target_pairs={{0,8},{4,12},{24,16},{28,20},{1,9},{5,13},{25,17},{29,21},{2,10},{... | collective-permute-start | bytes 2949128 | tf_op jit(solution)/shard_map/ppermute | solution.py:29
  228.5 16.8 %collective-permute-done.27 = bf16[160,3072]{1,0:T(8,128)(2,1)S(1)} collective-permute-done((bf16[160,3072]{1,0:T(8,128)(2,1)S(1)}, bf16[160,3072]{1,0:T(8,128)(2,1)S(1)}, u32[]{:S(2)}, u32[]{:S(2)}) %collective-permute-start.27) | collective-permute-done | bytes 983072 | tf_op jit(solution)/shard_map/ppermute | solution.py:29
  246.0 4.4 %collective-permute-start.28 = (bf16[160,3072]{1,0:T(8,128)(2,1)S(1)}, bf16[160,3072]{1,0:T(8,128)(2,1)S(1)}, u32[]{:S(2)}, u32[]{:S(2)}) collective-permute-start(bf16[160,3072]{1,0:T(8,128)(2,1)S(1)} %get-tuple-element.83), channel_id=1, source_target_pairs={{0,8},{4,12},{8,16},{12,20},{16,24},{20,28},{1,9},{5,13},{9,17},{1... | collective-permute-start | bytes 2949128 | tf_op jit(solution)/shard_map/ppermute | solution.py:29
  251.9 14.5 %collective-permute-done.31 = bf16[160,3072]{1,0:T(8,128)(2,1)S(1)} collective-permute-done((bf16[160,3072]{1,0:T(8,128)(2,1)S(1)}, bf16[160,3072]{1,0:T(8,128)(2,1)S(1)}, u32[]{:S(2)}, u32[]{:S(2)}) %collective-permute-start.31) | collective-permute-done | bytes 983072 | tf_op jit(solution)/shard_map/ppermute | solution.py:29
  266.3 14.4 %collective-permute-done.28 = bf16[160,3072]{1,0:T(8,128)(2,1)S(1)} collective-permute-done((bf16[160,3072]{1,0:T(8,128)(2,1)S(1)}, bf16[160,3072]{1,0:T(8,128)(2,1)S(1)}, u32[]{:S(2)}, u32[]{:S(2)}) %collective-permute-start.28) | collective-permute-done | bytes 983072 | tf_op jit(solution)/shard_map/ppermute | solution.py:29
  282.3 5.0 %collective-permute-start.32 = (bf16[160,3072]{1,0:T(8,128)(2,1)S(1)}, bf16[160,3072]{1,0:T(8,128)(2,1)S(1)}, u32[]{:S(2)}, u32[]{:S(2)}) collective-permute-start(bf16[160,3072]{1,0:T(8,128)(2,1)S(1)} %get-tuple-element.82), channel_id=1, source_target_pairs={{0,8},{4,12},{8,16},{12,20},{1,9},{5,13},{9,17},{13,21},{2,10},{6,... | collective-permute-start | bytes 2949128 | tf_op jit(solution)/shard_map/ppermute | solution.py:29
  287.4 16.7 %collective-permute-done.32 = bf16[160,3072]{1,0:T(8,128)(2,1)S(1)} collective-permute-done((bf16[160,3072]{1,0:T(8,128)(2,1)S(1)}, bf16[160,3072]{1,0:T(8,128)(2,1)S(1)}, u32[]{:S(2)}, u32[]{:S(2)}) %collective-permute-start.32) | collective-permute-done | bytes 983072 | tf_op jit(solution)/shard_map/ppermute | solution.py:29
  304.7 5.0 %collective-permute-start.33 = (bf16[160,3072]{1,0:T(8,128)(2,1)S(1)}, bf16[160,3072]{1,0:T(8,128)(2,1)S(1)}, u32[]{:S(2)}, u32[]{:S(2)}) collective-permute-start(bf16[160,3072]{1,0:T(8,128)(2,1)S(1)} %get-tuple-element.87), channel_id=1, source_target_pairs={{0,8},{4,12},{8,16},{12,20},{16,24},{20,28},{1,9},{5,13},{9,17},{1... | collective-permute-start | bytes 2949128 | tf_op jit(solution)/shard_map/ppermute | solution.py:29
  314.8 11.9 %collective-permute-done.33 = bf16[160,3072]{1,0:T(8,128)(2,1)S(1)} collective-permute-done((bf16[160,3072]{1,0:T(8,128)(2,1)S(1)}, bf16[160,3072]{1,0:T(8,128)(2,1)S(1)}, u32[]{:S(2)}, u32[]{:S(2)}) %collective-permute-start.33) | collective-permute-done | bytes 983072 | tf_op jit(solution)/shard_map/ppermute | solution.py:29
  328.3 7.4 %shard_map.84 = bf16[512,1024]{1,0:T(8,128)(2,1)} custom-call(bf16[512,3072]{1,0:T(8,128)(2,1)S(1)} %pad_maximum_fusion.query.key.value, bf16[512,3072]{1,0:T(8,128)(2,1)S(1)} %pad_maximum_fusion.query.key.value, bf16[512,3072]{1,0:T(8,128)(2,1)S(1)} %pad_maximum_fusion.query.key.value, bf16[176,1024]{1,0:T(8,128)(2,1)S(1)} %collective-permute-done.36.rims, ...), custom_call_target="tpu_custom_call" | custom-call | flops 2621440000 | bytes 5242880 | tf_op jit(solution)/shard_map/pallas_call | solution.py:128
  (213 shorter events, 71.6 us)
Async XLA Ops:
  0.0 15.2 %collective-permute-start.3 = (bf16[3,1024,1024]{2,1,0:T(8,128)(2,1)}, bf16[3,1024,1024]{2,1,0:T(8,128)(2,1)}, u32[]{:S(2)}, u32[]{:S(2)}) collective-permute-start(bf16[3,1024,1024]{2,1,0:T(8,128)(2,1)} %bitcast.74), channel_id=1, source_target_pairs={{0,4},{4,0},{8,12},{12,8},{16,20},{20,16},{24,28},{28,24},{1,5},{5... | collective-permute-start | bytes 18874376 | tf_op jit(solution)/shard_map/ppermute | solution.py:256
  19.6 16.6 %collective-permute-start.6 = (bf16[48,2048]{1,0:T(8,128)(2,1)S(1)}, bf16[48,2048]{1,0:T(8,128)(2,1)S(1)}, u32[]{:S(2)}, u32[]{:S(2)}) collective-permute-start(bf16[48,2048]{1,0:T(8,128)(2,1)S(1)} %get-tuple-element.105), channel_id=1, source_target_pairs={{0,16},{4,20},{8,24},{12,28},{16,0},{20,4},{24,8},{28,12},{1,17},{... | collective-permute-start | bytes 589832 | tf_op jit(solution)/shard_map/ppermute | solution.py:29
  22.2 19.6 %collective-permute-start.7 = (bf16[80,2048]{1,0:T(8,128)(2,1)S(1)}, bf16[80,2048]{1,0:T(8,128)(2,1)S(1)}, u32[]{:S(2)}, u32[]{:S(2)}) collective-permute-start(bf16[80,2048]{1,0:T(8,128)(2,1)S(1)} %copy-done.45), channel_id=1, source_target_pairs={{0,1},{1,0},{2,3},{3,2},{4,5},{5,4},{6,7},{7,6},{8,9},{9,8},{10,11... | collective-permute-start | bytes 983048 | tf_op jit(solution)/shard_map/ppermute | solution.py:25
  23.7 18.1 %collective-permute-start.8 = (bf16[80,2048]{1,0:T(8,128)(2,1)S(1)}, bf16[80,2048]{1,0:T(8,128)(2,1)S(1)}, u32[]{:S(2)}, u32[]{:S(2)}) collective-permute-start(bf16[80,2048]{1,0:T(8,128)(2,1)S(1)} %copy-done.44), channel_id=1, source_target_pairs={{0,2},{1,3},{2,0},{3,1},{4,6},{5,7},{6,4},{7,5},{8,10},{9,11},{10,... | collective-permute-start | bytes 983048 | tf_op jit(solution)/shard_map/ppermute | solution.py:25
  24.5 17.3 %collective-permute-start.9 = (bf16[80,2048]{1,0:T(8,128)(2,1)S(1)}, bf16[80,2048]{1,0:T(8,128)(2,1)S(1)}, u32[]{:S(2)}, u32[]{:S(2)}) collective-permute-start(bf16[80,2048]{1,0:T(8,128)(2,1)S(1)} %copy-done.43), channel_id=1, source_target_pairs={{0,3},{1,2},{2,1},{3,0},{4,7},{5,6},{6,5},{7,4},{8,11},{9,10},{10,... | collective-permute-start | bytes 983048 | tf_op jit(solution)/shard_map/ppermute | solution.py:25
  25.7 10.4 %collective-permute-start.5 = (bf16[48,2048]{1,0:T(8,128)(2,1)S(1)}, bf16[48,2048]{1,0:T(8,128)(2,1)S(1)}, u32[]{:S(2)}, u32[]{:S(2)}) collective-permute-start(bf16[48,2048]{1,0:T(8,128)(2,1)S(1)} %get-tuple-element.106), channel_id=1, source_target_pairs={{0,8},{4,12},{8,16},{12,20},{16,24},{20,28},{24,0},{28,4},{1,9},{5... | collective-permute-start | bytes 589832 | tf_op jit(solution)/shard_map/ppermute | solution.py:29
  44.2 19.0 %collective-permute-start.11 = (bf16[4,48,2048]{2,1,0:T(8,128)(2,1)S(1)}, bf16[4,48,2048]{2,1,0:T(8,128)(2,1)S(1)}, u32[]{:S(2)}, u32[]{:S(2)}) collective-permute-start(bf16[4,48,2048]{2,1,0:T(8,128)(2,1)S(1)} %pad_maximum_fusion.4.refs_0_), channel_id=1, source_target_pairs={{0,2},{1,3},{2,0},{3,1},{4,6},{5,7},{6,4},{7,5},{8,10},{9,11},{10,... | collective-permute-start | bytes 2359304 | tf_op jit(solution)/shard_map/ppermute | solution.py:25
  45.8 17.4 %collective-permute-start.10 = (bf16[4,48,2048]{2,1,0:T(8,128)(2,1)S(1)}, bf16[4,48,2048]{2,1,0:T(8,128)(2,1)S(1)}, u32[]{:S(2)}, u32[]{:S(2)}) collective-permute-start(bf16[4,48,2048]{2,1,0:T(8,128)(2,1)S(1)} %pad_maximum_fusion.4.refs_0_), channel_id=1, source_target_pairs={{0,1},{1,0},{2,3},{3,2},{4,5},{5,4},{6,7},{7,6},{8,9},{9,8},{10,11... | collective-permute-start | bytes 2359304 | tf_op jit(solution)/shard_map/ppermute | solution.py:25
  48.7 14.4 %collective-permute-start.12 = (bf16[80,2048]{1,0:T(8,128)(2,1)S(1)}, bf16[80,2048]{1,0:T(8,128)(2,1)S(1)}, u32[]{:S(2)}, u32[]{:S(2)}) collective-permute-start(bf16[80,2048]{1,0:T(8,128)(2,1)S(1)} %get-tuple-element.92), channel_id=1, source_target_pairs={{0,16},{4,20},{8,24},{12,28},{16,0},{20,4},{24,8},{28,12},{1,17},{... | collective-permute-start | bytes 983048 | tf_op jit(solution)/shard_map/ppermute | solution.py:29
  67.2 18.4 %collective-permute-start.14 = (bf16[4,48,1024]{2,1,0:T(8,128)(2,1)S(1)}, bf16[4,48,1024]{2,1,0:T(8,128)(2,1)S(1)}, u32[]{:S(2)}, u32[]{:S(2)}) collective-permute-start(bf16[4,48,1024]{2,1,0:T(8,128)(2,1)S(1)} %slice.140), channel_id=1, source_target_pairs={{0,2},{1,3},{2,0},{3,1},{4,6},{5,7},{6,4},{7,5},{8,10},{9,11},{10,... | collective-permute-start | bytes 1179656 | tf_op jit(solution)/shard_map/ppermute | solution.py:25
  68.9 16.7 %collective-permute-start.13 = (bf16[4,48,1024]{2,1,0:T(8,128)(2,1)S(1)}, bf16[4,48,1024]{2,1,0:T(8,128)(2,1)S(1)}, u32[]{:S(2)}, u32[]{:S(2)}) collective-permute-start(bf16[4,48,1024]{2,1,0:T(8,128)(2,1)S(1)} %slice.139), channel_id=1, source_target_pairs={{0,1},{1,0},{2,3},{3,2},{4,5},{5,4},{6,7},{7,6},{8,9},{9,8},{10,11... | collective-permute-start | bytes 1179656 | tf_op jit(solution)/shard_map/ppermute | solution.py:25
  69.3 12.7 %collective-permute-start.16 = (bf16[80,2048]{1,0:T(8,128)(2,1)}, bf16[80,2048]{1,0:T(8,128)(2,1)S(1)}, u32[]{:S(2)}, u32[]{:S(2)}) collective-permute-start(bf16[80,2048]{1,0:T(8,128)(2,1)} %get-tuple-element.89), channel_id=1, source_target_pairs={{0,8},{4,12},{8,16},{12,20},{16,24},{20,28},{24,0},{28,4},{1,9},{5... | collective-permute-start | bytes 983048 | tf_op jit(solution)/shard_map/ppermute | solution.py:29
  69.3 16.3 %collective-permute-start.15 = (bf16[80,2048]{1,0:T(8,128)(2,1)}, bf16[80,2048]{1,0:T(8,128)(2,1)S(1)}, u32[]{:S(2)}, u32[]{:S(2)}) collective-permute-start(bf16[80,2048]{1,0:T(8,128)(2,1)} %get-tuple-element.91), channel_id=1, source_target_pairs={{0,24},{4,28},{8,0},{12,4},{16,8},{20,12},{24,16},{28,20},{1,25},{... | collective-permute-start | bytes 983048 | tf_op jit(solution)/shard_map/ppermute | solution.py:29
  88.6 37.5 %collective-permute-start.18 = (bf16[4,80,2048]{2,1,0:T(8,128)(2,1)S(1)}, bf16[4,80,2048]{2,1,0:T(8,128)(2,1)S(1)}, u32[]{:S(2)}, u32[]{:S(2)}) collective-permute-start(bf16[4,80,2048]{2,1,0:T(8,128)(2,1)S(1)} %pad_maximum_fusion.2.refs_0_), channel_id=1, source_target_pairs={{0,2},{1,3},{2,0},{3,1},{4,6},{5,7},{6,4},{7,5},{8,10},{9,11},{10,... | collective-permute-start | bytes 3932168 | tf_op jit(solution)/shard_map/ppermute | solution.py:25
  90.4 36.8 %collective-permute-start.17 = (bf16[4,80,2048]{2,1,0:T(8,128)(2,1)S(1)}, bf16[4,80,2048]{2,1,0:T(8,128)(2,1)S(1)}, u32[]{:S(2)}, u32[]{:S(2)}) collective-permute-start(bf16[4,80,2048]{2,1,0:T(8,128)(2,1)S(1)} %pad_maximum_fusion.2.refs_0_), channel_id=1, source_target_pairs={{0,1},{1,0},{2,3},{3,2},{4,5},{5,4},{6,7},{7,6},{8,9},{9,8},{10,11... | collective-permute-start | bytes 3932168 | tf_op jit(solution)/shard_map/ppermute | solution.py:25
  100.1 25.9 %collective-permute-start.19 = (bf16[192,3072]{1,0:T(8,128)(2,1)}, bf16[192,3072]{1,0:T(8,128)(2,1)S(1)}, u32[]{:S(2)}, u32[]{:S(2)}) collective-permute-start(bf16[192,3072]{1,0:T(8,128)(2,1)} %shard_map.77), channel_id=1, source_target_pairs={{0,8},{4,12},{24,16},{28,20},{1,9},{5,13},{25,17},{29,21},{2,10},{... | collective-permute-start | bytes 3538952 | tf_op jit(solution)/shard_map/ppermute | solution.py:29
  131.5 21.6 %collective-permute-start.23 = (bf16[192,3072]{1,0:T(8,128)(2,1)S(1)}, bf16[192,3072]{1,0:T(8,128)(2,1)}, u32[]{:S(2)}, u32[]{:S(2)}) collective-permute-start(bf16[192,3072]{1,0:T(8,128)(2,1)S(1)} %add_convert_fusion.3), channel_id=1, source_target_pairs={{16,8},{20,12},{24,16},{28,20},{17,9},{21,13},{25,17},{29,21},{18,... | collective-permute-start | bytes 3538952 | tf_op jit(solution)/shard_map/ppermute | solution.py:29
  133.3 26.2 %collective-permute-start.22 = (bf16[192,3072]{1,0:T(8,128)(2,1)S(1)}, bf16[192,3072]{1,0:T(8,128)(2,1)}, u32[]{:S(2)}, u32[]{:S(2)}) collective-permute-start(bf16[192,3072]{1,0:T(8,128)(2,1)S(1)} %add_convert_fusion.3), channel_id=1, source_target_pairs={{0,8},{4,12},{8,16},{12,20},{1,9},{5,13},{9,17},{13,21},{2,10},{6,... | collective-permute-start | bytes 3538952 | tf_op jit(solution)/shard_map/ppermute | solution.py:29
  138.3 13.5 %collective-permute-start.21 = (bf16[4,80,1024]{2,1,0:T(8,128)(2,1)S(1)}, bf16[4,80,1024]{2,1,0:T(8,128)(2,1)S(1)}, u32[]{:S(2)}, u32[]{:S(2)}) collective-permute-start(bf16[4,80,1024]{2,1,0:T(8,128)(2,1)S(1)} %slice.142), channel_id=1, source_target_pairs={{0,2},{1,3},{2,0},{3,1},{4,6},{5,7},{6,4},{7,5},{8,10},{9,11},{10,... | collective-permute-start | bytes 1966088 | tf_op jit(solution)/shard_map/ppermute | solution.py:25
  140.0 13.1 %collective-permute-start.20 = (bf16[4,80,1024]{2,1,0:T(8,128)(2,1)S(1)}, bf16[4,80,1024]{2,1,0:T(8,128)(2,1)S(1)}, u32[]{:S(2)}, u32[]{:S(2)}) collective-permute-start(bf16[4,80,1024]{2,1,0:T(8,128)(2,1)S(1)} %slice.141), channel_id=1, source_target_pairs={{0,1},{1,0},{2,3},{3,2},{4,5},{5,4},{6,7},{7,6},{8,9},{9,8},{10,11... | collective-permute-start | bytes 1966088 | tf_op jit(solution)/shard_map/ppermute | solution.py:25
  162.9 27.6 %collective-permute-start.25 = (bf16[192,3072]{1,0:T(8,128)(2,1)S(1)}, bf16[192,3072]{1,0:T(8,128)(2,1)S(1)}, u32[]{:S(2)}, u32[]{:S(2)}) collective-permute-start(bf16[192,3072]{1,0:T(8,128)(2,1)S(1)} %get-tuple-element.79), channel_id=1, source_target_pairs={{8,0},{12,4},{16,8},{20,12},{24,16},{28,20},{9,1},{13,5},{17,9},{2... | collective-permute-start | bytes 3538952 | tf_op jit(solution)/shard_map/ppermute | solution.py:29
  164.3 27.4 %collective-permute-start.24 = (bf16[192,3072]{1,0:T(8,128)(2,1)S(1)}, bf16[192,3072]{1,0:T(8,128)(2,1)S(1)}, u32[]{:S(2)}, u32[]{:S(2)}) collective-permute-start(bf16[192,3072]{1,0:T(8,128)(2,1)S(1)} %get-tuple-element.80), channel_id=1, source_target_pairs={{0,8},{4,12},{8,16},{12,20},{16,24},{20,28},{1,9},{5,13},{9,17},{1... | collective-permute-start | bytes 3538952 | tf_op jit(solution)/shard_map/ppermute | solution.py:29
  195.0 20.9 %collective-permute-start.26 = (bf16[160,3072]{1,0:T(8,128)(2,1)S(1)}, bf16[160,3072]{1,0:T(8,128)(2,1)S(1)}, u32[]{:S(2)}, u32[]{:S(2)}) collective-permute-start(bf16[160,3072]{1,0:T(8,128)(2,1)S(1)} %get-tuple-element.85), channel_id=1, source_target_pairs={{0,8},{4,12},{24,16},{28,20},{1,9},{5,13},{25,17},{29,21},{2,10},{... | collective-permute-start | bytes 2949128 | tf_op jit(solution)/shard_map/ppermute | solution.py:29
  217.4 11.1 %collective-permute-start.29 = (bf16[160,3072]{1,0:T(8,128)(2,1)S(1)}, bf16[160,3072]{1,0:T(8,128)(2,1)S(1)}, u32[]{:S(2)}, u32[]{:S(2)}) collective-permute-start(bf16[160,3072]{1,0:T(8,128)(2,1)S(1)} %add_convert_fusion.7), channel_id=1, source_target_pairs={{16,8},{20,12},{24,16},{28,20},{17,9},{21,13},{25,17},{29,21},{18,... | collective-permute-start | bytes 2949128 | tf_op jit(solution)/shard_map/ppermute | solution.py:29
  218.1 27.2 %collective-permute-start.27 = (bf16[160,3072]{1,0:T(8,128)(2,1)S(1)}, bf16[160,3072]{1,0:T(8,128)(2,1)S(1)}, u32[]{:S(2)}, u32[]{:S(2)}) collective-permute-start(bf16[160,3072]{1,0:T(8,128)(2,1)S(1)} %add_convert_fusion.7), channel_id=1, source_target_pairs={{0,8},{4,12},{8,16},{12,20},{1,9},{5,13},{9,17},{13,21},{2,10},{6,... | collective-permute-start | bytes 2949128 | tf_op jit(solution)/shard_map/ppermute | solution.py:29
  223.2 43.2 %collective-permute-start.31 = (bf16[160,3072]{1,0:T(8,128)(2,1)S(1)}, bf16[160,3072]{1,0:T(8,128)(2,1)S(1)}, u32[]{:S(2)}, u32[]{:S(2)}) collective-permute-start(bf16[160,3072]{1,0:T(8,128)(2,1)S(1)} %get-tuple-element.86), channel_id=1, source_target_pairs={{0,8},{4,12},{24,16},{28,20},{1,9},{5,13},{25,17},{29,21},{2,10},{... | collective-permute-start | bytes 2949128 | tf_op jit(solution)/shard_map/ppermute | solution.py:29
  246.0 34.7 %collective-permute-start.28 = (bf16[160,3072]{1,0:T(8,128)(2,1)S(1)}, bf16[160,3072]{1,0:T(8,128)(2,1)S(1)}, u32[]{:S(2)}, u32[]{:S(2)}) collective-permute-start(bf16[160,3072]{1,0:T(8,128)(2,1)S(1)} %get-tuple-element.83), channel_id=1, source_target_pairs={{0,8},{4,12},{8,16},{12,20},{16,24},{20,28},{1,9},{5,13},{9,17},{1... | collective-permute-start | bytes 2949128 | tf_op jit(solution)/shard_map/ppermute | solution.py:29
  250.4 30.3 %collective-permute-start.30 = (bf16[160,3072]{1,0:T(8,128)(2,1)S(1)}, bf16[160,3072]{1,0:T(8,128)(2,1)S(1)}, u32[]{:S(2)}, u32[]{:S(2)}) collective-permute-start(bf16[160,3072]{1,0:T(8,128)(2,1)S(1)} %get-tuple-element.84), channel_id=1, source_target_pairs={{8,0},{12,4},{16,8},{20,12},{24,16},{28,20},{9,1},{13,5},{17,9},{2... | collective-permute-start | bytes 2949128 | tf_op jit(solution)/shard_map/ppermute | solution.py:29
  282.3 21.8 %collective-permute-start.32 = (bf16[160,3072]{1,0:T(8,128)(2,1)S(1)}, bf16[160,3072]{1,0:T(8,128)(2,1)S(1)}, u32[]{:S(2)}, u32[]{:S(2)}) collective-permute-start(bf16[160,3072]{1,0:T(8,128)(2,1)S(1)} %get-tuple-element.82), channel_id=1, source_target_pairs={{0,8},{4,12},{8,16},{12,20},{1,9},{5,13},{9,17},{13,21},{2,10},{6,... | collective-permute-start | bytes 2949128 | tf_op jit(solution)/shard_map/ppermute | solution.py:29
  304.7 21.9 %collective-permute-start.33 = (bf16[160,3072]{1,0:T(8,128)(2,1)S(1)}, bf16[160,3072]{1,0:T(8,128)(2,1)S(1)}, u32[]{:S(2)}, u32[]{:S(2)}) collective-permute-start(bf16[160,3072]{1,0:T(8,128)(2,1)S(1)} %get-tuple-element.87), channel_id=1, source_target_pairs={{0,8},{4,12},{8,16},{12,20},{16,24},{20,28},{1,9},{5,13},{9,17},{1... | collective-permute-start | bytes 2949128 | tf_op jit(solution)/shard_map/ppermute | solution.py:29
  309.7 16.9 %collective-permute-start.35 = (bf16[160,3072]{1,0:T(8,128)(2,1)S(1)}, bf16[160,3072]{1,0:T(8,128)(2,1)S(1)}, u32[]{:S(2)}, u32[]{:S(2)}) collective-permute-start(bf16[160,3072]{1,0:T(8,128)(2,1)S(1)} %get-tuple-element.88), channel_id=1, source_target_pairs={{8,0},{12,4},{16,8},{20,12},{24,16},{28,20},{9,1},{13,5},{17,9},{2... | collective-permute-start | bytes 2949128 | tf_op jit(solution)/shard_map/ppermute | solution.py:29
  313.5 14.0 %collective-permute-start.36 = (bf16[176,1024]{1,0:T(8,128)(2,1)S(1)}, bf16[176,1024]{1,0:T(8,128)(2,1)S(1)}, u32[]{:S(2)}, u32[]{:S(2)}) collective-permute-start(bf16[176,1024]{1,0:T(8,128)(2,1)S(1)} %pad_maximum_fusion.5), channel_id=1, source_target_pairs={{0,4},{4,8},{8,12},{12,16},{16,20},{20,24},{24,28},{1,5},{5,9},{9,... | collective-permute-start | bytes 1081352 | tf_op jit(solution)/shard_map/ppermute | solution.py:161
  (63 other events, 403.3 us)

commit v5 on v4

--- a/solution.py
+++ b/solution.py
@@ -11,7 +11,6 @@
 STAGES = (3, 5)
 ROUNDS = ((0, (1, 1), 2, 3, 4, 4), (1, (2, 3), 4, 5, 6, 7))
 CHAINS = (1, 2)
-LANES = 128
 RIM = 16
 
 
@@ -31,24 +30,13 @@
     )
 
 
-def dft_matrices(length, taps):
-    bins = length // 2 + 1
-    room = -(-bins // 8) * 8
-    k = np.arange(bins)[:, None]
+def dft_matrices(length):
+    half = length // 2
+    k = np.concatenate([np.arange(half), [half], np.arange(1, half)])[:, None]
     angle = 2.0 * np.pi * ((k * np.arange(length)[None, :]) % length) / length
-    weight = np.where((k == 0) | (k == length // 2), 1.0, 2.0) / length
-    analysis = np.zeros((2, room, length))
-    synthesis = np.zeros((2, room, length))
-    analysis[:, :bins] = np.stack([np.cos(angle), -np.sin(angle)])
-    synthesis[:, :bins] = np.stack([weight * np.cos(angle), -weight * np.sin(angle)])
-    return (
-        analysis.reshape(2 * room, length).astype(np.float32),
-        synthesis.reshape(2 * room, length)[:, taps:].T.astype(np.float32),
-    )
-
-
-def tile(*extents):
-    return 2 * LANES if all(e % (2 * LANES) == 0 for e in extents) else LANES
+    wave = np.where(np.arange(length)[:, None] <= half, np.cos(angle), -np.sin(angle))
+    weight = np.where((k == 0) | (k == half), 1.0, 2.0) / length
+    return wave.astype(np.float32), (weight * wave)[:, half:].T.astype(np.float32)
 
 
 def halves(value):
@@ -61,12 +49,11 @@
 
 
 def finish_kernel(
-    query, key, value, rims, short, long,
-    analysis_high, analysis_low, synthesis_high, synthesis_low, out, extended, signal,
+    query, key, value, rims, short, long, analysis, synthesis, out, extended, signal
 ):
     row_count = out.shape[0]
     taps = long.shape[0]
-    room = analysis_high.shape[0] // 2
+    length = 2 * taps
     reach = short.shape[0]
     for b, body in enumerate((query, key, value)):
         extended[b, :8] = rims[taps + RIM * b : taps + RIM * (b + 1)].astype(jnp.float32)[RIM - 8 :]
@@ -84,56 +71,60 @@
         gated = featurized(1, start, taps) * featurized(2, start, taps)
         signal[taps + start : 2 * taps + start] = gated.astype(jnp.bfloat16)
 
+    def both(product):
+        return product[: product.shape[0] // 2] + product[product.shape[0] // 2 :]
+
     long_high, long_low = halves(long[...])
-    tones = (
-        dot(analysis_high[:, :taps], long_high)
-        + dot(analysis_high[:, :taps], long_low)
-        + dot(analysis_low[:, :taps], long_high)
-    )
+    tones = both(dot(analysis[:, :taps], long_high)) + dot(analysis[:length, :taps], long_low)
+    first = lax.broadcasted_iota(jnp.int32, (taps, tones.shape[1]), 0) == 0
+    real_tones = tones[:taps]
+    cross_tones = jnp.where(first, 0.0, tones[taps:])
+    last_tones = jnp.where(first, tones[taps:], tones[:taps])
     for start in range(0, row_count, taps):
-        block = signal[start : start + 2 * taps]
-        spectrum = dot(analysis_high[...], block) + dot(analysis_low[...], block)
-        real = spectrum[:room] * tones[:room] - spectrum[room:] * tones[room:]
-        imag = spectrum[:room] * tones[room:] + spectrum[room:] * tones[:room]
-        high, low = halves(jnp.concatenate([real, imag], axis=0))
-        response = (
-            dot(synthesis_high[...], high)
-            + dot(synthesis_high[...], low)
-            + dot(synthesis_low[...], high)
+        spectrum = both(dot(analysis[...], signal[start : start + length]))
+        real, imag = spectrum[:taps], spectrum[taps:]
+        high, low = halves(
+            jnp.concatenate(
+                [
+                    real * real_tones - imag * cross_tones,
+                    real * cross_tones + imag * last_tones,
+                ],
+                axis=0,
+            )
         )
+        response = both(dot(synthesis[...], high)) + dot(synthesis[:taps], low)
         out[start : start + taps] = (featurized(0, start, taps) * response).astype(out.dtype)
 
 
 def finish(projected, rims, short_filter, long_filter):
     row_count = projected.shape[0]
     taps, channels = long_filter.shape
-    width = tile(channels)
-    count = channels // width
-    analysis, synthesis = (jnp.asarray(m) for m in dft_matrices(2 * taps, taps))
-    constants = (*halves(analysis), *halves(synthesis))
+    constants = [
+        jnp.concatenate(halves(jnp.asarray(matrix)), axis=0) for matrix in dft_matrices(2 * taps)
+    ]
 
     def branch(b):
-        return pl.BlockSpec((row_count, width), lambda i: (0, b * count + i))
+        return pl.BlockSpec((row_count, channels), lambda i: (0, b))
 
     operands = [*[projected] * 3, rims, short_filter, long_filter, *constants]
     specs = (
         [branch(b) for b in range(3)]
         + [
-            pl.BlockSpec((rims.shape[0], width), lambda i: (0, i)),
-            pl.BlockSpec((short_filter.shape[0], 3, width), lambda i: (0, 0, i)),
-            pl.BlockSpec((taps, width), lambda i: (0, i)),
+            pl.BlockSpec(rims.shape, lambda i: (0, 0)),
+            pl.BlockSpec(short_filter.shape, lambda i: (0, 0, 0)),
+            pl.BlockSpec(long_filter.shape, lambda i: (0, 0)),
         ]
         + [pl.BlockSpec(m.shape, lambda i: (0, 0)) for m in constants]
     )
     return pl.pallas_call(
         finish_kernel,
         out_shape=jax.ShapeDtypeStruct((row_count, channels), jnp.bfloat16),
-        grid=(count,),
+        grid=(1,),
         in_specs=specs,
-        out_specs=pl.BlockSpec((row_count, width), lambda i: (0, i)),
+        out_specs=pl.BlockSpec((row_count, channels), lambda i: (0, 0)),
         scratch_shapes=[
-            pltpu.VMEM((3, 8 + row_count, width), jnp.float32),
-            pltpu.VMEM((taps + row_count, width), jnp.bfloat16),
+            pltpu.VMEM((3, 8 + row_count, channels), jnp.float32),
+            pltpu.VMEM((taps + row_count, channels), jnp.bfloat16),
         ],
         compiler_params=pltpu.CompilerParams(vmem_limit_bytes=32 * 1024 * 1024),
         cost_estimate=pl.CostEstimate(
@@ -183,55 +174,70 @@
 def spread_far(near, columns):
     if columns != 4:
         return []
-    half = near[0].shape[-1] // 2
-    return [swap(near[1][..., :half], columns, 1), swap(near[0][..., half:], columns, 2)]
-
-
-def spread_all(value, near, far):
-    return [value, *near] + ([jnp.concatenate(far, axis=-1)] if far else [])
-
-
-def partial_kernel(place, *refs):
+    half = near[0].shape[0] // 2
+    return [swap(near[1][:half], columns, 1), swap(near[0][half:], columns, 2)]
+
+
+def partial_kernel(parts, place, *refs):
     *lefts, own, other, out, joined = refs
-    planes, columns, share, depth = joined.shape
-
-    @pl.when(pl.program_id(0) == 0)
+    size, columns, share, depth = joined.shape
+
+    @pl.when((pl.program_id(0) == 0) & (pl.program_id(1) == 0))
     def _():
-        for t, left in enumerate(lefts):
-            joined[:, place[0] ^ t] = left[...]
-
-    rows = joined[...].reshape(planes * columns * share, depth)
+        for (t, begin, end), left in zip(parts, lefts):
+            joined[begin:end, place[0] ^ t] = left[...]
+
+    rows = joined[...].reshape(size * columns * share, depth)
     half = depth // 2
     total = dot(rows[:, :half], own[0]) + dot(rows[:, half:], other[0])
     out[...] = total.astype(out.dtype)
 
 
-def partial_sums(place, lefts, own, other, size, at):
-    _, share, depth = lefts[0].shape
-    columns = len(lefts)
+def partial_sums(place, lefts, far, own, other, size, at):
+    planes, share, depth = lefts[0].shape
+    columns = len(lefts) + (1 if far else 0)
     channels = own.shape[2]
     rows = size * columns * share
-    weights = pl.BlockSpec((1, own.shape[1], channels), lambda b, _: (b, 0, 0))
-    left = pl.BlockSpec(
-        (size, share, depth), lambda b, place: (place[1] if at is None else at, 0, 0)
-    )
+    width = channels
+    count = channels // width
+    weights = pl.BlockSpec((1, own.shape[1], width), lambda b, n, _: (b, 0, n))
+
+    def block(shape, before=0):
+        return pl.BlockSpec(
+            shape, lambda b, n, place: (place[1] if at is None else at - before, 0, 0)
+        )
+
+    operands = list(lefts)
+    specs = [block((size, share, depth)) for _ in lefts]
+    parts = [(t, 0, size) for t in range(len(lefts))]
+    if far and size == planes:
+        operands += far
+        specs += [pl.BlockSpec(part.shape, lambda b, n, _: (0, 0, 0)) for part in far]
+        parts += [(len(lefts), 0, planes // 2), (len(lefts), planes // 2, planes)]
+    elif far:
+        second = at is not None and at * size >= planes // 2
+        operands.append(far[second])
+        specs.append(block((size, share, depth), planes // 2 // size if second else 0))
+        parts.append((len(lefts), 0, size))
     return pl.pallas_call(
-        partial_kernel,
+        lambda *refs: partial_kernel(parts, *refs),
         out_shape=jax.ShapeDtypeStruct((rows, 3 * channels), jnp.bfloat16),
         grid_spec=pltpu.PrefetchScalarGridSpec(
             num_scalar_prefetch=1,
-            grid=(3,),
-            in_specs=[left] * columns + [weights, weights],
-            out_specs=pl.BlockSpec((rows, channels), lambda b, _: (0, b)),
+            grid=(3, count),
+            in_specs=specs + [weights, weights],
+            out_specs=pl.BlockSpec((rows, width), lambda b, n, _: (0, b * count + n)),
             scratch_shapes=[pltpu.VMEM((size, columns, share, depth), jnp.bfloat16)],
         ),
-        compiler_params=pltpu.CompilerParams(vmem_limit_bytes=56 * 1024 * 1024),
+        compiler_params=pltpu.CompilerParams(
+            vmem_limit_bytes=(56 if size == 1 else 36) * 1024 * 1024
+        ),
         cost_estimate=pl.CostEstimate(
             flops=2 * rows * depth * 3 * channels,
             bytes_accessed=2 * rows * depth + 6 * depth * channels + 6 * rows * channels,
             transcendentals=0,
         ),
-    )(place, *lefts, own, other).reshape(size, columns * share, 3 * channels)
+    )(place, *operands, own, other).reshape(size, columns * share, 3 * channels)
 
 
 def on_device(tokens, gain, in_weight, short_filter, long_filter):
@@ -307,7 +313,7 @@
     normed, rows_of, own, lefts = {}, {}, {}, {}
 
     def product(stage, size, at):
-        return partial_sums(place, lefts[stage], weight, other_weight, size, at)
+        return partial_sums(place, *lefts[stage], weight, other_weight, size, at)
 
     def split(stage, blocks):
         terms = [block for part in blocks for block in part]
@@ -339,7 +345,7 @@
                 fresh[f"near{stage}"] = live[f"near{stage}"]
                 fresh[f"far{stage}"] = spread_far(live[f"near{stage}"], columns)
             if now == ready:
-                lefts[stage] = spread_all(own[stage], live[f"near{stage}"], live[f"far{stage}"])
+                lefts[stage] = [own[stage], *live[f"near{stage}"]], live[f"far{stage}"]
                 if now == first:
                     lead = product(stage, 1, None)[0]
                     split(stage, [product(stage, planes, 0)])

time: 337 us -> 332 us (0.985)
  local copies, waits for them, and re-layouts: 18.6 us -> 27.8 us
  Pallas kernels: 59 us -> 51.3 us
  waiting for transfers between devices: 158 us -> 152 us
    unnamed x114 -> x122, local copies, waits for them, and re-layouts: 12.6 us -> 21.8 us
    pallas_call x4, Pallas kernels: 51.6 us -> 45.3 us  [partial_sums(): pl.pallas_call(lambda *refs: partial_kernel(parts, *refs), out_shape=jax....]
    ppermute x21, waiting for transfers between devices: 138 us -> 132 us  [plane_shift(): lax.ppermute(value, 'ctx', [(a * CORES + c, b * CORES + c) for a, b in ed...]
  transfers between devices with their start and end apart: 37 -> 37, of which waited for: 20 -> 21; matrix products, arithmetic and copies ran while one was open for 3% -> 3% of each run, Pallas kernels for 15% -> 14%
where the time goes in v5:
time: 332 us; the launch traced here: 331 us
  waiting for transfers between devices  152 us (46%)
  starting transfers between devices  77.2 us (23%)
  Pallas kernels  51.3 us (15%)
  local copies, waits for them, and re-layouts  27.8 us (8%)
  other arithmetic  22.3 us (7%)
    ppermute x21, waiting for transfers between devices, plane_shift(): lax.ppermute(value, 'ctx', [(a * CORES + c, b * CORES + c) for a, b in ed...  132 us
    ppermute x21, starting transfers between devices, plane_shift(): lax.ppermute(value, 'ctx', [(a * CORES + c, b * CORES + c) for a, b in ed...  58.7 us
    pallas_call x4, Pallas kernels, partial_sums(): pl.pallas_call(lambda *refs: partial_kernel(parts, *refs), out_shape=jax....  45.3 us
    unnamed x122, local copies, waits for them, and re-layouts  21.8 us
    ppermute x14, waiting for transfers between devices, swap(): return lax.ppermute(value, 'fsdp', [(j, j ^ bits) for j in range(count)])  19.8 us
    ppermute x14, starting transfers between devices, swap(): return lax.ppermute(value, 'fsdp', [(j, j ^ bits) for j in range(count)])  16.5 us
    convert_element_type x5, other arithmetic, onward(): (term.astype(jnp.float32) + came.astype(jnp.float32)).astype(jnp.bfloat16)  7.24 us
  transfers between devices with their start and end apart: 37, of which 21 were waited for; matrix products, arithmetic and copies ran while one was open for 3% of the time, Pallas kernels for 14%

profile of v5, /device:TPU:0, one launch (start us, length us, event | category | flops | bytes accessed | tf_op | source)
XLA Modules:
  0.0 331.3 jit_solution(1380863571655702000)
XLA Ops:
  1.9 3.9 %collective-permute-start.2 = (bf16[48,2048]{1,0:T(8,128)(2,1)S(1)}, bf16[48,2048]{1,0:T(8,128)(2,1)S(1)}, u32[]{:S(2)}, u32[]{:S(2)}) collective-permute-start(bf16[48,2048]{1,0:T(8,128)(2,1)S(1)} %get-tuple-element.110), channel_id=1, source_target_pairs={{0,3},{1,2},{2,1},{3,0},{4,7},{5,6},{6,5},{7,4},{8,11},{9,10},{10,... | collective-permute-start | bytes 589832 | tf_op jit(solution)/shard_map/ppermute | solution.py:24
  7.6 4.0 %collective-permute-done.2.refs_7_ = bf16[48,2048]{1,0:T(8,128)(2,1)S(1)} collective-permute-done((bf16[48,2048]{1,0:T(8,128)(2,1)S(1)}, bf16[48,2048]{1,0:T(8,128)(2,1)S(1)}, u32[]{:S(2)}, u32[]{:S(2)}) %collective-permute-start.2) | collective-permute-done | bytes 196640 | tf_op jit(solution)/shard_map/ppermute | solution.py:24
  11.6 3.3 %collective-permute-done.1.refs_6_ = bf16[48,2048]{1,0:T(8,128)(2,1)S(1)} collective-permute-done((bf16[48,2048]{1,0:T(8,128)(2,1)S(1)}, bf16[48,2048]{1,0:T(8,128)(2,1)S(1)}, u32[]{:S(2)}, u32[]{:S(2)}) %collective-permute-start.1) | collective-permute-done | bytes 196640 | tf_op jit(solution)/shard_map/ppermute | solution.py:24
  27.3 8.9 %collective-permute-done.6.refs_2_ = bf16[48,2048]{1,0:T(8,128)(2,1)S(1)} collective-permute-done((bf16[48,2048]{1,0:T(8,128)(2,1)S(1)}, bf16[48,2048]{1,0:T(8,128)(2,1)S(1)}, u32[]{:S(2)}, u32[]{:S(2)}) %collective-permute-start.6) | collective-permute-done | bytes 196640 | tf_op jit(solution)/shard_map/ppermute | solution.py:28
  36.2 5.7 %collective-permute-done.4.refs_0_ = bf16[48,2048]{1,0:T(8,128)(2,1)S(1)} collective-permute-done((bf16[48,2048]{1,0:T(8,128)(2,1)S(1)}, bf16[48,2048]{1,0:T(8,128)(2,1)S(1)}, u32[]{:S(2)}, u32[]{:S(2)}) %collective-permute-start.4) | collective-permute-done | bytes 196640 | tf_op jit(solution)/shard_map/ppermute | solution.py:28
  48.8 14.4 %collective-permute-done.12.refs_2_ = bf16[80,2048]{1,0:T(8,128)(2,1)S(1)} collective-permute-done((bf16[80,2048]{1,0:T(8,128)(2,1)S(1)}, bf16[80,2048]{1,0:T(8,128)(2,1)S(1)}, u32[]{:S(2)}, u32[]{:S(2)}) %collective-permute-start.12) | collective-permute-done | bytes 327712 | tf_op jit(solution)/shard_map/ppermute | solution.py:28
  69.3 3.8 %collective-permute-start.15 = (bf16[80,2048]{1,0:T(8,128)(2,1)}, bf16[80,2048]{1,0:T(8,128)(2,1)S(1)}, u32[]{:S(2)}, u32[]{:S(2)}) collective-permute-start(bf16[80,2048]{1,0:T(8,128)(2,1)} %get-tuple-element.91), channel_id=1, source_target_pairs={{0,24},{4,28},{8,0},{12,4},{16,8},{20,12},{24,16},{28,20},{1,25},{... | collective-permute-start | bytes 983048 | tf_op jit(solution)/shard_map/ppermute | solution.py:28
  73.8 8.2 %collective-permute-done.16.refs_5_ = bf16[80,2048]{1,0:T(8,128)(2,1)S(1)} collective-permute-done((bf16[80,2048]{1,0:T(8,128)(2,1)}, bf16[80,2048]{1,0:T(8,128)(2,1)S(1)}, u32[]{:S(2)}, u32[]{:S(2)}) %collective-permute-start.16) | collective-permute-done | bytes 327712 | tf_op jit(solution)/shard_map/ppermute | solution.py:28
  82.0 3.6 %collective-permute-done.15.refs_4_ = bf16[80,2048]{1,0:T(8,128)(2,1)S(1)} collective-permute-done((bf16[80,2048]{1,0:T(8,128)(2,1)}, bf16[80,2048]{1,0:T(8,128)(2,1)S(1)}, u32[]{:S(2)}, u32[]{:S(2)}) %collective-permute-start.15) | collective-permute-done | bytes 327712 | tf_op jit(solution)/shard_map/ppermute | solution.py:28
  90.6 9.7 %shard_map.77 = bf16[192,3072]{1,0:T(8,128)(2,1)} custom-call(s32[2]{0:T(128)} %pad_add_fusion.refs_0_, bf16[4,48,2048]{2,1,0:T(8,128)(2,1)} %copy-done.16, bf16[4,48,2048]{2,1,0:T(8,128)(2,1)} %get-tuple-element.62.refs_2_, bf16[4,48,2048]{2,1,0:T(8,128)(2,1)} %get-tuple-element.63.refs_3_, bf16[2,48,2048]{2,1,0:T(8,128)(2,1)} %get-tuple-element.64.refs_4_, ...), custom_call_target="tpu_custom_call" | custom-call | flops 2415919104 | bytes 14548992 | tf_op jit(solution)/shard_map/pallas_call | solution.py:222
  105.5 12.9 %shard_map.79 = bf16[768,3072]{1,0:T(8,128)(2,1)S(1)} custom-call(s32[2]{0:T(128)S(1)} %copy-done.33, bf16[4,48,2048]{2,1,0:T(8,128)(2,1)S(1)} %copy-done.17, bf16[4,48,2048]{2,1,0:T(8,128)(2,1)S(1)} %copy-done.5, bf16[4,48,2048]{2,1,0:T(8,128)(2,1)S(1)} %copy-done.3, bf16[2,48,2048]{2,1,0:T(8,128)(2,1)S(1)} %copy-done.19, ...), custom_call_target="tpu_custom_call" | custom-call | flops 9663676416 | bytes 20447232 | tf_op jit(solution)/shard_map/pallas_call | solution.py:222
  120.5 5.7 %collective-permute-done.19.refs_2_ = bf16[192,3072]{1,0:T(8,128)(2,1)S(1)} collective-permute-done((bf16[192,3072]{1,0:T(8,128)(2,1)}, bf16[192,3072]{1,0:T(8,128)(2,1)S(1)}, u32[]{:S(2)}, u32[]{:S(2)}) %collective-permute-start.19) | collective-permute-done | bytes 1179680 | tf_op jit(solution)/shard_map/ppermute | solution.py:28
  132.3 5.9 %collective-permute-start.22 = (bf16[192,3072]{1,0:T(8,128)(2,1)S(1)}, bf16[192,3072]{1,0:T(8,128)(2,1)}, u32[]{:S(2)}, u32[]{:S(2)}) collective-permute-start(bf16[192,3072]{1,0:T(8,128)(2,1)S(1)} %add_convert_fusion.3), channel_id=1, source_target_pairs={{0,8},{4,12},{8,16},{12,20},{1,9},{5,13},{9,17},{13,21},{2,10},{6,... | collective-permute-start | bytes 3538952 | tf_op jit(solution)/shard_map/ppermute | solution.py:28
  140.8 11.0 %collective-permute-done.21.refs_1_ = bf16[2,80,2048]{2,1,0:T(8,128)(2,1)S(1)} collective-permute-done((bf16[2,80,2048]{2,1,0:T(8,128)(2,1)S(1)}, bf16[2,80,2048]{2,1,0:T(8,128)(2,1)S(1)}, u32[]{:S(2)}, u32[]{:S(2)}) %collective-permute-start.21) | collective-permute-done | bytes 655392 | tf_op jit(solution)/shard_map/ppermute | solution.py:24
  153.0 6.6 %collective-permute-done.22.refs_4_ = bf16[192,3072]{1,0:T(8,128)(2,1)} collective-permute-done((bf16[192,3072]{1,0:T(8,128)(2,1)S(1)}, bf16[192,3072]{1,0:T(8,128)(2,1)}, u32[]{:S(2)}, u32[]{:S(2)}) %collective-permute-start.22) | collective-permute-done | bytes 1179680 | tf_op jit(solution)/shard_map/ppermute | solution.py:28
  159.7 3.4 %add_convert_fusion.1 = (bf16[192,3072]{1,0:T(8,128)(2,1)S(1)}, bf16[192,3072]{1,0:T(8,128)(2,1)S(1)}) fusion(bf16[192,3072]{1,0:T(8,128)(2,1)} %get-tuple-element.75, bf16[768,3072]{1,0:T(8,128)(2,1)} %copy-done.15, bf16[192,3072]{1,0:T(8,128)(2,1)} %get-tuple-element.74), kind=kLoop, calls=%fused_computation.7 | loop fusion | flops 4718592 | bytes 7077888 | tf_op jit(solution)/shard_map/convert_element_type | solution.py:296
  164.4 6.2 %collective-permute-start.24 = (bf16[192,3072]{1,0:T(8,128)(2,1)S(1)}, bf16[192,3072]{1,0:T(8,128)(2,1)}, u32[]{:S(2)}, u32[]{:S(2)}) collective-permute-start(bf16[192,3072]{1,0:T(8,128)(2,1)S(1)} %get-tuple-element.80), channel_id=1, source_target_pairs={{0,8},{4,12},{8,16},{12,20},{16,24},{20,28},{1,9},{5,13},{9,17},{1... | collective-permute-start | bytes 3538952 | tf_op jit(solution)/shard_map/ppermute | solution.py:28
  173.3 11.2 %shard_map.82 = bf16[640,3072]{1,0:T(8,128)(2,1)S(1)} custom-call(s32[2]{0:T(128)S(1)} %copy-done.33, bf16[4,80,2048]{2,1,0:T(8,128)(2,1)S(1)} %copy-done.21, bf16[4,80,2048]{2,1,0:T(8,128)(2,1)S(1)} %copy-done.11, bf16[4,80,2048]{2,1,0:T(8,128)(2,1)S(1)} %copy-done.8, bf16[2,80,2048]{2,1,0:T(8,128)(2,1)S(1)} %copy-done.26, ...), custom_call_target="tpu_custom_call" | custom-call | flops 8053063680 | bytes 19136512 | tf_op jit(solution)/shard_map/pallas_call | solution.py:222
  186.4 3.5 %collective-permute-done.25.refs_2_ = bf16[192,3072]{1,0:T(8,128)(2,1)} collective-permute-done((bf16[192,3072]{1,0:T(8,128)(2,1)S(1)}, bf16[192,3072]{1,0:T(8,128)(2,1)}, u32[]{:S(2)}, u32[]{:S(2)}) %collective-permute-start.25) | collective-permute-done | bytes 1179680 | tf_op jit(solution)/shard_map/ppermute | solution.py:28
  193.4 4.6 %collective-permute-start.26 = (bf16[160,3072]{1,0:T(8,128)(2,1)S(1)}, bf16[160,3072]{1,0:T(8,128)(2,1)S(1)}, u32[]{:S(2)}, u32[]{:S(2)}) collective-permute-start(bf16[160,3072]{1,0:T(8,128)(2,1)S(1)} %get-tuple-element.85), channel_id=1, source_target_pairs={{0,8},{4,12},{24,16},{28,20},{1,9},{5,13},{25,17},{29,21},{2,10},{... | collective-permute-start | bytes 2949128 | tf_op jit(solution)/shard_map/ppermute | solution.py:28
  200.8 11.5 %shard_map.81 = bf16[640,3072]{1,0:T(8,128)(2,1)S(1)} custom-call(s32[2]{0:T(128)S(1)} %copy-done.33, bf16[4,80,2048]{2,1,0:T(8,128)(2,1)S(1)} %copy-done.22, bf16[4,80,2048]{2,1,0:T(8,128)(2,1)S(1)} %copy-done.11, bf16[4,80,2048]{2,1,0:T(8,128)(2,1)S(1)} %copy-done.8, bf16[2,80,2048]{2,1,0:T(8,128)(2,1)S(1)} %copy-done.24, ...), custom_call_target="tpu_custom_call" | custom-call | flops 8053063680 | bytes 19136512 | tf_op jit(solution)/shard_map/pallas_call | solution.py:222
  215.4 5.0 %collective-permute-start.27 = (bf16[160,3072]{1,0:T(8,128)(2,1)S(1)}, bf16[160,3072]{1,0:T(8,128)(2,1)S(1)}, u32[]{:S(2)}, u32[]{:S(2)}) collective-permute-start(bf16[160,3072]{1,0:T(8,128)(2,1)S(1)} %add_convert_fusion.7), channel_id=1, source_target_pairs={{0,8},{4,12},{8,16},{12,20},{1,9},{5,13},{9,17},{13,21},{2,10},{6,... | collective-permute-start | bytes 2949128 | tf_op jit(solution)/shard_map/ppermute | solution.py:28
  220.4 5.6 %collective-permute-start.31 = (bf16[160,3072]{1,0:T(8,128)(2,1)S(1)}, bf16[160,3072]{1,0:T(8,128)(2,1)S(1)}, u32[]{:S(2)}, u32[]{:S(2)}) collective-permute-start(bf16[160,3072]{1,0:T(8,128)(2,1)S(1)} %get-tuple-element.86), channel_id=1, source_target_pairs={{0,8},{4,12},{24,16},{28,20},{1,9},{5,13},{25,17},{29,21},{2,10},{... | collective-permute-start | bytes 2949128 | tf_op jit(solution)/shard_map/ppermute | solution.py:28
  226.0 16.5 %collective-permute-done.27 = bf16[160,3072]{1,0:T(8,128)(2,1)S(1)} collective-permute-done((bf16[160,3072]{1,0:T(8,128)(2,1)S(1)}, bf16[160,3072]{1,0:T(8,128)(2,1)S(1)}, u32[]{:S(2)}, u32[]{:S(2)}) %collective-permute-start.27) | collective-permute-done | bytes 983072 | tf_op jit(solution)/shard_map/ppermute | solution.py:28
  243.2 4.4 %collective-permute-start.28 = (bf16[160,3072]{1,0:T(8,128)(2,1)S(1)}, bf16[160,3072]{1,0:T(8,128)(2,1)S(1)}, u32[]{:S(2)}, u32[]{:S(2)}) collective-permute-start(bf16[160,3072]{1,0:T(8,128)(2,1)S(1)} %get-tuple-element.83), channel_id=1, source_target_pairs={{0,8},{4,12},{8,16},{12,20},{16,24},{20,28},{1,9},{5,13},{9,17},{1... | collective-permute-start | bytes 2949128 | tf_op jit(solution)/shard_map/ppermute | solution.py:28
  249.1 14.5 %collective-permute-done.31 = bf16[160,3072]{1,0:T(8,128)(2,1)S(1)} collective-permute-done((bf16[160,3072]{1,0:T(8,128)(2,1)S(1)}, bf16[160,3072]{1,0:T(8,128)(2,1)S(1)}, u32[]{:S(2)}, u32[]{:S(2)}) %collective-permute-start.31) | collective-permute-done | bytes 983072 | tf_op jit(solution)/shard_map/ppermute | solution.py:28
  263.6 14.3 %collective-permute-done.28 = bf16[160,3072]{1,0:T(8,128)(2,1)S(1)} collective-permute-done((bf16[160,3072]{1,0:T(8,128)(2,1)S(1)}, bf16[160,3072]{1,0:T(8,128)(2,1)S(1)}, u32[]{:S(2)}, u32[]{:S(2)}) %collective-permute-start.28) | collective-permute-done | bytes 983072 | tf_op jit(solution)/shard_map/ppermute | solution.py:28
  279.5 5.0 %collective-permute-start.32 = (bf16[160,3072]{1,0:T(8,128)(2,1)S(1)}, bf16[160,3072]{1,0:T(8,128)(2,1)S(1)}, u32[]{:S(2)}, u32[]{:S(2)}) collective-permute-start(bf16[160,3072]{1,0:T(8,128)(2,1)S(1)} %get-tuple-element.82), channel_id=1, source_target_pairs={{0,8},{4,12},{8,16},{12,20},{1,9},{5,13},{9,17},{13,21},{2,10},{6,... | collective-permute-start | bytes 2949128 | tf_op jit(solution)/shard_map/ppermute | solution.py:28
  284.6 16.7 %collective-permute-done.32 = bf16[160,3072]{1,0:T(8,128)(2,1)S(1)} collective-permute-done((bf16[160,3072]{1,0:T(8,128)(2,1)S(1)}, bf16[160,3072]{1,0:T(8,128)(2,1)S(1)}, u32[]{:S(2)}, u32[]{:S(2)}) %collective-permute-start.32) | collective-permute-done | bytes 983072 | tf_op jit(solution)/shard_map/ppermute | solution.py:28
  302.0 5.3 %collective-permute-start.33 = (bf16[160,3072]{1,0:T(8,128)(2,1)S(1)}, bf16[160,3072]{1,0:T(8,128)(2,1)S(1)}, u32[]{:S(2)}, u32[]{:S(2)}) collective-permute-start(bf16[160,3072]{1,0:T(8,128)(2,1)S(1)} %get-tuple-element.87), channel_id=1, source_target_pairs={{0,8},{4,12},{8,16},{12,20},{16,24},{20,28},{1,9},{5,13},{9,17},{1... | collective-permute-start | bytes 2949128 | tf_op jit(solution)/shard_map/ppermute | solution.py:28
  313.2 9.6 %collective-permute-done.33 = bf16[160,3072]{1,0:T(8,128)(2,1)S(1)} collective-permute-done((bf16[160,3072]{1,0:T(8,128)(2,1)S(1)}, bf16[160,3072]{1,0:T(8,128)(2,1)S(1)}, u32[]{:S(2)}, u32[]{:S(2)}) %collective-permute-start.33) | collective-permute-done | bytes 983072 | tf_op jit(solution)/shard_map/ppermute | solution.py:28
  325.3 6.0 %shard_map.84 = bf16[512,1024]{1,0:T(8,128)(2,1)} custom-call(bf16[512,3072]{1,0:T(8,128)(2,1)S(1)} %pad_maximum_fusion.query.key.value, bf16[512,3072]{1,0:T(8,128)(2,1)S(1)} %pad_maximum_fusion.query.key.value, bf16[512,3072]{1,0:T(8,128)(2,1)S(1)} %pad_maximum_fusion.query.key.value, bf16[176,1024]{1,0:T(8,128)(2,1)S(1)} %collective-permute-done.36.rims, ...), custom_call_target="tpu_custom_call" | custom-call | flops 2621440000 | bytes 5242880 | tf_op jit(solution)/shard_map/pallas_call | solution.py:119
  (219 shorter events, 79.6 us)
Async XLA Ops:
  0.0 15.2 %collective-permute-start.3 = (bf16[3,1024,1024]{2,1,0:T(8,128)(2,1)}, bf16[3,1024,1024]{2,1,0:T(8,128)(2,1)}, u32[]{:S(2)}, u32[]{:S(2)}) collective-permute-start(bf16[3,1024,1024]{2,1,0:T(8,128)(2,1)} %bitcast.71), channel_id=1, source_target_pairs={{0,4},{4,0},{8,12},{12,8},{16,20},{20,16},{24,28},{28,24},{1,5},{5... | collective-permute-start | bytes 18874376 | tf_op jit(solution)/shard_map/ppermute | solution.py:262
  19.6 16.6 %collective-permute-start.6 = (bf16[48,2048]{1,0:T(8,128)(2,1)S(1)}, bf16[48,2048]{1,0:T(8,128)(2,1)S(1)}, u32[]{:S(2)}, u32[]{:S(2)}) collective-permute-start(bf16[48,2048]{1,0:T(8,128)(2,1)S(1)} %get-tuple-element.105), channel_id=1, source_target_pairs={{0,16},{4,20},{8,24},{12,28},{16,0},{20,4},{24,8},{28,12},{1,17},{... | collective-permute-start | bytes 589832 | tf_op jit(solution)/shard_map/ppermute | solution.py:28
  22.2 19.6 %collective-permute-start.7 = (bf16[80,2048]{1,0:T(8,128)(2,1)S(1)}, bf16[80,2048]{1,0:T(8,128)(2,1)S(1)}, u32[]{:S(2)}, u32[]{:S(2)}) collective-permute-start(bf16[80,2048]{1,0:T(8,128)(2,1)S(1)} %copy-done.52), channel_id=1, source_target_pairs={{0,1},{1,0},{2,3},{3,2},{4,5},{5,4},{6,7},{7,6},{8,9},{9,8},{10,11... | collective-permute-start | bytes 983048 | tf_op jit(solution)/shard_map/ppermute | solution.py:24
  23.7 18.1 %collective-permute-start.8 = (bf16[80,2048]{1,0:T(8,128)(2,1)S(1)}, bf16[80,2048]{1,0:T(8,128)(2,1)S(1)}, u32[]{:S(2)}, u32[]{:S(2)}) collective-permute-start(bf16[80,2048]{1,0:T(8,128)(2,1)S(1)} %copy-done.51), channel_id=1, source_target_pairs={{0,2},{1,3},{2,0},{3,1},{4,6},{5,7},{6,4},{7,5},{8,10},{9,11},{10,... | collective-permute-start | bytes 983048 | tf_op jit(solution)/shard_map/ppermute | solution.py:24
  24.5 17.4 %collective-permute-start.9 = (bf16[80,2048]{1,0:T(8,128)(2,1)S(1)}, bf16[80,2048]{1,0:T(8,128)(2,1)S(1)}, u32[]{:S(2)}, u32[]{:S(2)}) collective-permute-start(bf16[80,2048]{1,0:T(8,128)(2,1)S(1)} %copy-done.50), channel_id=1, source_target_pairs={{0,3},{1,2},{2,1},{3,0},{4,7},{5,6},{6,5},{7,4},{8,11},{9,10},{10,... | collective-permute-start | bytes 983048 | tf_op jit(solution)/shard_map/ppermute | solution.py:24
  25.7 10.5 %collective-permute-start.5 = (bf16[48,2048]{1,0:T(8,128)(2,1)S(1)}, bf16[48,2048]{1,0:T(8,128)(2,1)S(1)}, u32[]{:S(2)}, u32[]{:S(2)}) collective-permute-start(bf16[48,2048]{1,0:T(8,128)(2,1)S(1)} %get-tuple-element.106), channel_id=1, source_target_pairs={{0,8},{4,12},{8,16},{12,20},{16,24},{20,28},{24,0},{28,4},{1,9},{5... | collective-permute-start | bytes 589832 | tf_op jit(solution)/shard_map/ppermute | solution.py:28
  44.2 18.9 %collective-permute-start.11 = (bf16[4,48,2048]{2,1,0:T(8,128)(2,1)S(1)}, bf16[4,48,2048]{2,1,0:T(8,128)(2,1)S(1)}, u32[]{:S(2)}, u32[]{:S(2)}) collective-permute-start(bf16[4,48,2048]{2,1,0:T(8,128)(2,1)S(1)} %pad_maximum_fusion.4.refs_1_), channel_id=1, source_target_pairs={{0,2},{1,3},{2,0},{3,1},{4,6},{5,7},{6,4},{7,5},{8,10},{9,11},{10,... | collective-permute-start | bytes 2359304 | tf_op jit(solution)/shard_map/ppermute | solution.py:24
  45.8 17.4 %collective-permute-start.10 = (bf16[4,48,2048]{2,1,0:T(8,128)(2,1)S(1)}, bf16[4,48,2048]{2,1,0:T(8,128)(2,1)S(1)}, u32[]{:S(2)}, u32[]{:S(2)}) collective-permute-start(bf16[4,48,2048]{2,1,0:T(8,128)(2,1)S(1)} %pad_maximum_fusion.4.refs_1_), channel_id=1, source_target_pairs={{0,1},{1,0},{2,3},{3,2},{4,5},{5,4},{6,7},{7,6},{8,9},{9,8},{10,11... | collective-permute-start | bytes 2359304 | tf_op jit(solution)/shard_map/ppermute | solution.py:24
  48.8 14.4 %collective-permute-start.12 = (bf16[80,2048]{1,0:T(8,128)(2,1)S(1)}, bf16[80,2048]{1,0:T(8,128)(2,1)S(1)}, u32[]{:S(2)}, u32[]{:S(2)}) collective-permute-start(bf16[80,2048]{1,0:T(8,128)(2,1)S(1)} %get-tuple-element.92), channel_id=1, source_target_pairs={{0,16},{4,20},{8,24},{12,28},{16,0},{20,4},{24,8},{28,12},{1,17},{... | collective-permute-start | bytes 983048 | tf_op jit(solution)/shard_map/ppermute | solution.py:28
  67.1 18.5 %collective-permute-start.14 = (bf16[2,48,2048]{2,1,0:T(8,128)(2,1)S(1)}, bf16[2,48,2048]{2,1,0:T(8,128)(2,1)S(1)}, u32[]{:S(2)}, u32[]{:S(2)}) collective-permute-start(bf16[2,48,2048]{2,1,0:T(8,128)(2,1)S(1)} %slice.140), channel_id=1, source_target_pairs={{0,2},{1,3},{2,0},{3,1},{4,6},{5,7},{6,4},{7,5},{8,10},{9,11},{10,... | collective-permute-start | bytes 1179656 | tf_op jit(solution)/shard_map/ppermute | solution.py:24
  68.8 16.8 %collective-permute-start.13 = (bf16[2,48,2048]{2,1,0:T(8,128)(2,1)S(1)}, bf16[2,48,2048]{2,1,0:T(8,128)(2,1)S(1)}, u32[]{:S(2)}, u32[]{:S(2)}) collective-permute-start(bf16[2,48,2048]{2,1,0:T(8,128)(2,1)S(1)} %slice.139), channel_id=1, source_target_pairs={{0,1},{1,0},{2,3},{3,2},{4,5},{5,4},{6,7},{7,6},{8,9},{9,8},{10,11... | collective-permute-start | bytes 1179656 | tf_op jit(solution)/shard_map/ppermute | solution.py:24
  69.3 12.7 %collective-permute-start.16 = (bf16[80,2048]{1,0:T(8,128)(2,1)}, bf16[80,2048]{1,0:T(8,128)(2,1)S(1)}, u32[]{:S(2)}, u32[]{:S(2)}) collective-permute-start(bf16[80,2048]{1,0:T(8,128)(2,1)} %get-tuple-element.89), channel_id=1, source_target_pairs={{0,8},{4,12},{8,16},{12,20},{16,24},{20,28},{24,0},{28,4},{1,9},{5... | collective-permute-start | bytes 983048 | tf_op jit(solution)/shard_map/ppermute | solution.py:28
  69.3 16.3 %collective-permute-start.15 = (bf16[80,2048]{1,0:T(8,128)(2,1)}, bf16[80,2048]{1,0:T(8,128)(2,1)S(1)}, u32[]{:S(2)}, u32[]{:S(2)}) collective-permute-start(bf16[80,2048]{1,0:T(8,128)(2,1)} %get-tuple-element.91), channel_id=1, source_target_pairs={{0,24},{4,28},{8,0},{12,4},{16,8},{20,12},{24,16},{28,20},{1,25},{... | collective-permute-start | bytes 983048 | tf_op jit(solution)/shard_map/ppermute | solution.py:28
  88.5 37.7 %collective-permute-start.18 = (bf16[4,80,2048]{2,1,0:T(8,128)(2,1)S(1)}, bf16[4,80,2048]{2,1,0:T(8,128)(2,1)S(1)}, u32[]{:S(2)}, u32[]{:S(2)}) collective-permute-start(bf16[4,80,2048]{2,1,0:T(8,128)(2,1)S(1)} %pad_maximum_fusion.2.refs_1_), channel_id=1, source_target_pairs={{0,2},{1,3},{2,0},{3,1},{4,6},{5,7},{6,4},{7,5},{8,10},{9,11},{10,... | collective-permute-start | bytes 3932168 | tf_op jit(solution)/shard_map/ppermute | solution.py:24
  90.2 37.0 %collective-permute-start.17 = (bf16[4,80,2048]{2,1,0:T(8,128)(2,1)S(1)}, bf16[4,80,2048]{2,1,0:T(8,128)(2,1)S(1)}, u32[]{:S(2)}, u32[]{:S(2)}) collective-permute-start(bf16[4,80,2048]{2,1,0:T(8,128)(2,1)S(1)} %pad_maximum_fusion.2.refs_1_), channel_id=1, source_target_pairs={{0,1},{1,0},{2,3},{3,2},{4,5},{5,4},{6,7},{7,6},{8,9},{9,8},{10,11... | collective-permute-start | bytes 3932168 | tf_op jit(solution)/shard_map/ppermute | solution.py:24
  100.3 25.9 %collective-permute-start.19 = (bf16[192,3072]{1,0:T(8,128)(2,1)}, bf16[192,3072]{1,0:T(8,128)(2,1)S(1)}, u32[]{:S(2)}, u32[]{:S(2)}) collective-permute-start(bf16[192,3072]{1,0:T(8,128)(2,1)} %shard_map.77), channel_id=1, source_target_pairs={{0,8},{4,12},{24,16},{28,20},{1,9},{5,13},{25,17},{29,21},{2,10},{... | collective-permute-start | bytes 3538952 | tf_op jit(solution)/shard_map/ppermute | solution.py:28
  131.6 21.4 %collective-permute-start.23 = (bf16[192,3072]{1,0:T(8,128)(2,1)S(1)}, bf16[192,3072]{1,0:T(8,128)(2,1)S(1)}, u32[]{:S(2)}, u32[]{:S(2)}) collective-permute-start(bf16[192,3072]{1,0:T(8,128)(2,1)S(1)} %add_convert_fusion.3), channel_id=1, source_target_pairs={{16,8},{20,12},{24,16},{28,20},{17,9},{21,13},{25,17},{29,21},{18,... | collective-permute-start | bytes 3538952 | tf_op jit(solution)/shard_map/ppermute | solution.py:28
  132.3 27.3 %collective-permute-start.22 = (bf16[192,3072]{1,0:T(8,128)(2,1)S(1)}, bf16[192,3072]{1,0:T(8,128)(2,1)}, u32[]{:S(2)}, u32[]{:S(2)}) collective-permute-start(bf16[192,3072]{1,0:T(8,128)(2,1)S(1)} %add_convert_fusion.3), channel_id=1, source_target_pairs={{0,8},{4,12},{8,16},{12,20},{1,9},{5,13},{9,17},{13,21},{2,10},{6,... | collective-permute-start | bytes 3538952 | tf_op jit(solution)/shard_map/ppermute | solution.py:28
  138.4 13.5 %collective-permute-start.21 = (bf16[2,80,2048]{2,1,0:T(8,128)(2,1)S(1)}, bf16[2,80,2048]{2,1,0:T(8,128)(2,1)S(1)}, u32[]{:S(2)}, u32[]{:S(2)}) collective-permute-start(bf16[2,80,2048]{2,1,0:T(8,128)(2,1)S(1)} %slice.142), channel_id=1, source_target_pairs={{0,2},{1,3},{2,0},{3,1},{4,6},{5,7},{6,4},{7,5},{8,10},{9,11},{10,... | collective-permute-start | bytes 1966088 | tf_op jit(solution)/shard_map/ppermute | solution.py:24
  140.0 13.1 %collective-permute-start.20 = (bf16[2,80,2048]{2,1,0:T(8,128)(2,1)S(1)}, bf16[2,80,2048]{2,1,0:T(8,128)(2,1)S(1)}, u32[]{:S(2)}, u32[]{:S(2)}) collective-permute-start(bf16[2,80,2048]{2,1,0:T(8,128)(2,1)S(1)} %slice.141), channel_id=1, source_target_pairs={{0,1},{1,0},{2,3},{3,2},{4,5},{5,4},{6,7},{7,6},{8,9},{9,8},{10,11... | collective-permute-start | bytes 1966088 | tf_op jit(solution)/shard_map/ppermute | solution.py:24
  163.1 26.9 %collective-permute-start.25 = (bf16[192,3072]{1,0:T(8,128)(2,1)S(1)}, bf16[192,3072]{1,0:T(8,128)(2,1)}, u32[]{:S(2)}, u32[]{:S(2)}) collective-permute-start(bf16[192,3072]{1,0:T(8,128)(2,1)S(1)} %get-tuple-element.79), channel_id=1, source_target_pairs={{8,0},{12,4},{16,8},{20,12},{24,16},{28,20},{9,1},{13,5},{17,9},{2... | collective-permute-start | bytes 3538952 | tf_op jit(solution)/shard_map/ppermute | solution.py:28
  164.4 26.6 %collective-permute-start.24 = (bf16[192,3072]{1,0:T(8,128)(2,1)S(1)}, bf16[192,3072]{1,0:T(8,128)(2,1)}, u32[]{:S(2)}, u32[]{:S(2)}) collective-permute-start(bf16[192,3072]{1,0:T(8,128)(2,1)S(1)} %get-tuple-element.80), channel_id=1, source_target_pairs={{0,8},{4,12},{8,16},{12,20},{16,24},{20,28},{1,9},{5,13},{9,17},{1... | collective-permute-start | bytes 3538952 | tf_op jit(solution)/shard_map/ppermute | solution.py:28
  193.4 20.9 %collective-permute-start.26 = (bf16[160,3072]{1,0:T(8,128)(2,1)S(1)}, bf16[160,3072]{1,0:T(8,128)(2,1)S(1)}, u32[]{:S(2)}, u32[]{:S(2)}) collective-permute-start(bf16[160,3072]{1,0:T(8,128)(2,1)S(1)} %get-tuple-element.85), channel_id=1, source_target_pairs={{0,8},{4,12},{24,16},{28,20},{1,9},{5,13},{25,17},{29,21},{2,10},{... | collective-permute-start | bytes 2949128 | tf_op jit(solution)/shard_map/ppermute | solution.py:28
  214.6 11.4 %collective-permute-start.29 = (bf16[160,3072]{1,0:T(8,128)(2,1)S(1)}, bf16[160,3072]{1,0:T(8,128)(2,1)S(1)}, u32[]{:S(2)}, u32[]{:S(2)}) collective-permute-start(bf16[160,3072]{1,0:T(8,128)(2,1)S(1)} %add_convert_fusion.7), channel_id=1, source_target_pairs={{16,8},{20,12},{24,16},{28,20},{17,9},{21,13},{25,17},{29,21},{18,... | collective-permute-start | bytes 2949128 | tf_op jit(solution)/shard_map/ppermute | solution.py:28
  215.4 27.2 %collective-permute-start.27 = (bf16[160,3072]{1,0:T(8,128)(2,1)S(1)}, bf16[160,3072]{1,0:T(8,128)(2,1)S(1)}, u32[]{:S(2)}, u32[]{:S(2)}) collective-permute-start(bf16[160,3072]{1,0:T(8,128)(2,1)S(1)} %add_convert_fusion.7), channel_id=1, source_target_pairs={{0,8},{4,12},{8,16},{12,20},{1,9},{5,13},{9,17},{13,21},{2,10},{6,... | collective-permute-start | bytes 2949128 | tf_op jit(solution)/shard_map/ppermute | solution.py:28
  220.4 43.2 %collective-permute-start.31 = (bf16[160,3072]{1,0:T(8,128)(2,1)S(1)}, bf16[160,3072]{1,0:T(8,128)(2,1)S(1)}, u32[]{:S(2)}, u32[]{:S(2)}) collective-permute-start(bf16[160,3072]{1,0:T(8,128)(2,1)S(1)} %get-tuple-element.86), channel_id=1, source_target_pairs={{0,8},{4,12},{24,16},{28,20},{1,9},{5,13},{25,17},{29,21},{2,10},{... | collective-permute-start | bytes 2949128 | tf_op jit(solution)/shard_map/ppermute | solution.py:28
  243.2 34.7 %collective-permute-start.28 = (bf16[160,3072]{1,0:T(8,128)(2,1)S(1)}, bf16[160,3072]{1,0:T(8,128)(2,1)S(1)}, u32[]{:S(2)}, u32[]{:S(2)}) collective-permute-start(bf16[160,3072]{1,0:T(8,128)(2,1)S(1)} %get-tuple-element.83), channel_id=1, source_target_pairs={{0,8},{4,12},{8,16},{12,20},{16,24},{20,28},{1,9},{5,13},{9,17},{1... | collective-permute-start | bytes 2949128 | tf_op jit(solution)/shard_map/ppermute | solution.py:28
  247.7 30.2 %collective-permute-start.30 = (bf16[160,3072]{1,0:T(8,128)(2,1)S(1)}, bf16[160,3072]{1,0:T(8,128)(2,1)S(1)}, u32[]{:S(2)}, u32[]{:S(2)}) collective-permute-start(bf16[160,3072]{1,0:T(8,128)(2,1)S(1)} %get-tuple-element.84), channel_id=1, source_target_pairs={{8,0},{12,4},{16,8},{20,12},{24,16},{28,20},{9,1},{13,5},{17,9},{2... | collective-permute-start | bytes 2949128 | tf_op jit(solution)/shard_map/ppermute | solution.py:28
  279.5 21.8 %collective-permute-start.32 = (bf16[160,3072]{1,0:T(8,128)(2,1)S(1)}, bf16[160,3072]{1,0:T(8,128)(2,1)S(1)}, u32[]{:S(2)}, u32[]{:S(2)}) collective-permute-start(bf16[160,3072]{1,0:T(8,128)(2,1)S(1)} %get-tuple-element.82), channel_id=1, source_target_pairs={{0,8},{4,12},{8,16},{12,20},{1,9},{5,13},{9,17},{13,21},{2,10},{6,... | collective-permute-start | bytes 2949128 | tf_op jit(solution)/shard_map/ppermute | solution.py:28
  302.0 20.9 %collective-permute-start.33 = (bf16[160,3072]{1,0:T(8,128)(2,1)S(1)}, bf16[160,3072]{1,0:T(8,128)(2,1)S(1)}, u32[]{:S(2)}, u32[]{:S(2)}) collective-permute-start(bf16[160,3072]{1,0:T(8,128)(2,1)S(1)} %get-tuple-element.87), channel_id=1, source_target_pairs={{0,8},{4,12},{8,16},{12,20},{16,24},{20,28},{1,9},{5,13},{9,17},{1... | collective-permute-start | bytes 2949128 | tf_op jit(solution)/shard_map/ppermute | solution.py:28
  307.3 16.4 %collective-permute-start.35 = (bf16[160,3072]{1,0:T(8,128)(2,1)S(1)}, bf16[160,3072]{1,0:T(8,128)(2,1)S(1)}, u32[]{:S(2)}, u32[]{:S(2)}) collective-permute-start(bf16[160,3072]{1,0:T(8,128)(2,1)S(1)} %get-tuple-element.88), channel_id=1, source_target_pairs={{8,0},{12,4},{16,8},{20,12},{24,16},{28,20},{9,1},{13,5},{17,9},{2... | collective-permute-start | bytes 2949128 | tf_op jit(solution)/shard_map/ppermute | solution.py:28
  311.7 12.8 %collective-permute-start.36 = (bf16[176,1024]{1,0:T(8,128)(2,1)S(1)}, bf16[176,1024]{1,0:T(8,128)(2,1)S(1)}, u32[]{:S(2)}, u32[]{:S(2)}) collective-permute-start(bf16[176,1024]{1,0:T(8,128)(2,1)S(1)} %pad_maximum_fusion.5), channel_id=1, source_target_pairs={{0,4},{4,8},{8,12},{12,16},{16,20},{20,24},{24,28},{1,5},{5,9},{9,... | collective-permute-start | bytes 1081352 | tf_op jit(solution)/shard_map/ppermute | solution.py:152
  (68 other events, 411.7 us)

commit v6 on v5

--- a/solution.py
+++ b/solution.py
@@ -10,6 +10,7 @@
 EPS = 1e-06
 STAGES = (3, 5)
 ROUNDS = ((0, (1, 1), 2, 3, 4, 4), (1, (2, 3), 4, 5, 6, 7))
+LOOSE = (("planes12", 2), ("near1", 4), ("sums0", 4))
 CHAINS = (1, 2)
 RIM = 16
 
@@ -357,7 +358,9 @@
                     send_sums(now - first + 1, terms, arrived)
                     for terms, arrived in zip(chains[stage], sums[stage])
                 ]
+        loose = {name: fresh.pop(name) for name in list(fresh) if (name, now) in LOOSE}
         live = together(fresh)
+        live.update(loose)
         other_weight = live.pop("weight", other_weight)
         for stage in range(count):
             for distances in around:

time: 332 us -> 323 us (0.973)
  waiting for transfers between devices: 152 us -> 142 us
  starting transfers between devices: 77.2 us -> 84.3 us
  local copies, waits for them, and re-layouts: 27.8 us -> 22.5 us
    ppermute x21, waiting for transfers between devices: 132 us -> 106 us  [plane_shift(): lax.ppermute(value, 'ctx', [(a * CORES + c, b * CORES + c) for a, b in ed...]
    ppermute x14, waiting for transfers between devices: 19.8 us -> 35.5 us  [swap(): return lax.ppermute(value, 'fsdp', [(j, j ^ bits) for j in range(count)])]
    ppermute x21, starting transfers between devices: 58.7 us -> 66.9 us  [plane_shift(): lax.ppermute(value, 'ctx', [(a * CORES + c, b * CORES + c) for a, b in ed...]
    unnamed x122 -> x118, local copies, waits for them, and re-layouts: 21.8 us -> 14.9 us
  transfers between devices with their start and end apart: 37 -> 37, of which waited for: 21 -> 22; matrix products, arithmetic and copies ran while one was open for 3% -> 4% of each run, Pallas kernels for 14% -> 14%
where the time goes in v6:
time: 323 us; the launch traced here: 322 us
  waiting for transfers between devices  142 us (44%)
  starting transfers between devices  84.3 us (26%)
  Pallas kernels  50.8 us (16%)
  local copies, waits for them, and re-layouts  22.5 us (7%)
  other arithmetic  21.6 us (7%)
    ppermute x21, waiting for transfers between devices, plane_shift(): lax.ppermute(value, 'ctx', [(a * CORES + c, b * CORES + c) for a, b in ed...  106 us
    ppermute x21, starting transfers between devices, plane_shift(): lax.ppermute(value, 'ctx', [(a * CORES + c, b * CORES + c) for a, b in ed...  66.9 us
    pallas_call x4, Pallas kernels, partial_sums(): pl.pallas_call(lambda *refs: partial_kernel(parts, *refs), out_shape=jax....  44.8 us
    ppermute x14, waiting for transfers between devices, swap(): return lax.ppermute(value, 'fsdp', [(j, j ^ bits) for j in range(count)])  35.5 us
    ppermute x14, starting transfers between devices, swap(): return lax.ppermute(value, 'fsdp', [(j, j ^ bits) for j in range(count)])  15.4 us
    unnamed x118, local copies, waits for them, and re-layouts  14.9 us
  transfers between devices with their start and end apart: 37, of which 22 were waited for; matrix products, arithmetic and copies ran while one was open for 4% of the time, Pallas kernels for 14%

profile of v6, /device:TPU:0, one launch (start us, length us, event | category | flops | bytes accessed | tf_op | source)
XLA Modules:
  0.0 321.7 jit_solution(6296657204455586049)
XLA Ops:
  1.9 3.9 %collective-permute-start.2 = (bf16[48,2048]{1,0:T(8,128)(2,1)S(1)}, bf16[48,2048]{1,0:T(8,128)(2,1)S(1)}, u32[]{:S(2)}, u32[]{:S(2)}) collective-permute-start(bf16[48,2048]{1,0:T(8,128)(2,1)S(1)} %get-tuple-element.102), channel_id=1, source_target_pairs={{0,3},{1,2},{2,1},{3,0},{4,7},{5,6},{6,5},{7,4},{8,11},{9,10},{10,... | collective-permute-start | bytes 589832 | tf_op jit(solution)/shard_map/ppermute | solution.py:25
  7.6 4.0 %collective-permute-done.2.refs_7_ = bf16[48,2048]{1,0:T(8,128)(2,1)S(1)} collective-permute-done((bf16[48,2048]{1,0:T(8,128)(2,1)S(1)}, bf16[48,2048]{1,0:T(8,128)(2,1)S(1)}, u32[]{:S(2)}, u32[]{:S(2)}) %collective-permute-start.2) | collective-permute-done | bytes 196640 | tf_op jit(solution)/shard_map/ppermute | solution.py:25
  11.6 3.3 %collective-permute-done.1.refs_6_ = bf16[48,2048]{1,0:T(8,128)(2,1)S(1)} collective-permute-done((bf16[48,2048]{1,0:T(8,128)(2,1)S(1)}, bf16[48,2048]{1,0:T(8,128)(2,1)S(1)}, u32[]{:S(2)}, u32[]{:S(2)}) %collective-permute-start.1) | collective-permute-done | bytes 196640 | tf_op jit(solution)/shard_map/ppermute | solution.py:25
  27.3 8.9 %collective-permute-done.6.refs_2_ = bf16[48,2048]{1,0:T(8,128)(2,1)S(1)} collective-permute-done((bf16[48,2048]{1,0:T(8,128)(2,1)S(1)}, bf16[48,2048]{1,0:T(8,128)(2,1)S(1)}, u32[]{:S(2)}, u32[]{:S(2)}) %collective-permute-start.6) | collective-permute-done | bytes 196640 | tf_op jit(solution)/shard_map/ppermute | solution.py:29
  36.2 5.7 %collective-permute-done.4.refs_0_ = bf16[48,2048]{1,0:T(8,128)(2,1)S(1)} collective-permute-done((bf16[48,2048]{1,0:T(8,128)(2,1)S(1)}, bf16[48,2048]{1,0:T(8,128)(2,1)S(1)}, u32[]{:S(2)}, u32[]{:S(2)}) %collective-permute-start.4) | collective-permute-done | bytes 196640 | tf_op jit(solution)/shard_map/ppermute | solution.py:29
  48.9 12.6 %collective-permute-done.11.refs_1_ = bf16[4,48,2048]{2,1,0:T(8,128)(2,1)S(1)} collective-permute-done((bf16[4,48,2048]{2,1,0:T(8,128)(2,1)S(1)}, bf16[4,48,2048]{2,1,0:T(8,128)(2,1)S(1)}, u32[]{:S(2)}, u32[]{:S(2)}) %collective-permute-start.11) | collective-permute-done | bytes 786464 | tf_op jit(solution)/shard_map/ppermute | solution.py:25
  70.0 3.8 %collective-permute-start.14 = (bf16[80,2048]{1,0:T(8,128)(2,1)S(1)}, bf16[80,2048]{1,0:T(8,128)(2,1)S(1)}, u32[]{:S(2)}, u32[]{:S(2)}) collective-permute-start(bf16[80,2048]{1,0:T(8,128)(2,1)S(1)} %get-tuple-element.84), channel_id=1, source_target_pairs={{0,24},{4,28},{8,0},{12,4},{16,8},{20,12},{24,16},{28,20},{1,25},{... | collective-permute-start | bytes 983048 | tf_op jit(solution)/shard_map/ppermute | solution.py:29
  74.5 8.3 %collective-permute-done.15.refs_5_ = bf16[80,2048]{1,0:T(8,128)(2,1)S(1)} collective-permute-done((bf16[80,2048]{1,0:T(8,128)(2,1)}, bf16[80,2048]{1,0:T(8,128)(2,1)S(1)}, u32[]{:S(2)}, u32[]{:S(2)}) %collective-permute-start.15) | collective-permute-done | bytes 327712 | tf_op jit(solution)/shard_map/ppermute | solution.py:29
  86.5 9.2 %shard_map.78 = bf16[192,3072]{1,0:T(8,128)(2,1)} custom-call(s32[2]{0:T(128)} %pad_add_fusion.refs_0_, bf16[4,48,2048]{2,1,0:T(8,128)(2,1)} %copy-done.9, bf16[4,48,2048]{2,1,0:T(8,128)(2,1)} %get-tuple-element.57.refs_2_, bf16[4,48,2048]{2,1,0:T(8,128)(2,1)} %get-tuple-element.58.refs_3_, bf16[2,48,2048]{2,1,0:T(8,128)(2,1)} %get-tuple-element.59.refs_4_, ...), custom_call_target="tpu_custom_call" | custom-call | flops 2415919104 | bytes 14548992 | tf_op jit(solution)/shard_map/pallas_call | solution.py:223
  95.6 10.1 %collective-permute-start.21 = (bf16[192,3072]{1,0:T(8,128)(2,1)}, bf16[192,3072]{1,0:T(8,128)(2,1)S(1)}, u32[]{:S(2)}, u32[]{:S(2)}) collective-permute-start(bf16[192,3072]{1,0:T(8,128)(2,1)} %shard_map.78), channel_id=1, source_target_pairs={{0,8},{4,12},{24,16},{28,20},{1,9},{5,13},{25,17},{29,21},{2,10},{... | collective-permute-start | bytes 3538952 | tf_op jit(solution)/shard_map/ppermute | solution.py:29
  110.2 12.9 %shard_map.77 = bf16[768,3072]{1,0:T(8,128)(2,1)S(1)} custom-call(s32[2]{0:T(128)S(1)} %copy-done.30, bf16[4,48,2048]{2,1,0:T(8,128)(2,1)S(1)} %copy-done.10, bf16[4,48,2048]{2,1,0:T(8,128)(2,1)S(1)} %copy-done.5, bf16[4,48,2048]{2,1,0:T(8,128)(2,1)S(1)} %copy-done.3, bf16[2,48,2048]{2,1,0:T(8,128)(2,1)S(1)} %copy-done.16, ...), custom_call_target="tpu_custom_call" | custom-call | flops 9663676416 | bytes 20447232 | tf_op jit(solution)/shard_map/pallas_call | solution.py:223
  123.2 2.8 collective-permute-done.21
  128.1 5.0 %collective-permute-start.22 = (bf16[192,3072]{1,0:T(8,128)(2,1)S(1)}, bf16[192,3072]{1,0:T(8,128)(2,1)}, u32[]{:S(2)}, u32[]{:S(2)}) collective-permute-start(bf16[192,3072]{1,0:T(8,128)(2,1)S(1)} %add_convert_fusion.3), channel_id=1, source_target_pairs={{0,8},{4,12},{8,16},{12,20},{1,9},{5,13},{9,17},{13,21},{2,10},{6,... | collective-permute-start | bytes 3538952 | tf_op jit(solution)/shard_map/ppermute | solution.py:29
  134.4 3.7 %collective-permute-done.17.refs_3_ = bf16[4,80,2048]{2,1,0:T(8,128)(2,1)S(1)} collective-permute-done((bf16[4,80,2048]{2,1,0:T(8,128)(2,1)S(1)}, bf16[4,80,2048]{2,1,0:T(8,128)(2,1)S(1)}, u32[]{:S(2)}, u32[]{:S(2)}) %collective-permute-start.17) | collective-permute-done | bytes 1310752 | tf_op jit(solution)/shard_map/ppermute | solution.py:25
  139.3 8.1 %collective-permute-done.20.refs_1_ = bf16[2,80,2048]{2,1,0:T(8,128)(2,1)S(1)} collective-permute-done((bf16[2,80,2048]{2,1,0:T(8,128)(2,1)S(1)}, bf16[2,80,2048]{2,1,0:T(8,128)(2,1)S(1)}, u32[]{:S(2)}, u32[]{:S(2)}) %collective-permute-start.20) | collective-permute-done | bytes 655392 | tf_op jit(solution)/shard_map/ppermute | solution.py:25
  150.7 3.4 %add_convert_fusion.1 = (bf16[192,3072]{1,0:T(8,128)(2,1)S(1)}, bf16[192,3072]{1,0:T(8,128)(2,1)S(1)}) fusion(bf16[192,3072]{1,0:T(8,128)(2,1)} %get-tuple-element.67, bf16[768,3072]{1,0:T(8,128)(2,1)} %copy-done.8, bf16[192,3072]{1,0:T(8,128)(2,1)} %get-tuple-element.66), kind=kLoop, calls=%fused_computation.7 | loop fusion | flops 4718592 | bytes 7077888 | tf_op jit(solution)/shard_map/convert_element_type | solution.py:297
  155.4 6.1 %collective-permute-start.24 = (bf16[192,3072]{1,0:T(8,128)(2,1)S(1)}, bf16[192,3072]{1,0:T(8,128)(2,1)}, u32[]{:S(2)}, u32[]{:S(2)}) collective-permute-start(bf16[192,3072]{1,0:T(8,128)(2,1)S(1)} %get-tuple-element.72), channel_id=1, source_target_pairs={{0,8},{4,12},{8,16},{12,20},{16,24},{20,28},{1,9},{5,13},{9,17},{1... | collective-permute-start | bytes 3538952 | tf_op jit(solution)/shard_map/ppermute | solution.py:29
  164.3 11.2 %shard_map.81 = bf16[640,3072]{1,0:T(8,128)(2,1)S(1)} custom-call(s32[2]{0:T(128)S(1)} %copy-done.30, bf16[4,80,2048]{2,1,0:T(8,128)(2,1)S(1)} %copy-done.18, bf16[4,80,2048]{2,1,0:T(8,128)(2,1)S(1)} %copy-done.12, bf16[4,80,2048]{2,1,0:T(8,128)(2,1)S(1)} %copy-done.14, bf16[2,80,2048]{2,1,0:T(8,128)(2,1)S(1)} %copy-done.23, ...), custom_call_target="tpu_custom_call" | custom-call | flops 8053063680 | bytes 19136512 | tf_op jit(solution)/shard_map/pallas_call | solution.py:223
  182.1 4.6 %collective-permute-start.26 = (bf16[160,3072]{1,0:T(8,128)(2,1)S(1)}, bf16[160,3072]{1,0:T(8,128)(2,1)S(1)}, u32[]{:S(2)}, u32[]{:S(2)}) collective-permute-start(bf16[160,3072]{1,0:T(8,128)(2,1)S(1)} %get-tuple-element.77), channel_id=1, source_target_pairs={{0,8},{4,12},{24,16},{28,20},{1,9},{5,13},{25,17},{29,21},{2,10},{... | collective-permute-start | bytes 2949128 | tf_op jit(solution)/shard_map/ppermute | solution.py:29
  189.5 11.5 %shard_map.80 = bf16[640,3072]{1,0:T(8,128)(2,1)S(1)} custom-call(s32[2]{0:T(128)S(1)} %copy-done.30, bf16[4,80,2048]{2,1,0:T(8,128)(2,1)S(1)} %copy-done.19, bf16[4,80,2048]{2,1,0:T(8,128)(2,1)S(1)} %copy-done.12, bf16[4,80,2048]{2,1,0:T(8,128)(2,1)S(1)} %copy-done.14, bf16[2,80,2048]{2,1,0:T(8,128)(2,1)S(1)} %copy-done.21, ...), custom_call_target="tpu_custom_call" | custom-call | flops 8053063680 | bytes 19136512 | tf_op jit(solution)/shard_map/pallas_call | solution.py:223
  203.5 5.0 %collective-permute-start.27 = (bf16[160,3072]{1,0:T(8,128)(2,1)S(1)}, bf16[160,3072]{1,0:T(8,128)(2,1)S(1)}, u32[]{:S(2)}, u32[]{:S(2)}) collective-permute-start(bf16[160,3072]{1,0:T(8,128)(2,1)S(1)} %add_convert_fusion.7), channel_id=1, source_target_pairs={{0,8},{4,12},{8,16},{12,20},{1,9},{5,13},{9,17},{13,21},{2,10},{6,... | collective-permute-start | bytes 2949128 | tf_op jit(solution)/shard_map/ppermute | solution.py:29
  208.6 4.6 %collective-permute-start.31 = (bf16[160,3072]{1,0:T(8,128)(2,1)S(1)}, bf16[160,3072]{1,0:T(8,128)(2,1)S(1)}, u32[]{:S(2)}, u32[]{:S(2)}) collective-permute-start(bf16[160,3072]{1,0:T(8,128)(2,1)S(1)} %get-tuple-element.78), channel_id=1, source_target_pairs={{0,8},{4,12},{24,16},{28,20},{1,9},{5,13},{25,17},{29,21},{2,10},{... | collective-permute-start | bytes 2949128 | tf_op jit(solution)/shard_map/ppermute | solution.py:29
  213.1 17.6 %collective-permute-done.27 = bf16[160,3072]{1,0:T(8,128)(2,1)S(1)} collective-permute-done((bf16[160,3072]{1,0:T(8,128)(2,1)S(1)}, bf16[160,3072]{1,0:T(8,128)(2,1)S(1)}, u32[]{:S(2)}, u32[]{:S(2)}) %collective-permute-start.27) | collective-permute-done | bytes 983072 | tf_op jit(solution)/shard_map/ppermute | solution.py:29
  231.4 4.4 %collective-permute-start.28 = (bf16[160,3072]{1,0:T(8,128)(2,1)S(1)}, bf16[160,3072]{1,0:T(8,128)(2,1)S(1)}, u32[]{:S(2)}, u32[]{:S(2)}) collective-permute-start(bf16[160,3072]{1,0:T(8,128)(2,1)S(1)} %get-tuple-element.75), channel_id=1, source_target_pairs={{0,8},{4,12},{8,16},{12,20},{16,24},{20,28},{1,9},{5,13},{9,17},{1... | collective-permute-start | bytes 2949128 | tf_op jit(solution)/shard_map/ppermute | solution.py:29
  237.3 14.5 %collective-permute-done.31 = bf16[160,3072]{1,0:T(8,128)(2,1)S(1)} collective-permute-done((bf16[160,3072]{1,0:T(8,128)(2,1)S(1)}, bf16[160,3072]{1,0:T(8,128)(2,1)S(1)}, u32[]{:S(2)}, u32[]{:S(2)}) %collective-permute-start.31) | collective-permute-done | bytes 983072 | tf_op jit(solution)/shard_map/ppermute | solution.py:29
  251.8 14.3 %collective-permute-done.28 = bf16[160,3072]{1,0:T(8,128)(2,1)S(1)} collective-permute-done((bf16[160,3072]{1,0:T(8,128)(2,1)S(1)}, bf16[160,3072]{1,0:T(8,128)(2,1)S(1)}, u32[]{:S(2)}, u32[]{:S(2)}) %collective-permute-start.28) | collective-permute-done | bytes 983072 | tf_op jit(solution)/shard_map/ppermute | solution.py:29
  267.6 5.0 %collective-permute-start.32 = (bf16[160,3072]{1,0:T(8,128)(2,1)S(1)}, bf16[160,3072]{1,0:T(8,128)(2,1)S(1)}, u32[]{:S(2)}, u32[]{:S(2)}) collective-permute-start(bf16[160,3072]{1,0:T(8,128)(2,1)S(1)} %get-tuple-element.74), channel_id=1, source_target_pairs={{0,8},{4,12},{8,16},{12,20},{1,9},{5,13},{9,17},{13,21},{2,10},{6,... | collective-permute-start | bytes 2949128 | tf_op jit(solution)/shard_map/ppermute | solution.py:29
  272.7 17.3 %collective-permute-done.32 = bf16[160,3072]{1,0:T(8,128)(2,1)S(1)} collective-permute-done((bf16[160,3072]{1,0:T(8,128)(2,1)S(1)}, bf16[160,3072]{1,0:T(8,128)(2,1)S(1)}, u32[]{:S(2)}, u32[]{:S(2)}) %collective-permute-start.32) | collective-permute-done | bytes 983072 | tf_op jit(solution)/shard_map/ppermute | solution.py:29
  290.7 7.0 %collective-permute-start.33 = (bf16[160,3072]{1,0:T(8,128)(2,1)S(1)}, bf16[160,3072]{1,0:T(8,128)(2,1)S(1)}, u32[]{:S(2)}, u32[]{:S(2)}) collective-permute-start(bf16[160,3072]{1,0:T(8,128)(2,1)S(1)} %get-tuple-element.79), channel_id=1, source_target_pairs={{0,8},{4,12},{8,16},{12,20},{16,24},{20,28},{1,9},{5,13},{9,17},{1... | collective-permute-start | bytes 2949128 | tf_op jit(solution)/shard_map/ppermute | solution.py:29
  303.6 7.3 %collective-permute-done.33 = bf16[160,3072]{1,0:T(8,128)(2,1)S(1)} collective-permute-done((bf16[160,3072]{1,0:T(8,128)(2,1)S(1)}, bf16[160,3072]{1,0:T(8,128)(2,1)S(1)}, u32[]{:S(2)}, u32[]{:S(2)}) %collective-permute-start.33) | collective-permute-done | bytes 983072 | tf_op jit(solution)/shard_map/ppermute | solution.py:29
  310.8 3.2 %collective-permute-done.35 = bf16[160,3072]{1,0:T(8,128)(2,1)S(1)} collective-permute-done((bf16[160,3072]{1,0:T(8,128)(2,1)S(1)}, bf16[160,3072]{1,0:T(8,128)(2,1)S(1)}, u32[]{:S(2)}, u32[]{:S(2)}) %collective-permute-start.35) | collective-permute-done | bytes 983072 | tf_op jit(solution)/shard_map/ppermute | solution.py:29
  315.7 6.0 %shard_map.83 = bf16[512,1024]{1,0:T(8,128)(2,1)} custom-call(bf16[512,3072]{1,0:T(8,128)(2,1)S(1)} %pad_maximum_fusion.query.key.value, bf16[512,3072]{1,0:T(8,128)(2,1)S(1)} %pad_maximum_fusion.query.key.value, bf16[512,3072]{1,0:T(8,128)(2,1)S(1)} %pad_maximum_fusion.query.key.value, bf16[176,1024]{1,0:T(8,128)(2,1)S(1)} %collective-permute-done.36.rims, ...), custom_call_target="tpu_custom_call" | custom-call | flops 2621440000 | bytes 5242880 | tf_op jit(solution)/shard_map/pallas_call | solution.py:120
  (215 shorter events, 75.9 us)
Async XLA Ops:
  0.0 15.2 %collective-permute-start.3 = (bf16[3,1024,1024]{2,1,0:T(8,128)(2,1)}, bf16[3,1024,1024]{2,1,0:T(8,128)(2,1)}, u32[]{:S(2)}, u32[]{:S(2)}) collective-permute-start(bf16[3,1024,1024]{2,1,0:T(8,128)(2,1)} %bitcast.71), channel_id=1, source_target_pairs={{0,4},{4,0},{8,12},{12,8},{16,20},{20,16},{24,28},{28,24},{1,5},{5... | collective-permute-start | bytes 18874376 | tf_op jit(solution)/shard_map/ppermute | solution.py:263
  19.6 16.6 %collective-permute-start.6 = (bf16[48,2048]{1,0:T(8,128)(2,1)S(1)}, bf16[48,2048]{1,0:T(8,128)(2,1)S(1)}, u32[]{:S(2)}, u32[]{:S(2)}) collective-permute-start(bf16[48,2048]{1,0:T(8,128)(2,1)S(1)} %get-tuple-element.97), channel_id=1, source_target_pairs={{0,16},{4,20},{8,24},{12,28},{16,0},{20,4},{24,8},{28,12},{1,17},{... | collective-permute-start | bytes 589832 | tf_op jit(solution)/shard_map/ppermute | solution.py:29
  22.2 19.6 %collective-permute-start.7 = (bf16[80,2048]{1,0:T(8,128)(2,1)S(1)}, bf16[80,2048]{1,0:T(8,128)(2,1)S(1)}, u32[]{:S(2)}, u32[]{:S(2)}) collective-permute-start(bf16[80,2048]{1,0:T(8,128)(2,1)S(1)} %copy-done.48), channel_id=1, source_target_pairs={{0,1},{1,0},{2,3},{3,2},{4,5},{5,4},{6,7},{7,6},{8,9},{9,8},{10,11... | collective-permute-start | bytes 983048 | tf_op jit(solution)/shard_map/ppermute | solution.py:25
  23.7 18.1 %collective-permute-start.8 = (bf16[80,2048]{1,0:T(8,128)(2,1)S(1)}, bf16[80,2048]{1,0:T(8,128)(2,1)S(1)}, u32[]{:S(2)}, u32[]{:S(2)}) collective-permute-start(bf16[80,2048]{1,0:T(8,128)(2,1)S(1)} %copy-done.47), channel_id=1, source_target_pairs={{0,2},{1,3},{2,0},{3,1},{4,6},{5,7},{6,4},{7,5},{8,10},{9,11},{10,... | collective-permute-start | bytes 983048 | tf_op jit(solution)/shard_map/ppermute | solution.py:25
  24.5 17.4 %collective-permute-start.9 = (bf16[80,2048]{1,0:T(8,128)(2,1)S(1)}, bf16[80,2048]{1,0:T(8,128)(2,1)S(1)}, u32[]{:S(2)}, u32[]{:S(2)}) collective-permute-start(bf16[80,2048]{1,0:T(8,128)(2,1)S(1)} %copy-done.46), channel_id=1, source_target_pairs={{0,3},{1,2},{2,1},{3,0},{4,7},{5,6},{6,5},{7,4},{8,11},{9,10},{10,... | collective-permute-start | bytes 983048 | tf_op jit(solution)/shard_map/ppermute | solution.py:25
  25.7 10.4 %collective-permute-start.5 = (bf16[48,2048]{1,0:T(8,128)(2,1)S(1)}, bf16[48,2048]{1,0:T(8,128)(2,1)S(1)}, u32[]{:S(2)}, u32[]{:S(2)}) collective-permute-start(bf16[48,2048]{1,0:T(8,128)(2,1)S(1)} %get-tuple-element.98), channel_id=1, source_target_pairs={{0,8},{4,12},{8,16},{12,20},{16,24},{20,28},{24,0},{28,4},{1,9},{5... | collective-permute-start | bytes 589832 | tf_op jit(solution)/shard_map/ppermute | solution.py:29
  44.2 17.3 %collective-permute-start.11 = (bf16[4,48,2048]{2,1,0:T(8,128)(2,1)S(1)}, bf16[4,48,2048]{2,1,0:T(8,128)(2,1)S(1)}, u32[]{:S(2)}, u32[]{:S(2)}) collective-permute-start(bf16[4,48,2048]{2,1,0:T(8,128)(2,1)S(1)} %pad_maximum_fusion.4.refs_1_), channel_id=1, source_target_pairs={{0,2},{1,3},{2,0},{3,1},{4,6},{5,7},{6,4},{7,5},{8,10},{9,11},{10,... | collective-permute-start | bytes 2359304 | tf_op jit(solution)/shard_map/ppermute | solution.py:25
  45.8 16.8 %collective-permute-start.10 = (bf16[4,48,2048]{2,1,0:T(8,128)(2,1)S(1)}, bf16[4,48,2048]{2,1,0:T(8,128)(2,1)S(1)}, u32[]{:S(2)}, u32[]{:S(2)}) collective-permute-start(bf16[4,48,2048]{2,1,0:T(8,128)(2,1)S(1)} %pad_maximum_fusion.4.refs_1_), channel_id=1, source_target_pairs={{0,1},{1,0},{2,3},{3,2},{4,5},{5,4},{6,7},{7,6},{8,9},{9,8},{10,11... | collective-permute-start | bytes 2359304 | tf_op jit(solution)/shard_map/ppermute | solution.py:25
  67.1 17.7 %collective-permute-start.13 = (bf16[2,48,2048]{2,1,0:T(8,128)(2,1)}, bf16[2,48,2048]{2,1,0:T(8,128)(2,1)S(1)}, u32[]{:S(2)}, u32[]{:S(2)}) collective-permute-start(bf16[2,48,2048]{2,1,0:T(8,128)(2,1)} %slice.138), channel_id=1, source_target_pairs={{0,2},{1,3},{2,0},{3,1},{4,6},{5,7},{6,4},{7,5},{8,10},{9,11},{10,... | collective-permute-start | bytes 1179656 | tf_op jit(solution)/shard_map/ppermute | solution.py:25
  68.3 16.5 %collective-permute-start.12 = (bf16[2,48,2048]{2,1,0:T(8,128)(2,1)}, bf16[2,48,2048]{2,1,0:T(8,128)(2,1)S(1)}, u32[]{:S(2)}, u32[]{:S(2)}) collective-permute-start(bf16[2,48,2048]{2,1,0:T(8,128)(2,1)} %slice.137), channel_id=1, source_target_pairs={{0,1},{1,0},{2,3},{3,2},{4,5},{5,4},{6,7},{7,6},{8,9},{9,8},{10,11... | collective-permute-start | bytes 1179656 | tf_op jit(solution)/shard_map/ppermute | solution.py:25
  70.0 12.8 %collective-permute-start.15 = (bf16[80,2048]{1,0:T(8,128)(2,1)}, bf16[80,2048]{1,0:T(8,128)(2,1)S(1)}, u32[]{:S(2)}, u32[]{:S(2)}) collective-permute-start(bf16[80,2048]{1,0:T(8,128)(2,1)} %get-tuple-element.81), channel_id=1, source_target_pairs={{0,8},{4,12},{8,16},{12,20},{16,24},{20,28},{24,0},{28,4},{1,9},{5... | collective-permute-start | bytes 983048 | tf_op jit(solution)/shard_map/ppermute | solution.py:29
  70.0 14.7 %collective-permute-start.14 = (bf16[80,2048]{1,0:T(8,128)(2,1)S(1)}, bf16[80,2048]{1,0:T(8,128)(2,1)S(1)}, u32[]{:S(2)}, u32[]{:S(2)}) collective-permute-start(bf16[80,2048]{1,0:T(8,128)(2,1)S(1)} %get-tuple-element.84), channel_id=1, source_target_pairs={{0,24},{4,28},{8,0},{12,4},{16,8},{20,12},{24,16},{28,20},{1,25},{... | collective-permute-start | bytes 983048 | tf_op jit(solution)/shard_map/ppermute | solution.py:29
  73.9 31.9 %collective-permute-start.16 = (bf16[80,2048]{1,0:T(8,128)(2,1)}, bf16[80,2048]{1,0:T(8,128)(2,1)}, u32[]{:S(2)}, u32[]{:S(2)}) collective-permute-start(bf16[80,2048]{1,0:T(8,128)(2,1)} %get-tuple-element.83), channel_id=1, source_target_pairs={{0,16},{4,20},{8,24},{12,28},{16,0},{20,4},{24,8},{28,12},{1,17},{... | collective-permute-start | bytes 983048 | tf_op jit(solution)/shard_map/ppermute | solution.py:29
  95.6 30.4 %collective-permute-start.21 = (bf16[192,3072]{1,0:T(8,128)(2,1)}, bf16[192,3072]{1,0:T(8,128)(2,1)S(1)}, u32[]{:S(2)}, u32[]{:S(2)}) collective-permute-start(bf16[192,3072]{1,0:T(8,128)(2,1)} %shard_map.78), channel_id=1, source_target_pairs={{0,8},{4,12},{24,16},{28,20},{1,9},{5,13},{25,17},{29,21},{2,10},{... | collective-permute-start | bytes 3538952 | tf_op jit(solution)/shard_map/ppermute | solution.py:29
  106.9 26.2 %collective-permute-start.19 = (bf16[4,80,2048]{2,1,0:T(8,128)(2,1)S(1)}, bf16[4,80,2048]{2,1,0:T(8,128)(2,1)S(1)}, u32[]{:S(2)}, u32[]{:S(2)}) collective-permute-start(bf16[4,80,2048]{2,1,0:T(8,128)(2,1)S(1)} %pad_maximum_fusion.2.refs_1_), channel_id=1, source_target_pairs={{0,1},{1,0},{2,3},{3,2},{4,5},{5,4},{6,7},{7,6},{8,9},{9,8},{10,11... | collective-permute-start | bytes 3932168 | tf_op jit(solution)/shard_map/ppermute | solution.py:25
  108.4 29.7 %collective-permute-start.17 = (bf16[4,80,2048]{2,1,0:T(8,128)(2,1)S(1)}, bf16[4,80,2048]{2,1,0:T(8,128)(2,1)S(1)}, u32[]{:S(2)}, u32[]{:S(2)}) collective-permute-start(bf16[4,80,2048]{2,1,0:T(8,128)(2,1)S(1)} %pad_maximum_fusion.2.refs_1_), channel_id=1, source_target_pairs={{0,2},{1,3},{2,0},{3,1},{4,6},{5,7},{6,4},{7,5},{8,10},{9,11},{10,... | collective-permute-start | bytes 3932168 | tf_op jit(solution)/shard_map/ppermute | solution.py:25
  126.4 23.4 %collective-permute-start.23 = (bf16[192,3072]{1,0:T(8,128)(2,1)S(1)}, bf16[192,3072]{1,0:T(8,128)(2,1)}, u32[]{:S(2)}, u32[]{:S(2)}) collective-permute-start(bf16[192,3072]{1,0:T(8,128)(2,1)S(1)} %add_convert_fusion.3), channel_id=1, source_target_pairs={{16,8},{20,12},{24,16},{28,20},{17,9},{21,13},{25,17},{29,21},{18,... | collective-permute-start | bytes 3538952 | tf_op jit(solution)/shard_map/ppermute | solution.py:29
  128.1 22.4 %collective-permute-start.22 = (bf16[192,3072]{1,0:T(8,128)(2,1)S(1)}, bf16[192,3072]{1,0:T(8,128)(2,1)}, u32[]{:S(2)}, u32[]{:S(2)}) collective-permute-start(bf16[192,3072]{1,0:T(8,128)(2,1)S(1)} %add_convert_fusion.3), channel_id=1, source_target_pairs={{0,8},{4,12},{8,16},{12,20},{1,9},{5,13},{9,17},{13,21},{2,10},{6,... | collective-permute-start | bytes 3538952 | tf_op jit(solution)/shard_map/ppermute | solution.py:29
  133.1 14.2 %collective-permute-start.20 = (bf16[2,80,2048]{2,1,0:T(8,128)(2,1)S(1)}, bf16[2,80,2048]{2,1,0:T(8,128)(2,1)S(1)}, u32[]{:S(2)}, u32[]{:S(2)}) collective-permute-start(bf16[2,80,2048]{2,1,0:T(8,128)(2,1)S(1)} %slice.173), channel_id=1, source_target_pairs={{0,2},{1,3},{2,0},{3,1},{4,6},{5,7},{6,4},{7,5},{8,10},{9,11},{10,... | collective-permute-start | bytes 1966088 | tf_op jit(solution)/shard_map/ppermute | solution.py:25
  139.2 10.7 %collective-permute-start.18 = (bf16[2,80,2048]{2,1,0:T(8,128)(2,1)S(1)}, bf16[2,80,2048]{2,1,0:T(8,128)(2,1)S(1)}, u32[]{:S(2)}, u32[]{:S(2)}) collective-permute-start(bf16[2,80,2048]{2,1,0:T(8,128)(2,1)S(1)} %slice.172), channel_id=1, source_target_pairs={{0,1},{1,0},{2,3},{3,2},{4,5},{5,4},{6,7},{7,6},{8,9},{9,8},{10,11... | collective-permute-start | bytes 1966088 | tf_op jit(solution)/shard_map/ppermute | solution.py:25
  154.1 23.3 %collective-permute-start.25 = (bf16[192,3072]{1,0:T(8,128)(2,1)S(1)}, bf16[192,3072]{1,0:T(8,128)(2,1)}, u32[]{:S(2)}, u32[]{:S(2)}) collective-permute-start(bf16[192,3072]{1,0:T(8,128)(2,1)S(1)} %get-tuple-element.71), channel_id=1, source_target_pairs={{8,0},{12,4},{16,8},{20,12},{24,16},{28,20},{9,1},{13,5},{17,9},{2... | collective-permute-start | bytes 3538952 | tf_op jit(solution)/shard_map/ppermute | solution.py:29
  155.4 24.2 %collective-permute-start.24 = (bf16[192,3072]{1,0:T(8,128)(2,1)S(1)}, bf16[192,3072]{1,0:T(8,128)(2,1)}, u32[]{:S(2)}, u32[]{:S(2)}) collective-permute-start(bf16[192,3072]{1,0:T(8,128)(2,1)S(1)} %get-tuple-element.72), channel_id=1, source_target_pairs={{0,8},{4,12},{8,16},{12,20},{16,24},{20,28},{1,9},{5,13},{9,17},{1... | collective-permute-start | bytes 3538952 | tf_op jit(solution)/shard_map/ppermute | solution.py:29
  182.1 20.4 %collective-permute-start.26 = (bf16[160,3072]{1,0:T(8,128)(2,1)S(1)}, bf16[160,3072]{1,0:T(8,128)(2,1)S(1)}, u32[]{:S(2)}, u32[]{:S(2)}) collective-permute-start(bf16[160,3072]{1,0:T(8,128)(2,1)S(1)} %get-tuple-element.77), channel_id=1, source_target_pairs={{0,8},{4,12},{24,16},{28,20},{1,9},{5,13},{25,17},{29,21},{2,10},{... | collective-permute-start | bytes 2949128 | tf_op jit(solution)/shard_map/ppermute | solution.py:29
  202.8 10.3 %collective-permute-start.29 = (bf16[160,3072]{1,0:T(8,128)(2,1)S(1)}, bf16[160,3072]{1,0:T(8,128)(2,1)S(1)}, u32[]{:S(2)}, u32[]{:S(2)}) collective-permute-start(bf16[160,3072]{1,0:T(8,128)(2,1)S(1)} %add_convert_fusion.7), channel_id=1, source_target_pairs={{16,8},{20,12},{24,16},{28,20},{17,9},{21,13},{25,17},{29,21},{18,... | collective-permute-start | bytes 2949128 | tf_op jit(solution)/shard_map/ppermute | solution.py:29
  203.5 27.2 %collective-permute-start.27 = (bf16[160,3072]{1,0:T(8,128)(2,1)S(1)}, bf16[160,3072]{1,0:T(8,128)(2,1)S(1)}, u32[]{:S(2)}, u32[]{:S(2)}) collective-permute-start(bf16[160,3072]{1,0:T(8,128)(2,1)S(1)} %add_convert_fusion.7), channel_id=1, source_target_pairs={{0,8},{4,12},{8,16},{12,20},{1,9},{5,13},{9,17},{13,21},{2,10},{6,... | collective-permute-start | bytes 2949128 | tf_op jit(solution)/shard_map/ppermute | solution.py:29
  208.6 43.2 %collective-permute-start.31 = (bf16[160,3072]{1,0:T(8,128)(2,1)S(1)}, bf16[160,3072]{1,0:T(8,128)(2,1)S(1)}, u32[]{:S(2)}, u32[]{:S(2)}) collective-permute-start(bf16[160,3072]{1,0:T(8,128)(2,1)S(1)} %get-tuple-element.78), channel_id=1, source_target_pairs={{0,8},{4,12},{24,16},{28,20},{1,9},{5,13},{25,17},{29,21},{2,10},{... | collective-permute-start | bytes 2949128 | tf_op jit(solution)/shard_map/ppermute | solution.py:29
  231.4 34.6 %collective-permute-start.28 = (bf16[160,3072]{1,0:T(8,128)(2,1)S(1)}, bf16[160,3072]{1,0:T(8,128)(2,1)S(1)}, u32[]{:S(2)}, u32[]{:S(2)}) collective-permute-start(bf16[160,3072]{1,0:T(8,128)(2,1)S(1)} %get-tuple-element.75), channel_id=1, source_target_pairs={{0,8},{4,12},{8,16},{12,20},{16,24},{20,28},{1,9},{5,13},{9,17},{1... | collective-permute-start | bytes 2949128 | tf_op jit(solution)/shard_map/ppermute | solution.py:29
  235.9 30.1 %collective-permute-start.30 = (bf16[160,3072]{1,0:T(8,128)(2,1)S(1)}, bf16[160,3072]{1,0:T(8,128)(2,1)S(1)}, u32[]{:S(2)}, u32[]{:S(2)}) collective-permute-start(bf16[160,3072]{1,0:T(8,128)(2,1)S(1)} %get-tuple-element.76), channel_id=1, source_target_pairs={{8,0},{12,4},{16,8},{20,12},{24,16},{28,20},{9,1},{13,5},{17,9},{2... | collective-permute-start | bytes 2949128 | tf_op jit(solution)/shard_map/ppermute | solution.py:29
  267.6 22.4 %collective-permute-start.32 = (bf16[160,3072]{1,0:T(8,128)(2,1)S(1)}, bf16[160,3072]{1,0:T(8,128)(2,1)S(1)}, u32[]{:S(2)}, u32[]{:S(2)}) collective-permute-start(bf16[160,3072]{1,0:T(8,128)(2,1)S(1)} %get-tuple-element.74), channel_id=1, source_target_pairs={{0,8},{4,12},{8,16},{12,20},{1,9},{5,13},{9,17},{13,21},{2,10},{6,... | collective-permute-start | bytes 2949128 | tf_op jit(solution)/shard_map/ppermute | solution.py:29
  290.7 20.1 %collective-permute-start.33 = (bf16[160,3072]{1,0:T(8,128)(2,1)S(1)}, bf16[160,3072]{1,0:T(8,128)(2,1)S(1)}, u32[]{:S(2)}, u32[]{:S(2)}) collective-permute-start(bf16[160,3072]{1,0:T(8,128)(2,1)S(1)} %get-tuple-element.79), channel_id=1, source_target_pairs={{0,8},{4,12},{8,16},{12,20},{16,24},{20,28},{1,9},{5,13},{9,17},{1... | collective-permute-start | bytes 2949128 | tf_op jit(solution)/shard_map/ppermute | solution.py:29
  297.7 16.4 %collective-permute-start.35 = (bf16[160,3072]{1,0:T(8,128)(2,1)S(1)}, bf16[160,3072]{1,0:T(8,128)(2,1)S(1)}, u32[]{:S(2)}, u32[]{:S(2)}) collective-permute-start(bf16[160,3072]{1,0:T(8,128)(2,1)S(1)} %get-tuple-element.80), channel_id=1, source_target_pairs={{8,0},{12,4},{16,8},{20,12},{24,16},{28,20},{9,1},{13,5},{17,9},{2... | collective-permute-start | bytes 2949128 | tf_op jit(solution)/shard_map/ppermute | solution.py:29
  302.0 12.8 %collective-permute-start.36 = (bf16[176,1024]{1,0:T(8,128)(2,1)S(1)}, bf16[176,1024]{1,0:T(8,128)(2,1)S(1)}, u32[]{:S(2)}, u32[]{:S(2)}) collective-permute-start(bf16[176,1024]{1,0:T(8,128)(2,1)S(1)} %pad_maximum_fusion.5), channel_id=1, source_target_pairs={{0,4},{4,8},{8,12},{12,16},{16,20},{20,24},{24,28},{1,5},{5,9},{9,... | collective-permute-start | bytes 1081352 | tf_op jit(solution)/shard_map/ppermute | solution.py:153
  (66 other events, 466.8 us)

commit v7 on v6

--- a/solution.py
+++ b/solution.py
@@ -10,8 +10,8 @@
 EPS = 1e-06
 STAGES = (3, 5)
 ROUNDS = ((0, (1, 1), 2, 3, 4, 4), (1, (2, 3), 4, 5, 6, 7))
-LOOSE = (("planes12", 2), ("near1", 4), ("sums0", 4))
-CHAINS = (1, 2)
+LOOSE = (("planes12", 2), ("near0", 2), ("near1", 4), ("sums0", 4))
+CHAINS = (1, 1)
 RIM = 16
 
 

time: 323 us -> 313 us (0.969)
  starting transfers between devices: 84.3 us -> 67.6 us
  waiting for transfers between devices: 142 us -> 152 us
  local copies, waits for them, and re-layouts: 22.5 us -> 18.7 us
    ppermute x21 -> x16, starting transfers between devices: 66.9 us -> 48.7 us  [plane_shift(): lax.ppermute(value, 'ctx', [(a * CORES + c, b * CORES + c) for a, b in ed...]
    ppermute x21 -> x16, waiting for transfers between devices: 106 us -> 120 us  [plane_shift(): lax.ppermute(value, 'ctx', [(a * CORES + c, b * CORES + c) for a, b in ed...]
    unnamed x118 -> x116, local copies, waits for them, and re-layouts: 14.9 us -> 13.8 us
  transfers between devices with their start and end apart: 37 -> 32, of which waited for: 22 -> 19; matrix products, arithmetic and copies ran while one was open for 4% -> 4% of each run, Pallas kernels for 14% -> 14%
where the time goes in v7:
time: 313 us; the launch traced here: 312 us
  waiting for transfers between devices  152 us (49%)
  starting transfers between devices  67.6 us (22%)
  Pallas kernels  50.5 us (16%)
  other arithmetic  22.1 us (7%)
  local copies, waits for them, and re-layouts  18.7 us (6%)
    ppermute x16, waiting for transfers between devices, plane_shift(): lax.ppermute(value, 'ctx', [(a * CORES + c, b * CORES + c) for a, b in ed...  120 us
    ppermute x16, starting transfers between devices, plane_shift(): lax.ppermute(value, 'ctx', [(a * CORES + c, b * CORES + c) for a, b in ed...  48.7 us
    pallas_call x4, Pallas kernels, partial_sums(): pl.pallas_call(lambda *refs: partial_kernel(parts, *refs), out_shape=jax....  44.6 us
    ppermute x14, waiting for transfers between devices, swap(): return lax.ppermute(value, 'fsdp', [(j, j ^ bits) for j in range(count)])  32.4 us
    ppermute x14, starting transfers between devices, swap(): return lax.ppermute(value, 'fsdp', [(j, j ^ bits) for j in range(count)])  16.9 us
    unnamed x116, local copies, waits for them, and re-layouts  13.8 us
  transfers between devices with their start and end apart: 32, of which 19 were waited for; matrix products, arithmetic and copies ran while one was open for 4% of the time, Pallas kernels for 14%

profile of v7, /device:TPU:0, one launch (start us, length us, event | category | flops | bytes accessed | tf_op | source)
XLA Modules:
  0.0 312.0 jit_solution(16932804681812890212)
XLA Ops:
  1.9 3.9 %collective-permute-start.2 = (bf16[48,2048]{1,0:T(8,128)(2,1)S(1)}, bf16[48,2048]{1,0:T(8,128)(2,1)S(1)}, u32[]{:S(2)}, u32[]{:S(2)}) collective-permute-start(bf16[48,2048]{1,0:T(8,128)(2,1)S(1)} %get-tuple-element.92), channel_id=1, source_target_pairs={{0,3},{1,2},{2,1},{3,0},{4,7},{5,6},{6,5},{7,4},{8,11},{9,10},{10,... | collective-permute-start | bytes 589832 | tf_op jit(solution)/shard_map/ppermute | solution.py:25
  7.6 4.0 %collective-permute-done.2.refs_7_ = bf16[48,2048]{1,0:T(8,128)(2,1)S(1)} collective-permute-done((bf16[48,2048]{1,0:T(8,128)(2,1)S(1)}, bf16[48,2048]{1,0:T(8,128)(2,1)S(1)}, u32[]{:S(2)}, u32[]{:S(2)}) %collective-permute-start.2) | collective-permute-done | bytes 196640 | tf_op jit(solution)/shard_map/ppermute | solution.py:25
  11.6 3.3 %collective-permute-done.1.refs_6_ = bf16[48,2048]{1,0:T(8,128)(2,1)S(1)} collective-permute-done((bf16[48,2048]{1,0:T(8,128)(2,1)S(1)}, bf16[48,2048]{1,0:T(8,128)(2,1)S(1)}, u32[]{:S(2)}, u32[]{:S(2)}) %collective-permute-start.1) | collective-permute-done | bytes 196640 | tf_op jit(solution)/shard_map/ppermute | solution.py:25
  19.6 2.7 collective-permute-start.6
  27.3 8.9 %collective-permute-done.6.refs_2_ = bf16[48,2048]{1,0:T(8,128)(2,1)S(1)} collective-permute-done((bf16[48,2048]{1,0:T(8,128)(2,1)S(1)}, bf16[48,2048]{1,0:T(8,128)(2,1)S(1)}, u32[]{:S(2)}, u32[]{:S(2)}) %collective-permute-start.6) | collective-permute-done | bytes 196640 | tf_op jit(solution)/shard_map/ppermute | solution.py:29
  36.2 5.7 %collective-permute-done.4.refs_0_ = bf16[48,2048]{1,0:T(8,128)(2,1)S(1)} collective-permute-done((bf16[48,2048]{1,0:T(8,128)(2,1)S(1)}, bf16[48,2048]{1,0:T(8,128)(2,1)S(1)}, u32[]{:S(2)}, u32[]{:S(2)}) %collective-permute-start.4) | collective-permute-done | bytes 196640 | tf_op jit(solution)/shard_map/ppermute | solution.py:29
  49.0 12.5 %collective-permute-done.12.refs_2_ = bf16[4,48,2048]{2,1,0:T(8,128)(2,1)S(1)} collective-permute-done((bf16[4,48,2048]{2,1,0:T(8,128)(2,1)S(1)}, bf16[4,48,2048]{2,1,0:T(8,128)(2,1)S(1)}, u32[]{:S(2)}, u32[]{:S(2)}) %collective-permute-start.12) | collective-permute-done | bytes 786464 | tf_op jit(solution)/shard_map/ppermute | solution.py:25
  66.2 3.8 %collective-permute-start.14 = (bf16[80,2048]{1,0:T(8,128)(2,1)S(1)}, bf16[80,2048]{1,0:T(8,128)(2,1)S(1)}, u32[]{:S(2)}, u32[]{:S(2)}) collective-permute-start(bf16[80,2048]{1,0:T(8,128)(2,1)S(1)} %get-tuple-element.74), channel_id=1, source_target_pairs={{0,24},{4,28},{8,0},{12,4},{16,8},{20,12},{24,16},{28,20},{1,25},{... | collective-permute-start | bytes 983048 | tf_op jit(solution)/shard_map/ppermute | solution.py:29
  70.6 8.3 %collective-permute-done.15.refs_5_ = bf16[80,2048]{1,0:T(8,128)(2,1)S(1)} collective-permute-done((bf16[80,2048]{1,0:T(8,128)(2,1)}, bf16[80,2048]{1,0:T(8,128)(2,1)S(1)}, u32[]{:S(2)}, u32[]{:S(2)}) %collective-permute-start.15) | collective-permute-done | bytes 327712 | tf_op jit(solution)/shard_map/ppermute | solution.py:29
  82.1 9.2 %shard_map.77 = bf16[192,3072]{1,0:T(8,128)(2,1)} custom-call(s32[2]{0:T(128)} %pad_add_fusion.refs_0_, bf16[4,48,2048]{2,1,0:T(8,128)(2,1)} %copy-done.9, bf16[4,48,2048]{2,1,0:T(8,128)(2,1)} %get-tuple-element.53.refs_2_, bf16[4,48,2048]{2,1,0:T(8,128)(2,1)} %get-tuple-element.54.refs_3_, bf16[2,48,2048]{2,1,0:T(8,128)(2,1)} %get-tuple-element.55.refs_4_, ...), custom_call_target="tpu_custom_call" | custom-call | flops 2415919104 | bytes 14548992 | tf_op jit(solution)/shard_map/pallas_call | solution.py:223
  91.4 10.2 %collective-permute-start.21 = (bf16[192,3072]{1,0:T(8,128)(2,1)}, bf16[192,3072]{1,0:T(8,128)(2,1)S(1)}, u32[]{:S(2)}, u32[]{:S(2)}) collective-permute-start(bf16[192,3072]{1,0:T(8,128)(2,1)} %shard_map.77), channel_id=1, source_target_pairs={{0,8},{4,12},{24,16},{28,20},{1,9},{5,13},{25,17},{29,21},{2,10},{... | collective-permute-start | bytes 3538952 | tf_op jit(solution)/shard_map/ppermute | solution.py:29
  106.0 12.9 %shard_map.76 = bf16[768,3072]{1,0:T(8,128)(2,1)S(1)} custom-call(s32[2]{0:T(128)S(1)} %copy-done.30, bf16[4,48,2048]{2,1,0:T(8,128)(2,1)S(1)} %copy-done.10, bf16[4,48,2048]{2,1,0:T(8,128)(2,1)S(1)} %copy-done.5, bf16[4,48,2048]{2,1,0:T(8,128)(2,1)S(1)} %copy-done.7, bf16[2,48,2048]{2,1,0:T(8,128)(2,1)S(1)} %copy-done.16, ...), custom_call_target="tpu_custom_call" | custom-call | flops 9663676416 | bytes 20447232 | tf_op jit(solution)/shard_map/pallas_call | solution.py:223
  119.0 2.8 collective-permute-done.21
  124.0 4.9 %collective-permute-start.22 = (bf16[192,3072]{1,0:T(8,128)(2,1)S(1)}, bf16[192,3072]{1,0:T(8,128)(2,1)}, u32[]{:S(2)}, u32[]{:S(2)}) collective-permute-start(bf16[192,3072]{1,0:T(8,128)(2,1)S(1)} %add_convert_fusion.5), channel_id=1, source_target_pairs={{0,8},{4,12},{8,16},{12,20},{1,9},{5,13},{9,17},{13,21},{2,10},{6,... | collective-permute-start | bytes 3538952 | tf_op jit(solution)/shard_map/ppermute | solution.py:29
  134.8 7.3 %collective-permute-done.20.refs_1_ = bf16[2,80,2048]{2,1,0:T(8,128)(2,1)S(1)} collective-permute-done((bf16[2,80,2048]{2,1,0:T(8,128)(2,1)S(1)}, bf16[2,80,2048]{2,1,0:T(8,128)(2,1)S(1)}, u32[]{:S(2)}, u32[]{:S(2)}) %collective-permute-start.20) | collective-permute-done | bytes 655392 | tf_op jit(solution)/shard_map/ppermute | solution.py:25
  142.1 2.2 collective-permute-done.18.refs_0_
  146.3 3.4 %add_convert_fusion.3 = (bf16[192,3072]{1,0:T(8,128)(2,1)S(1)}, bf16[192,3072]{1,0:T(8,128)(2,1)S(1)}) fusion(bf16[192,3072]{1,0:T(8,128)(2,1)} %get-tuple-element.63, bf16[768,3072]{1,0:T(8,128)(2,1)} %copy-done.8, bf16[192,3072]{1,0:T(8,128)(2,1)} %get-tuple-element.62), kind=kLoop, calls=%fused_computation.13 | loop fusion | flops 4718592 | bytes 7077888 | tf_op jit(solution)/shard_map/convert_element_type | solution.py:297
  151.0 6.2 %collective-permute-start.24 = (bf16[192,3072]{1,0:T(8,128)(2,1)S(1)}, bf16[192,3072]{1,0:T(8,128)(2,1)}, u32[]{:S(2)}, u32[]{:S(2)}) collective-permute-start(bf16[192,3072]{1,0:T(8,128)(2,1)S(1)} %get-tuple-element.68), channel_id=1, source_target_pairs={{0,8},{4,12},{8,16},{12,20},{16,24},{20,28},{1,9},{5,13},{9,17},{1... | collective-permute-start | bytes 3538952 | tf_op jit(solution)/shard_map/ppermute | solution.py:29
  157.2 2.8 copy-done.2
  160.0 11.2 %shard_map.80 = bf16[640,3072]{1,0:T(8,128)(2,1)S(1)} custom-call(s32[2]{0:T(128)S(1)} %copy-done.30, bf16[4,80,2048]{2,1,0:T(8,128)(2,1)S(1)} %copy-done.18, bf16[4,80,2048]{2,1,0:T(8,128)(2,1)S(1)} %copy-done.12, bf16[4,80,2048]{2,1,0:T(8,128)(2,1)S(1)} %copy-done.14, bf16[2,80,2048]{2,1,0:T(8,128)(2,1)S(1)} %copy-done.23, ...), custom_call_target="tpu_custom_call" | custom-call | flops 8053063680 | bytes 19136512 | tf_op jit(solution)/shard_map/pallas_call | solution.py:223
  173.1 2.2 collective-permute-done.24.refs_1_
  175.3 2.5 select_bitcast_fusion
  177.8 4.6 %collective-permute-start.26 = (bf16[320,3072]{1,0:T(8,128)(2,1)S(1)}, bf16[320,3072]{1,0:T(8,128)(2,1)S(1)}, u32[]{:S(2)}, u32[]{:S(2)}) collective-permute-start(bf16[320,3072]{1,0:T(8,128)(2,1)S(1)} %select_bitcast_fusion), channel_id=1, source_target_pairs={{0,8},{4,12},{24,16},{28,20},{1,9},{5,13},{25,17},{29,21},{2,10},{... | collective-permute-start | bytes 5898248 | tf_op jit(solution)/shard_map/ppermute | solution.py:29
  182.5 2.8 copy-done.3
  185.2 11.2 %shard_map.79 = bf16[640,3072]{1,0:T(8,128)(2,1)S(1)} custom-call(s32[2]{0:T(128)S(1)} %copy-done.30, bf16[4,80,2048]{2,1,0:T(8,128)(2,1)S(1)} %copy-done.19, bf16[4,80,2048]{2,1,0:T(8,128)(2,1)S(1)} %copy-done.12, bf16[4,80,2048]{2,1,0:T(8,128)(2,1)S(1)} %copy-done.14, bf16[2,80,2048]{2,1,0:T(8,128)(2,1)S(1)} %copy-done.21, ...), custom_call_target="tpu_custom_call" | custom-call | flops 8053063680 | bytes 19136512 | tf_op jit(solution)/shard_map/pallas_call | solution.py:223
  196.5 22.3 %collective-permute-done.26 = bf16[320,3072]{1,0:T(8,128)(2,1)S(1)} collective-permute-done((bf16[320,3072]{1,0:T(8,128)(2,1)S(1)}, bf16[320,3072]{1,0:T(8,128)(2,1)S(1)}, u32[]{:S(2)}, u32[]{:S(2)}) %collective-permute-start.26) | collective-permute-done | bytes 1966112 | tf_op jit(solution)/shard_map/ppermute | solution.py:29
  220.4 5.0 %collective-permute-start.27 = (bf16[320,3072]{1,0:T(8,128)(2,1)S(1)}, bf16[320,3072]{1,0:T(8,128)(2,1)S(1)}, u32[]{:S(2)}, u32[]{:S(2)}) collective-permute-start(bf16[320,3072]{1,0:T(8,128)(2,1)S(1)} %add_convert_fusion.1), channel_id=1, source_target_pairs={{0,8},{4,12},{8,16},{12,20},{1,9},{5,13},{9,17},{13,21},{2,10},{6,... | collective-permute-start | bytes 5898248 | tf_op jit(solution)/shard_map/ppermute | solution.py:29
  225.4 36.9 %collective-permute-done.27 = bf16[320,3072]{1,0:T(8,128)(2,1)S(1)} collective-permute-done((bf16[320,3072]{1,0:T(8,128)(2,1)S(1)}, bf16[320,3072]{1,0:T(8,128)(2,1)S(1)}, u32[]{:S(2)}, u32[]{:S(2)}) %collective-permute-start.27) | collective-permute-done | bytes 1966112 | tf_op jit(solution)/shard_map/ppermute | solution.py:29
  263.9 4.5 %collective-permute-start.28 = (bf16[320,3072]{1,0:T(8,128)(2,1)S(1)}, bf16[320,3072]{1,0:T(8,128)(2,1)S(1)}, u32[]{:S(2)}, u32[]{:S(2)}) collective-permute-start(bf16[320,3072]{1,0:T(8,128)(2,1)S(1)} %get-tuple-element.69), channel_id=1, source_target_pairs={{0,8},{4,12},{8,16},{12,20},{16,24},{20,28},{1,9},{5,13},{9,17},{1... | collective-permute-start | bytes 5898248 | tf_op jit(solution)/shard_map/ppermute | solution.py:29
  269.7 2.6 add_convert_fusion.2
  274.4 29.5 %collective-permute-done.28 = bf16[320,3072]{1,0:T(8,128)(2,1)S(1)} collective-permute-done((bf16[320,3072]{1,0:T(8,128)(2,1)S(1)}, bf16[320,3072]{1,0:T(8,128)(2,1)S(1)}, u32[]{:S(2)}, u32[]{:S(2)}) %collective-permute-start.28) | collective-permute-done | bytes 1966112 | tf_op jit(solution)/shard_map/ppermute | solution.py:29
  306.1 5.9 %shard_map.82 = bf16[512,1024]{1,0:T(8,128)(2,1)} custom-call(bf16[512,3072]{1,0:T(8,128)(2,1)S(1)} %pad_maximum_fusion.query.key.value, bf16[512,3072]{1,0:T(8,128)(2,1)S(1)} %pad_maximum_fusion.query.key.value, bf16[512,3072]{1,0:T(8,128)(2,1)S(1)} %pad_maximum_fusion.query.key.value, bf16[176,1024]{1,0:T(8,128)(2,1)S(1)} %collective-permute-done.31.rims, ...), custom_call_target="tpu_custom_call" | custom-call | flops 2621440000 | bytes 5242880 | tf_op jit(solution)/shard_map/pallas_call | solution.py:120
  (200 shorter events, 55.1 us)
Async XLA Ops:
  0.0 15.2 %collective-permute-start.3 = (bf16[3,1024,1024]{2,1,0:T(8,128)(2,1)}, bf16[3,1024,1024]{2,1,0:T(8,128)(2,1)}, u32[]{:S(2)}, u32[]{:S(2)}) collective-permute-start(bf16[3,1024,1024]{2,1,0:T(8,128)(2,1)} %bitcast.63), channel_id=1, source_target_pairs={{0,4},{4,0},{8,12},{12,8},{16,20},{20,16},{24,28},{28,24},{1,5},{5... | collective-permute-start | bytes 18874376 | tf_op jit(solution)/shard_map/ppermute | solution.py:263
  1.9 9.7 %collective-permute-start.2 = (bf16[48,2048]{1,0:T(8,128)(2,1)S(1)}, bf16[48,2048]{1,0:T(8,128)(2,1)S(1)}, u32[]{:S(2)}, u32[]{:S(2)}) collective-permute-start(bf16[48,2048]{1,0:T(8,128)(2,1)S(1)} %get-tuple-element.92), channel_id=1, source_target_pairs={{0,3},{1,2},{2,1},{3,0},{4,7},{5,6},{6,5},{7,4},{8,11},{9,10},{10,... | collective-permute-start | bytes 589832 | tf_op jit(solution)/shard_map/ppermute | solution.py:25
  5.8 9.1 %collective-permute-start.1 = (bf16[48,2048]{1,0:T(8,128)(2,1)S(1)}, bf16[48,2048]{1,0:T(8,128)(2,1)S(1)}, u32[]{:S(2)}, u32[]{:S(2)}) collective-permute-start(bf16[48,2048]{1,0:T(8,128)(2,1)S(1)} %get-tuple-element.93), channel_id=1, source_target_pairs={{0,2},{1,3},{2,0},{3,1},{4,6},{5,7},{6,4},{7,5},{8,10},{9,11},{10,... | collective-permute-start | bytes 589832 | tf_op jit(solution)/shard_map/ppermute | solution.py:25
  6.3 8.9 %collective-permute-start = (bf16[48,2048]{1,0:T(8,128)(2,1)S(1)}, bf16[48,2048]{1,0:T(8,128)(2,1)S(1)}, u32[]{:S(2)}, u32[]{:S(2)}) collective-permute-start(bf16[48,2048]{1,0:T(8,128)(2,1)S(1)} %get-tuple-element.94), channel_id=1, source_target_pairs={{0,1},{1,0},{2,3},{3,2},{4,5},{5,4},{6,7},{7,6},{8,9},{9,8},{10,11... | collective-permute-start | bytes 589832 | tf_op jit(solution)/shard_map/ppermute | solution.py:25
  19.6 16.6 %collective-permute-start.6 = (bf16[48,2048]{1,0:T(8,128)(2,1)S(1)}, bf16[48,2048]{1,0:T(8,128)(2,1)S(1)}, u32[]{:S(2)}, u32[]{:S(2)}) collective-permute-start(bf16[48,2048]{1,0:T(8,128)(2,1)S(1)} %get-tuple-element.87), channel_id=1, source_target_pairs={{0,16},{4,20},{8,24},{12,28},{16,0},{20,4},{24,8},{28,12},{1,17},{... | collective-permute-start | bytes 589832 | tf_op jit(solution)/shard_map/ppermute | solution.py:29
  22.2 19.6 %collective-permute-start.7 = (bf16[80,2048]{1,0:T(8,128)(2,1)S(1)}, bf16[80,2048]{1,0:T(8,128)(2,1)S(1)}, u32[]{:S(2)}, u32[]{:S(2)}) collective-permute-start(bf16[80,2048]{1,0:T(8,128)(2,1)S(1)} %copy-done.47), channel_id=1, source_target_pairs={{0,1},{1,0},{2,3},{3,2},{4,5},{5,4},{6,7},{7,6},{8,9},{9,8},{10,11... | collective-permute-start | bytes 983048 | tf_op jit(solution)/shard_map/ppermute | solution.py:25
  23.7 18.1 %collective-permute-start.8 = (bf16[80,2048]{1,0:T(8,128)(2,1)S(1)}, bf16[80,2048]{1,0:T(8,128)(2,1)S(1)}, u32[]{:S(2)}, u32[]{:S(2)}) collective-permute-start(bf16[80,2048]{1,0:T(8,128)(2,1)S(1)} %copy-done.46), channel_id=1, source_target_pairs={{0,2},{1,3},{2,0},{3,1},{4,6},{5,7},{6,4},{7,5},{8,10},{9,11},{10,... | collective-permute-start | bytes 983048 | tf_op jit(solution)/shard_map/ppermute | solution.py:25
  24.5 17.3 %collective-permute-start.9 = (bf16[80,2048]{1,0:T(8,128)(2,1)S(1)}, bf16[80,2048]{1,0:T(8,128)(2,1)S(1)}, u32[]{:S(2)}, u32[]{:S(2)}) collective-permute-start(bf16[80,2048]{1,0:T(8,128)(2,1)S(1)} %copy-done.45), channel_id=1, source_target_pairs={{0,3},{1,2},{2,1},{3,0},{4,7},{5,6},{6,5},{7,4},{8,11},{9,10},{10,... | collective-permute-start | bytes 983048 | tf_op jit(solution)/shard_map/ppermute | solution.py:25
  25.7 10.4 %collective-permute-start.5 = (bf16[48,2048]{1,0:T(8,128)(2,1)S(1)}, bf16[48,2048]{1,0:T(8,128)(2,1)S(1)}, u32[]{:S(2)}, u32[]{:S(2)}) collective-permute-start(bf16[48,2048]{1,0:T(8,128)(2,1)S(1)} %get-tuple-element.88), channel_id=1, source_target_pairs={{0,8},{4,12},{8,16},{12,20},{16,24},{20,28},{24,0},{28,4},{1,9},{5... | collective-permute-start | bytes 589832 | tf_op jit(solution)/shard_map/ppermute | solution.py:29
  36.1 5.7 %collective-permute-start.4 = (bf16[48,2048]{1,0:T(8,128)(2,1)S(1)}, bf16[48,2048]{1,0:T(8,128)(2,1)S(1)}, u32[]{:S(2)}, u32[]{:S(2)}) collective-permute-start(bf16[48,2048]{1,0:T(8,128)(2,1)S(1)} %get-tuple-element.89), channel_id=1, source_target_pairs={{0,24},{4,28},{8,0},{12,4},{16,8},{20,12},{24,16},{28,20},{1,25},{... | collective-permute-start | bytes 589832 | tf_op jit(solution)/shard_map/ppermute | solution.py:29
  44.2 17.3 %collective-permute-start.12 = (bf16[4,48,2048]{2,1,0:T(8,128)(2,1)S(1)}, bf16[4,48,2048]{2,1,0:T(8,128)(2,1)S(1)}, u32[]{:S(2)}, u32[]{:S(2)}) collective-permute-start(bf16[4,48,2048]{2,1,0:T(8,128)(2,1)S(1)} %pad_maximum_fusion.4.refs_1_), channel_id=1, source_target_pairs={{0,1},{1,0},{2,3},{3,2},{4,5},{5,4},{6,7},{7,6},{8,9},{9,8},{10,11... | collective-permute-start | bytes 2359304 | tf_op jit(solution)/shard_map/ppermute | solution.py:25
  45.8 18.1 %collective-permute-start.10 = (bf16[4,48,2048]{2,1,0:T(8,128)(2,1)S(1)}, bf16[4,48,2048]{2,1,0:T(8,128)(2,1)S(1)}, u32[]{:S(2)}, u32[]{:S(2)}) collective-permute-start(bf16[4,48,2048]{2,1,0:T(8,128)(2,1)S(1)} %pad_maximum_fusion.4.refs_1_), channel_id=1, source_target_pairs={{0,2},{1,3},{2,0},{3,1},{4,6},{5,7},{6,4},{7,5},{8,10},{9,11},{10,... | collective-permute-start | bytes 2359304 | tf_op jit(solution)/shard_map/ppermute | solution.py:25
  61.6 18.9 %collective-permute-start.13 = (bf16[2,48,2048]{2,1,0:T(8,128)(2,1)S(1)}, bf16[2,48,2048]{2,1,0:T(8,128)(2,1)S(1)}, u32[]{:S(2)}, u32[]{:S(2)}) collective-permute-start(bf16[2,48,2048]{2,1,0:T(8,128)(2,1)S(1)} %slice.125), channel_id=1, source_target_pairs={{0,2},{1,3},{2,0},{3,1},{4,6},{5,7},{6,4},{7,5},{8,10},{9,11},{10,... | collective-permute-start | bytes 1179656 | tf_op jit(solution)/shard_map/ppermute | solution.py:25
  64.8 15.7 %collective-permute-start.11 = (bf16[2,48,2048]{2,1,0:T(8,128)(2,1)}, bf16[2,48,2048]{2,1,0:T(8,128)(2,1)S(1)}, u32[]{:S(2)}, u32[]{:S(2)}) collective-permute-start(bf16[2,48,2048]{2,1,0:T(8,128)(2,1)} %slice.124), channel_id=1, source_target_pairs={{0,1},{1,0},{2,3},{3,2},{4,5},{5,4},{6,7},{7,6},{8,9},{9,8},{10,11... | collective-permute-start | bytes 1179656 | tf_op jit(solution)/shard_map/ppermute | solution.py:25
  66.1 12.8 %collective-permute-start.15 = (bf16[80,2048]{1,0:T(8,128)(2,1)}, bf16[80,2048]{1,0:T(8,128)(2,1)S(1)}, u32[]{:S(2)}, u32[]{:S(2)}) collective-permute-start(bf16[80,2048]{1,0:T(8,128)(2,1)} %get-tuple-element.71), channel_id=1, source_target_pairs={{0,8},{4,12},{8,16},{12,20},{16,24},{20,28},{24,0},{28,4},{1,9},{5... | collective-permute-start | bytes 983048 | tf_op jit(solution)/shard_map/ppermute | solution.py:29
  66.2 14.3 %collective-permute-start.14 = (bf16[80,2048]{1,0:T(8,128)(2,1)S(1)}, bf16[80,2048]{1,0:T(8,128)(2,1)S(1)}, u32[]{:S(2)}, u32[]{:S(2)}) collective-permute-start(bf16[80,2048]{1,0:T(8,128)(2,1)S(1)} %get-tuple-element.74), channel_id=1, source_target_pairs={{0,24},{4,28},{8,0},{12,4},{16,8},{20,12},{24,16},{28,20},{1,25},{... | collective-permute-start | bytes 983048 | tf_op jit(solution)/shard_map/ppermute | solution.py:29
  70.0 31.6 %collective-permute-start.16 = (bf16[80,2048]{1,0:T(8,128)(2,1)}, bf16[80,2048]{1,0:T(8,128)(2,1)}, u32[]{:S(2)}, u32[]{:S(2)}) collective-permute-start(bf16[80,2048]{1,0:T(8,128)(2,1)} %get-tuple-element.73), channel_id=1, source_target_pairs={{0,16},{4,20},{8,24},{12,28},{16,0},{20,4},{24,8},{28,12},{1,17},{... | collective-permute-start | bytes 983048 | tf_op jit(solution)/shard_map/ppermute | solution.py:29
  91.4 30.5 %collective-permute-start.21 = (bf16[192,3072]{1,0:T(8,128)(2,1)}, bf16[192,3072]{1,0:T(8,128)(2,1)S(1)}, u32[]{:S(2)}, u32[]{:S(2)}) collective-permute-start(bf16[192,3072]{1,0:T(8,128)(2,1)} %shard_map.77), channel_id=1, source_target_pairs={{0,8},{4,12},{24,16},{28,20},{1,9},{5,13},{25,17},{29,21},{2,10},{... | collective-permute-start | bytes 3538952 | tf_op jit(solution)/shard_map/ppermute | solution.py:29
  102.8 26.5 %collective-permute-start.19 = (bf16[4,80,2048]{2,1,0:T(8,128)(2,1)S(1)}, bf16[4,80,2048]{2,1,0:T(8,128)(2,1)S(1)}, u32[]{:S(2)}, u32[]{:S(2)}) collective-permute-start(bf16[4,80,2048]{2,1,0:T(8,128)(2,1)S(1)} %pad_maximum_fusion.2.refs_1_), channel_id=1, source_target_pairs={{0,1},{1,0},{2,3},{3,2},{4,5},{5,4},{6,7},{7,6},{8,9},{9,8},{10,11... | collective-permute-start | bytes 3932168 | tf_op jit(solution)/shard_map/ppermute | solution.py:25
  104.8 27.7 %collective-permute-start.17 = (bf16[4,80,2048]{2,1,0:T(8,128)(2,1)S(1)}, bf16[4,80,2048]{2,1,0:T(8,128)(2,1)S(1)}, u32[]{:S(2)}, u32[]{:S(2)}) collective-permute-start(bf16[4,80,2048]{2,1,0:T(8,128)(2,1)S(1)} %pad_maximum_fusion.2.refs_1_), channel_id=1, source_target_pairs={{0,2},{1,3},{2,0},{3,1},{4,6},{5,7},{6,4},{7,5},{8,10},{9,11},{10,... | collective-permute-start | bytes 3932168 | tf_op jit(solution)/shard_map/ppermute | solution.py:25
  122.2 22.1 %collective-permute-start.23 = (bf16[192,3072]{1,0:T(8,128)(2,1)S(1)}, bf16[192,3072]{1,0:T(8,128)(2,1)}, u32[]{:S(2)}, u32[]{:S(2)}) collective-permute-start(bf16[192,3072]{1,0:T(8,128)(2,1)S(1)} %add_convert_fusion.5), channel_id=1, source_target_pairs={{16,8},{20,12},{24,16},{28,20},{17,9},{21,13},{25,17},{29,21},{18,... | collective-permute-start | bytes 3538952 | tf_op jit(solution)/shard_map/ppermute | solution.py:29
  124.0 22.3 %collective-permute-start.22 = (bf16[192,3072]{1,0:T(8,128)(2,1)S(1)}, bf16[192,3072]{1,0:T(8,128)(2,1)}, u32[]{:S(2)}, u32[]{:S(2)}) collective-permute-start(bf16[192,3072]{1,0:T(8,128)(2,1)S(1)} %add_convert_fusion.5), channel_id=1, source_target_pairs={{0,8},{4,12},{8,16},{12,20},{1,9},{5,13},{9,17},{13,21},{2,10},{6,... | collective-permute-start | bytes 3538952 | tf_op jit(solution)/shard_map/ppermute | solution.py:29
  129.3 12.8 %collective-permute-start.20 = (bf16[2,80,2048]{2,1,0:T(8,128)(2,1)S(1)}, bf16[2,80,2048]{2,1,0:T(8,128)(2,1)S(1)}, u32[]{:S(2)}, u32[]{:S(2)}) collective-permute-start(bf16[2,80,2048]{2,1,0:T(8,128)(2,1)S(1)} %slice.129), channel_id=1, source_target_pairs={{0,2},{1,3},{2,0},{3,1},{4,6},{5,7},{6,4},{7,5},{8,10},{9,11},{10,... | collective-permute-start | bytes 1966088 | tf_op jit(solution)/shard_map/ppermute | solution.py:25
  133.7 10.7 %collective-permute-start.18 = (bf16[2,80,2048]{2,1,0:T(8,128)(2,1)S(1)}, bf16[2,80,2048]{2,1,0:T(8,128)(2,1)S(1)}, u32[]{:S(2)}, u32[]{:S(2)}) collective-permute-start(bf16[2,80,2048]{2,1,0:T(8,128)(2,1)S(1)} %slice.128), channel_id=1, source_target_pairs={{0,1},{1,0},{2,3},{3,2},{4,5},{5,4},{6,7},{7,6},{8,9},{9,8},{10,11... | collective-permute-start | bytes 1966088 | tf_op jit(solution)/shard_map/ppermute | solution.py:25
  149.7 23.4 %collective-permute-start.25 = (bf16[192,3072]{1,0:T(8,128)(2,1)S(1)}, bf16[192,3072]{1,0:T(8,128)(2,1)}, u32[]{:S(2)}, u32[]{:S(2)}) collective-permute-start(bf16[192,3072]{1,0:T(8,128)(2,1)S(1)} %get-tuple-element.67), channel_id=1, source_target_pairs={{8,0},{12,4},{16,8},{20,12},{24,16},{28,20},{9,1},{13,5},{17,9},{2... | collective-permute-start | bytes 3538952 | tf_op jit(solution)/shard_map/ppermute | solution.py:29
  151.0 24.3 %collective-permute-start.24 = (bf16[192,3072]{1,0:T(8,128)(2,1)S(1)}, bf16[192,3072]{1,0:T(8,128)(2,1)}, u32[]{:S(2)}, u32[]{:S(2)}) collective-permute-start(bf16[192,3072]{1,0:T(8,128)(2,1)S(1)} %get-tuple-element.68), channel_id=1, source_target_pairs={{0,8},{4,12},{8,16},{12,20},{16,24},{20,28},{1,9},{5,13},{9,17},{1... | collective-permute-start | bytes 3538952 | tf_op jit(solution)/shard_map/ppermute | solution.py:29
  177.8 40.9 %collective-permute-start.26 = (bf16[320,3072]{1,0:T(8,128)(2,1)S(1)}, bf16[320,3072]{1,0:T(8,128)(2,1)S(1)}, u32[]{:S(2)}, u32[]{:S(2)}) collective-permute-start(bf16[320,3072]{1,0:T(8,128)(2,1)S(1)} %select_bitcast_fusion), channel_id=1, source_target_pairs={{0,8},{4,12},{24,16},{28,20},{1,9},{5,13},{25,17},{29,21},{2,10},{... | collective-permute-start | bytes 5898248 | tf_op jit(solution)/shard_map/ppermute | solution.py:29
  219.5 6.0 %collective-permute-start.29 = (bf16[320,3072]{1,0:T(8,128)(2,1)S(1)}, bf16[320,3072]{1,0:T(8,128)(2,1)S(1)}, u32[]{:S(2)}, u32[]{:S(2)}) collective-permute-start(bf16[320,3072]{1,0:T(8,128)(2,1)S(1)} %add_convert_fusion.1), channel_id=1, source_target_pairs={{16,8},{20,12},{24,16},{28,20},{17,9},{21,13},{25,17},{29,21},{18,... | collective-permute-start | bytes 5898248 | tf_op jit(solution)/shard_map/ppermute | solution.py:29
  220.4 41.9 %collective-permute-start.27 = (bf16[320,3072]{1,0:T(8,128)(2,1)S(1)}, bf16[320,3072]{1,0:T(8,128)(2,1)S(1)}, u32[]{:S(2)}, u32[]{:S(2)}) collective-permute-start(bf16[320,3072]{1,0:T(8,128)(2,1)S(1)} %add_convert_fusion.1), channel_id=1, source_target_pairs={{0,8},{4,12},{8,16},{12,20},{1,9},{5,13},{9,17},{13,21},{2,10},{6,... | collective-permute-start | bytes 5898248 | tf_op jit(solution)/shard_map/ppermute | solution.py:29
  263.9 40.1 %collective-permute-start.28 = (bf16[320,3072]{1,0:T(8,128)(2,1)S(1)}, bf16[320,3072]{1,0:T(8,128)(2,1)S(1)}, u32[]{:S(2)}, u32[]{:S(2)}) collective-permute-start(bf16[320,3072]{1,0:T(8,128)(2,1)S(1)} %get-tuple-element.69), channel_id=1, source_target_pairs={{0,8},{4,12},{8,16},{12,20},{16,24},{20,28},{1,9},{5,13},{9,17},{1... | collective-permute-start | bytes 5898248 | tf_op jit(solution)/shard_map/ppermute | solution.py:29
  268.4 35.5 %collective-permute-start.30 = (bf16[320,3072]{1,0:T(8,128)(2,1)S(1)}, bf16[320,3072]{1,0:T(8,128)(2,1)S(1)}, u32[]{:S(2)}, u32[]{:S(2)}) collective-permute-start(bf16[320,3072]{1,0:T(8,128)(2,1)S(1)} %get-tuple-element.70), channel_id=1, source_target_pairs={{8,0},{12,4},{16,8},{20,12},{24,16},{28,20},{9,1},{13,5},{17,9},{2... | collective-permute-start | bytes 5898248 | tf_op jit(solution)/shard_map/ppermute | solution.py:29
  272.9 32.3 %collective-permute-start.31 = (bf16[176,1024]{1,0:T(8,128)(2,1)S(1)}, bf16[176,1024]{1,0:T(8,128)(2,1)S(1)}, u32[]{:S(2)}, u32[]{:S(2)}) collective-permute-start(bf16[176,1024]{1,0:T(8,128)(2,1)S(1)} %pad_maximum_fusion.5), channel_id=1, source_target_pairs={{0,4},{4,8},{8,12},{12,16},{16,20},{20,24},{24,28},{1,5},{5,9},{9,... | collective-permute-start | bytes 1081352 | tf_op jit(solution)/shard_map/ppermute | solution.py:153
  (60 other events, 505.2 us)

commit v8 on v7

--- a/solution.py
+++ b/solution.py
@@ -352,7 +352,7 @@
                     split(stage, [product(stage, planes, 0)])
                     fresh[f"sums{stage}"] = [send_sums(1, chains[stage][0], [None], lead)]
                 else:
-                    fresh[f"lead{stage}"] = product(stage, planes // 2, 0)
+                    fresh[f"lead{stage}"] = product(stage, 1, None)
             if first < now < first + steps:
                 fresh[f"sums{stage}"] = [
                     send_sums(now - first + 1, terms, arrived)
@@ -369,10 +369,12 @@
                 sums[stage] = live.pop(f"sums{stage}")
 
     last = count - 1
-    split(last, [live[f"lead{last}"], product(last, planes // 2, 1)])
+    split(last, [product(last, planes, 0)])
+    leads = jnp.split(live[f"lead{last}"][0], CHAINS[last], axis=0)
     for step in range(1, planes):
         sums[last] = [
-            send_sums(step, terms, arrived) for terms, arrived in zip(chains[last], sums[last])
+            send_sums(step, terms, arrived, lead if step == 1 else None)
+            for terms, arrived, lead in zip(chains[last], sums[last], leads)
         ]
 
     def summed(stage):

time: 313 us -> 309 us (0.987)
  Pallas kernels: 50.5 us -> 59.6 us
  waiting for transfers between devices: 152 us -> 143 us
  starting transfers between devices: 67.6 us -> 61.7 us
    pallas_call x4, Pallas kernels: 44.6 us -> 53.7 us  [partial_sums(): pl.pallas_call(lambda *refs: partial_kernel(parts, *refs), out_shape=jax....]
    ppermute x16, waiting for transfers between devices: 120 us -> 112 us  [plane_shift(): lax.ppermute(value, 'ctx', [(a * CORES + c, b * CORES + c) for a, b in ed...]
    convert_element_type x4, other arithmetic: 6.04 us -> 10.9 us  [onward(): (term.astype(jnp.float32) + came.astype(jnp.float32)).astype(jnp.bfloat16)]
    ppermute x16, starting transfers between devices: 48.7 us -> 44 us  [plane_shift(): lax.ppermute(value, 'ctx', [(a * CORES + c, b * CORES + c) for a, b in ed...]
    unnamed x116 -> x118, local copies, waits for them, and re-layouts: 13.8 us -> 13.7 us
  transfers between devices with their start and end apart: 32 -> 32, of which waited for: 19 -> 17; matrix products, arithmetic and copies ran while one was open for 4% -> 5% of each run, Pallas kernels for 14% -> 17%
where the time goes in v8:
time: 309 us
  waiting for transfers between devices  143 us (46%)
  starting transfers between devices  61.7 us (20%)
  Pallas kernels  59.6 us (19%)
  other arithmetic  25.2 us (8%)
  local copies, waits for them, and re-layouts  17.8 us (6%)
    ppermute x16, waiting for transfers between devices, plane_shift(): lax.ppermute(value, 'ctx', [(a * CORES + c, b * CORES + c) for a, b in ed...  112 us
    pallas_call x4, Pallas kernels, partial_sums(): pl.pallas_call(lambda *refs: partial_kernel(parts, *refs), out_shape=jax....  53.7 us
    ppermute x16, starting transfers between devices, plane_shift(): lax.ppermute(value, 'ctx', [(a * CORES + c, b * CORES + c) for a, b in ed...  44 us
    ppermute x14, waiting for transfers between devices, swap(): return lax.ppermute(value, 'fsdp', [(j, j ^ bits) for j in range(count)])  31.7 us
    ppermute x14, starting transfers between devices, swap(): return lax.ppermute(value, 'fsdp', [(j, j ^ bits) for j in range(count)])  15.6 us
    unnamed x118, local copies, waits for them, and re-layouts  13.7 us
    convert_element_type x4, other arithmetic, onward(): (term.astype(jnp.float32) + came.astype(jnp.float32)).astype(jnp.bfloat16)  10.9 us
  transfers between devices with their start and end apart: 32, of which 17 were waited for; matrix products, arithmetic and copies ran while one was open for 5% of the time, Pallas kernels for 17%

profile of v8, /device:TPU:0, one launch (start us, length us, event | category | flops | bytes accessed | tf_op | source)
XLA Modules:
  0.0 308.6 jit_solution(7355099228230326327)
XLA Ops:
  1.9 2.9 collective-permute-start
  7.6 3.0 collective-permute-done.refs_5_
  10.5 4.8 %collective-permute-done.1.refs_6_ = bf16[48,2048]{1,0:T(8,128)(2,1)S(1)} collective-permute-done((bf16[48,2048]{1,0:T(8,128)(2,1)S(1)}, bf16[48,2048]{1,0:T(8,128)(2,1)S(1)}, u32[]{:S(2)}, u32[]{:S(2)}) %collective-permute-start.1) | collective-permute-done | bytes 196640 | tf_op jit(solution)/shard_map/ppermute | solution.py:25
  19.8 3.7 %collective-permute-start.4 = (bf16[48,2048]{1,0:T(8,128)(2,1)S(1)}, bf16[48,2048]{1,0:T(8,128)(2,1)S(1)}, u32[]{:S(2)}, u32[]{:S(2)}) collective-permute-start(bf16[48,2048]{1,0:T(8,128)(2,1)S(1)} %get-tuple-element.89), channel_id=1, source_target_pairs={{0,24},{4,28},{8,0},{12,4},{16,8},{20,12},{24,16},{28,20},{1,25},{... | collective-permute-start | bytes 589832 | tf_op jit(solution)/shard_map/ppermute | solution.py:29
  28.5 6.9 %collective-permute-done.5.refs_1_ = bf16[48,2048]{1,0:T(8,128)(2,1)S(1)} collective-permute-done((bf16[48,2048]{1,0:T(8,128)(2,1)S(1)}, bf16[48,2048]{1,0:T(8,128)(2,1)S(1)}, u32[]{:S(2)}, u32[]{:S(2)}) %collective-permute-start.5) | collective-permute-done | bytes 196640 | tf_op jit(solution)/shard_map/ppermute | solution.py:29
  35.4 5.4 %collective-permute-done.6.refs_2_ = bf16[48,2048]{1,0:T(8,128)(2,1)S(1)} collective-permute-done((bf16[48,2048]{1,0:T(8,128)(2,1)S(1)}, bf16[48,2048]{1,0:T(8,128)(2,1)S(1)}, u32[]{:S(2)}, u32[]{:S(2)}) %collective-permute-start.6) | collective-permute-done | bytes 196640 | tf_op jit(solution)/shard_map/ppermute | solution.py:29
  48.1 13.7 %collective-permute-done.10.refs_3_ = bf16[4,48,2048]{2,1,0:T(8,128)(2,1)S(1)} collective-permute-done((bf16[4,48,2048]{2,1,0:T(8,128)(2,1)S(1)}, bf16[4,48,2048]{2,1,0:T(8,128)(2,1)S(1)}, u32[]{:S(2)}, u32[]{:S(2)}) %collective-permute-start.10) | collective-permute-done | bytes 786464 | tf_op jit(solution)/shard_map/ppermute | solution.py:25
  65.2 2.6 collective-permute-start.14
  69.1 11.1 %collective-permute-done.14.refs_4_ = bf16[80,2048]{1,0:T(8,128)(2,1)S(1)} collective-permute-done((bf16[80,2048]{1,0:T(8,128)(2,1)}, bf16[80,2048]{1,0:T(8,128)(2,1)S(1)}, u32[]{:S(2)}, u32[]{:S(2)}) %collective-permute-start.14) | collective-permute-done | bytes 327712 | tf_op jit(solution)/shard_map/ppermute | solution.py:29
  80.1 3.7 %collective-permute-done.15.refs_5_ = bf16[80,2048]{1,0:T(8,128)(2,1)S(1)} collective-permute-done((bf16[80,2048]{1,0:T(8,128)(2,1)}, bf16[80,2048]{1,0:T(8,128)(2,1)S(1)}, u32[]{:S(2)}, u32[]{:S(2)}) %collective-permute-start.15) | collective-permute-done | bytes 327712 | tf_op jit(solution)/shard_map/ppermute | solution.py:29
  85.5 9.2 %shard_map.77 = bf16[192,3072]{1,0:T(8,128)(2,1)} custom-call(s32[2]{0:T(128)} %pad_add_fusion.refs_0_, bf16[4,48,2048]{2,1,0:T(8,128)(2,1)} %copy-done.11, bf16[4,48,2048]{2,1,0:T(8,128)(2,1)} %get-tuple-element.53.refs_2_, bf16[4,48,2048]{2,1,0:T(8,128)(2,1)} %get-tuple-element.54.refs_3_, bf16[2,48,2048]{2,1,0:T(8,128)(2,1)} %get-tuple-element.55.refs_4_, ...), custom_call_target="tpu_custom_call" | custom-call | flops 2415919104 | bytes 14548992 | tf_op jit(solution)/shard_map/pallas_call | solution.py:223
  94.8 8.2 %collective-permute-start.21 = (bf16[192,3072]{1,0:T(8,128)(2,1)}, bf16[192,3072]{1,0:T(8,128)(2,1)S(1)}, u32[]{:S(2)}, u32[]{:S(2)}) collective-permute-start(bf16[192,3072]{1,0:T(8,128)(2,1)} %shard_map.77), channel_id=1, source_target_pairs={{0,8},{4,12},{24,16},{28,20},{1,9},{5,13},{25,17},{29,21},{2,10},{... | collective-permute-start | bytes 3538952 | tf_op jit(solution)/shard_map/ppermute | solution.py:29
  107.2 13.9 %shard_map.76 = bf16[768,3072]{1,0:T(8,128)(2,1)} custom-call(s32[2]{0:T(128)S(1)} %copy-done.25, bf16[4,48,2048]{2,1,0:T(8,128)(2,1)S(1)} %copy-done.12, bf16[4,48,2048]{2,1,0:T(8,128)(2,1)S(1)} %copy-done.10, bf16[4,48,2048]{2,1,0:T(8,128)(2,1)S(1)} %copy-done.8, bf16[2,48,2048]{2,1,0:T(8,128)(2,1)S(1)} %copy-done.16, bf16[2,48,2048]{2,1,0:T(8,128)(2,1)S(1)} %copy-done.21, ...), custom_call_target="tpu_custom_call" | custom-call | flops 9663676416 | bytes 20447232 | tf_op jit(solution)/shard_map/pallas_call | solution.py:223
  124.6 5.3 %collective-permute-start.22 = (bf16[192,3072]{1,0:T(8,128)(2,1)S(1)}, bf16[192,3072]{1,0:T(8,128)(2,1)}, u32[]{:S(2)}, u32[]{:S(2)}) collective-permute-start(bf16[192,3072]{1,0:T(8,128)(2,1)S(1)} %add_convert_fusion.7), channel_id=1, source_target_pairs={{0,8},{4,12},{8,16},{12,20},{1,9},{5,13},{9,17},{13,21},{2,10},{6,... | collective-permute-start | bytes 3538952 | tf_op jit(solution)/shard_map/ppermute | solution.py:29
  135.1 7.3 %collective-permute-done.18.refs_0_ = bf16[2,80,2048]{2,1,0:T(8,128)(2,1)S(1)} collective-permute-done((bf16[2,80,2048]{2,1,0:T(8,128)(2,1)S(1)}, bf16[2,80,2048]{2,1,0:T(8,128)(2,1)S(1)}, u32[]{:S(2)}, u32[]{:S(2)}) %collective-permute-start.18) | collective-permute-done | bytes 655392 | tf_op jit(solution)/shard_map/ppermute | solution.py:25
  144.4 2.9 collective-permute-done.22.refs_4_
  147.3 3.2 %add_convert_fusion.5 = (bf16[192,3072]{1,0:T(8,128)(2,1)S(1)}, bf16[192,3072]{1,0:T(8,128)(2,1)S(1)}) fusion(bf16[192,3072]{1,0:T(8,128)(2,1)} %get-tuple-element.63, bf16[768,3072]{1,0:T(8,128)(2,1)} %shard_map.76, bf16[192,3072]{1,0:T(8,128)(2,1)} %get-tuple-element.62), kind=kLoop, calls=%fused_computation.11 | loop fusion | flops 4718592 | bytes 7077888 | tf_op jit(solution)/shard_map/convert_element_type | solution.py:297
  150.6 4.6 %collective-permute-start.24 = (bf16[192,3072]{1,0:T(8,128)(2,1)S(1)}, bf16[192,3072]{1,0:T(8,128)(2,1)S(1)}, u32[]{:S(2)}, u32[]{:S(2)}) collective-permute-start(bf16[192,3072]{1,0:T(8,128)(2,1)S(1)} %get-tuple-element.70), channel_id=1, source_target_pairs={{0,8},{4,12},{8,16},{12,20},{16,24},{20,28},{1,9},{5,13},{9,17},{1... | collective-permute-start | bytes 3538952 | tf_op jit(solution)/shard_map/ppermute | solution.py:29
  156.6 9.7 %shard_map.80 = bf16[320,3072]{1,0:T(8,128)(2,1)} custom-call(s32[2]{0:T(128)} %pad_add_fusion.refs_0_, bf16[4,80,2048]{2,1,0:T(8,128)(2,1)} %copy-done.5, bf16[4,80,2048]{2,1,0:T(8,128)(2,1)} %get-tuple-element.58.refs_2_, bf16[4,80,2048]{2,1,0:T(8,128)(2,1)} %get-tuple-element.59.refs_3_, bf16[2,80,2048]{2,1,0:T(8,128)(2,1)} %get-tuple-element.60.refs_4_, ...), custom_call_target="tpu_custom_call" | custom-call | flops 4026531840 | bytes 15859712 | tf_op jit(solution)/shard_map/pallas_call | solution.py:223
  166.3 7.8 %collective-permute-done.24.refs_1_ = bf16[192,3072]{1,0:T(8,128)(2,1)S(1)} collective-permute-done((bf16[192,3072]{1,0:T(8,128)(2,1)S(1)}, bf16[192,3072]{1,0:T(8,128)(2,1)S(1)}, u32[]{:S(2)}, u32[]{:S(2)}) %collective-permute-start.24) | collective-permute-done | bytes 1179680 | tf_op jit(solution)/shard_map/ppermute | solution.py:29
  176.2 4.8 %collective-permute-start.26 = (bf16[320,3072]{1,0:T(8,128)(2,1)}, bf16[320,3072]{1,0:T(8,128)(2,1)S(1)}, u32[]{:S(2)}, u32[]{:S(2)}) collective-permute-start(bf16[320,3072]{1,0:T(8,128)(2,1)} %bitcast.66), channel_id=1, source_target_pairs={{0,8},{4,12},{24,16},{28,20},{1,9},{5,13},{25,17},{29,21},{2,10},{... | collective-permute-start | bytes 5898248 | tf_op jit(solution)/shard_map/ppermute | solution.py:29
  181.1 2.8 copy-done
  186.2 20.9 %shard_map.79 = bf16[1280,3072]{1,0:T(8,128)(2,1)} custom-call(s32[2]{0:T(128)S(1)} %copy-done.26, bf16[4,80,2048]{2,1,0:T(8,128)(2,1)S(1)} %copy-done.6, bf16[4,80,2048]{2,1,0:T(8,128)(2,1)S(1)} %copy-done.4, bf16[4,80,2048]{2,1,0:T(8,128)(2,1)S(1)} %copy-done.2, bf16[2,80,2048]{2,1,0:T(8,128)(2,1)S(1)} %copy-done.14, bf16[2,80,2048]{2,1,0:T(8,128)(2,1)S(1)} %copy-done.18, ...), custom_call_target="tpu_custom_call" | custom-call | flops 16106127360 | bytes 25690112 | tf_op jit(solution)/shard_map/pallas_call | solution.py:223
  207.2 10.2 %collective-permute-done.26 = bf16[320,3072]{1,0:T(8,128)(2,1)S(1)} collective-permute-done((bf16[320,3072]{1,0:T(8,128)(2,1)}, bf16[320,3072]{1,0:T(8,128)(2,1)S(1)}, u32[]{:S(2)}, u32[]{:S(2)}) %collective-permute-start.26) | collective-permute-done | bytes 1966112 | tf_op jit(solution)/shard_map/ppermute | solution.py:29
  217.4 2.2 add_convert_fusion.3
  219.7 4.5 %collective-permute-start.27 = (bf16[320,3072]{1,0:T(8,128)(2,1)S(1)}, bf16[320,3072]{1,0:T(8,128)(2,1)S(1)}, u32[]{:S(2)}, u32[]{:S(2)}) collective-permute-start(bf16[320,3072]{1,0:T(8,128)(2,1)S(1)} %add_convert_fusion.3), channel_id=1, source_target_pairs={{0,8},{4,12},{8,16},{12,20},{1,9},{5,13},{9,17},{13,21},{2,10},{6,... | collective-permute-start | bytes 5898248 | tf_op jit(solution)/shard_map/ppermute | solution.py:29
  225.0 34.0 %collective-permute-done.27 = bf16[320,3072]{1,0:T(8,128)(2,1)S(1)} collective-permute-done((bf16[320,3072]{1,0:T(8,128)(2,1)S(1)}, bf16[320,3072]{1,0:T(8,128)(2,1)S(1)}, u32[]{:S(2)}, u32[]{:S(2)}) %collective-permute-start.27) | collective-permute-done | bytes 1966112 | tf_op jit(solution)/shard_map/ppermute | solution.py:29
  259.0 3.7 %add_convert_fusion.2 = (bf16[320,3072]{1,0:T(8,128)(2,1)S(1)}, bf16[320,3072]{1,0:T(8,128)(2,1)S(1)}) fusion(bf16[320,3072]{1,0:T(8,128)(2,1)S(1)} %collective-permute-done.27, bf16[1280,3072]{1,0:T(8,128)(2,1)} %shard_map.79, bf16[320,3072]{1,0:T(8,128)(2,1)S(1)} %collective-permute-done.29), kind=kLoop, calls=%fused_computation.2 | loop fusion | flops 7864320 | bytes 11796480 | tf_op jit(solution)/shard_map/convert_element_type | solution.py:297
  262.7 4.5 %collective-permute-start.28 = (bf16[320,3072]{1,0:T(8,128)(2,1)S(1)}, bf16[320,3072]{1,0:T(8,128)(2,1)S(1)}, u32[]{:S(2)}, u32[]{:S(2)}) collective-permute-start(bf16[320,3072]{1,0:T(8,128)(2,1)S(1)} %get-tuple-element.67), channel_id=1, source_target_pairs={{0,8},{4,12},{8,16},{12,20},{16,24},{20,28},{1,9},{5,13},{9,17},{1... | collective-permute-start | bytes 5898248 | tf_op jit(solution)/shard_map/ppermute | solution.py:29
  272.5 26.5 %collective-permute-done.28 = bf16[320,3072]{1,0:T(8,128)(2,1)S(1)} collective-permute-done((bf16[320,3072]{1,0:T(8,128)(2,1)S(1)}, bf16[320,3072]{1,0:T(8,128)(2,1)S(1)}, u32[]{:S(2)}, u32[]{:S(2)}) %collective-permute-start.28) | collective-permute-done | bytes 1966112 | tf_op jit(solution)/shard_map/ppermute | solution.py:29
  299.0 2.5 add_convert_fusion
  302.7 5.9 %shard_map.82 = bf16[512,1024]{1,0:T(8,128)(2,1)} custom-call(bf16[512,3072]{1,0:T(8,128)(2,1)S(1)} %pad_maximum_fusion.query.key.value, bf16[512,3072]{1,0:T(8,128)(2,1)S(1)} %pad_maximum_fusion.query.key.value, bf16[512,3072]{1,0:T(8,128)(2,1)S(1)} %pad_maximum_fusion.query.key.value, bf16[176,1024]{1,0:T(8,128)(2,1)S(1)} %collective-permute-done.31.rims, ...), custom_call_target="tpu_custom_call" | custom-call | flops 2621440000 | bytes 5242880 | tf_op jit(solution)/shard_map/pallas_call | solution.py:120
  (201 shorter events, 55.4 us)
Async XLA Ops:
  0.0 15.4 %collective-permute-start.3 = (bf16[3,1024,1024]{2,1,0:T(8,128)(2,1)}, bf16[3,1024,1024]{2,1,0:T(8,128)(2,1)}, u32[]{:S(2)}, u32[]{:S(2)}) collective-permute-start(bf16[3,1024,1024]{2,1,0:T(8,128)(2,1)} %bitcast.55), channel_id=1, source_target_pairs={{0,4},{4,0},{8,12},{12,8},{16,20},{20,16},{24,28},{28,24},{1,5},{5... | collective-permute-start | bytes 18874376 | tf_op jit(solution)/shard_map/ppermute | solution.py:263
  1.9 8.7 %collective-permute-start = (bf16[48,2048]{1,0:T(8,128)(2,1)S(1)}, bf16[48,2048]{1,0:T(8,128)(2,1)S(1)}, u32[]{:S(2)}, u32[]{:S(2)}) collective-permute-start(bf16[48,2048]{1,0:T(8,128)(2,1)S(1)} %get-tuple-element.94), channel_id=1, source_target_pairs={{0,1},{1,0},{2,3},{3,2},{4,5},{5,4},{6,7},{7,6},{8,9},{9,8},{10,11... | collective-permute-start | bytes 589832 | tf_op jit(solution)/shard_map/ppermute | solution.py:25
  4.8 10.6 %collective-permute-start.1 = (bf16[48,2048]{1,0:T(8,128)(2,1)S(1)}, bf16[48,2048]{1,0:T(8,128)(2,1)S(1)}, u32[]{:S(2)}, u32[]{:S(2)}) collective-permute-start(bf16[48,2048]{1,0:T(8,128)(2,1)S(1)} %get-tuple-element.93), channel_id=1, source_target_pairs={{0,2},{1,3},{2,0},{3,1},{4,6},{5,7},{6,4},{7,5},{8,10},{9,11},{10,... | collective-permute-start | bytes 589832 | tf_op jit(solution)/shard_map/ppermute | solution.py:25
  6.3 9.1 %collective-permute-start.2 = (bf16[48,2048]{1,0:T(8,128)(2,1)S(1)}, bf16[48,2048]{1,0:T(8,128)(2,1)S(1)}, u32[]{:S(2)}, u32[]{:S(2)}) collective-permute-start(bf16[48,2048]{1,0:T(8,128)(2,1)S(1)} %get-tuple-element.92), channel_id=1, source_target_pairs={{0,3},{1,2},{2,1},{3,0},{4,7},{5,6},{6,5},{7,4},{8,11},{9,10},{10,... | collective-permute-start | bytes 589832 | tf_op jit(solution)/shard_map/ppermute | solution.py:25
  19.8 8.7 %collective-permute-start.4 = (bf16[48,2048]{1,0:T(8,128)(2,1)S(1)}, bf16[48,2048]{1,0:T(8,128)(2,1)S(1)}, u32[]{:S(2)}, u32[]{:S(2)}) collective-permute-start(bf16[48,2048]{1,0:T(8,128)(2,1)S(1)} %get-tuple-element.89), channel_id=1, source_target_pairs={{0,24},{4,28},{8,0},{12,4},{16,8},{20,12},{24,16},{28,20},{1,25},{... | collective-permute-start | bytes 589832 | tf_op jit(solution)/shard_map/ppermute | solution.py:29
  23.5 17.3 %collective-permute-start.7 = (bf16[80,2048]{1,0:T(8,128)(2,1)S(1)}, bf16[80,2048]{1,0:T(8,128)(2,1)S(1)}, u32[]{:S(2)}, u32[]{:S(2)}) collective-permute-start(bf16[80,2048]{1,0:T(8,128)(2,1)S(1)} %copy-done.47), channel_id=1, source_target_pairs={{0,1},{1,0},{2,3},{3,2},{4,5},{5,4},{6,7},{7,6},{8,9},{9,8},{10,11... | collective-permute-start | bytes 983048 | tf_op jit(solution)/shard_map/ppermute | solution.py:25
  24.7 16.1 %collective-permute-start.8 = (bf16[80,2048]{1,0:T(8,128)(2,1)S(1)}, bf16[80,2048]{1,0:T(8,128)(2,1)S(1)}, u32[]{:S(2)}, u32[]{:S(2)}) collective-permute-start(bf16[80,2048]{1,0:T(8,128)(2,1)S(1)} %copy-done.46), channel_id=1, source_target_pairs={{0,2},{1,3},{2,0},{3,1},{4,6},{5,7},{6,4},{7,5},{8,10},{9,11},{10,... | collective-permute-start | bytes 983048 | tf_op jit(solution)/shard_map/ppermute | solution.py:25
  25.5 15.2 %collective-permute-start.9 = (bf16[80,2048]{1,0:T(8,128)(2,1)S(1)}, bf16[80,2048]{1,0:T(8,128)(2,1)S(1)}, u32[]{:S(2)}, u32[]{:S(2)}) collective-permute-start(bf16[80,2048]{1,0:T(8,128)(2,1)S(1)} %copy-done.45), channel_id=1, source_target_pairs={{0,3},{1,2},{2,1},{3,0},{4,7},{5,6},{6,5},{7,4},{8,11},{9,10},{10,... | collective-permute-start | bytes 983048 | tf_op jit(solution)/shard_map/ppermute | solution.py:25
  27.0 8.4 %collective-permute-start.5 = (bf16[48,2048]{1,0:T(8,128)(2,1)S(1)}, bf16[48,2048]{1,0:T(8,128)(2,1)S(1)}, u32[]{:S(2)}, u32[]{:S(2)}) collective-permute-start(bf16[48,2048]{1,0:T(8,128)(2,1)S(1)} %get-tuple-element.88), channel_id=1, source_target_pairs={{0,8},{4,12},{8,16},{12,20},{16,24},{20,28},{24,0},{28,4},{1,9},{5... | collective-permute-start | bytes 589832 | tf_op jit(solution)/shard_map/ppermute | solution.py:29
  28.5 12.3 %collective-permute-start.6 = (bf16[48,2048]{1,0:T(8,128)(2,1)S(1)}, bf16[48,2048]{1,0:T(8,128)(2,1)S(1)}, u32[]{:S(2)}, u32[]{:S(2)}) collective-permute-start(bf16[48,2048]{1,0:T(8,128)(2,1)S(1)} %get-tuple-element.87), channel_id=1, source_target_pairs={{0,16},{4,20},{8,24},{12,28},{16,0},{20,4},{24,8},{28,12},{1,17},{... | collective-permute-start | bytes 589832 | tf_op jit(solution)/shard_map/ppermute | solution.py:29
  43.1 18.6 %collective-permute-start.10 = (bf16[4,48,2048]{2,1,0:T(8,128)(2,1)S(1)}, bf16[4,48,2048]{2,1,0:T(8,128)(2,1)S(1)}, u32[]{:S(2)}, u32[]{:S(2)}) collective-permute-start(bf16[4,48,2048]{2,1,0:T(8,128)(2,1)S(1)} %pad_maximum_fusion.4.refs_1_), channel_id=1, source_target_pairs={{0,2},{1,3},{2,0},{3,1},{4,6},{5,7},{6,4},{7,5},{8,10},{9,11},{10,... | collective-permute-start | bytes 2359304 | tf_op jit(solution)/shard_map/ppermute | solution.py:25
  43.7 19.6 %collective-permute-start.12 = (bf16[4,48,2048]{2,1,0:T(8,128)(2,1)S(1)}, bf16[4,48,2048]{2,1,0:T(8,128)(2,1)S(1)}, u32[]{:S(2)}, u32[]{:S(2)}) collective-permute-start(bf16[4,48,2048]{2,1,0:T(8,128)(2,1)S(1)} %pad_maximum_fusion.4.refs_1_), channel_id=1, source_target_pairs={{0,1},{1,0},{2,3},{3,2},{4,5},{5,4},{6,7},{7,6},{8,9},{9,8},{10,11... | collective-permute-start | bytes 2359304 | tf_op jit(solution)/shard_map/ppermute | solution.py:25
  61.8 22.0 %collective-permute-start.11 = (bf16[2,48,2048]{2,1,0:T(8,128)(2,1)S(1)}, bf16[2,48,2048]{2,1,0:T(8,128)(2,1)S(1)}, u32[]{:S(2)}, u32[]{:S(2)}) collective-permute-start(bf16[2,48,2048]{2,1,0:T(8,128)(2,1)S(1)} %slice.126), channel_id=1, source_target_pairs={{0,1},{1,0},{2,3},{3,2},{4,5},{5,4},{6,7},{7,6},{8,9},{9,8},{10,11... | collective-permute-start | bytes 1179656 | tf_op jit(solution)/shard_map/ppermute | solution.py:25
  63.4 20.5 %collective-permute-start.13 = (bf16[2,48,2048]{2,1,0:T(8,128)(2,1)S(1)}, bf16[2,48,2048]{2,1,0:T(8,128)(2,1)S(1)}, u32[]{:S(2)}, u32[]{:S(2)}) collective-permute-start(bf16[2,48,2048]{2,1,0:T(8,128)(2,1)S(1)} %slice.127), channel_id=1, source_target_pairs={{0,2},{1,3},{2,0},{3,1},{4,6},{5,7},{6,4},{7,5},{8,10},{9,11},{10,... | collective-permute-start | bytes 1179656 | tf_op jit(solution)/shard_map/ppermute | solution.py:25
  65.2 14.9 %collective-permute-start.14 = (bf16[80,2048]{1,0:T(8,128)(2,1)}, bf16[80,2048]{1,0:T(8,128)(2,1)S(1)}, u32[]{:S(2)}, u32[]{:S(2)}) collective-permute-start(bf16[80,2048]{1,0:T(8,128)(2,1)} %get-tuple-element.74), channel_id=1, source_target_pairs={{0,24},{4,28},{8,0},{12,4},{16,8},{20,12},{24,16},{28,20},{1,25},{... | collective-permute-start | bytes 983048 | tf_op jit(solution)/shard_map/ppermute | solution.py:29
  67.8 16.0 %collective-permute-start.15 = (bf16[80,2048]{1,0:T(8,128)(2,1)}, bf16[80,2048]{1,0:T(8,128)(2,1)S(1)}, u32[]{:S(2)}, u32[]{:S(2)}) collective-permute-start(bf16[80,2048]{1,0:T(8,128)(2,1)} %get-tuple-element.71), channel_id=1, source_target_pairs={{0,8},{4,12},{8,16},{12,20},{16,24},{20,28},{24,0},{28,4},{1,9},{5... | collective-permute-start | bytes 983048 | tf_op jit(solution)/shard_map/ppermute | solution.py:29
  67.8 35.1 %collective-permute-start.16 = (bf16[80,2048]{1,0:T(8,128)(2,1)}, bf16[80,2048]{1,0:T(8,128)(2,1)}, u32[]{:S(2)}, u32[]{:S(2)}) collective-permute-start(bf16[80,2048]{1,0:T(8,128)(2,1)} %get-tuple-element.73), channel_id=1, source_target_pairs={{0,16},{4,20},{8,24},{12,28},{16,0},{20,4},{24,8},{28,12},{1,17},{... | collective-permute-start | bytes 983048 | tf_op jit(solution)/shard_map/ppermute | solution.py:29
  94.8 28.2 %collective-permute-start.21 = (bf16[192,3072]{1,0:T(8,128)(2,1)}, bf16[192,3072]{1,0:T(8,128)(2,1)S(1)}, u32[]{:S(2)}, u32[]{:S(2)}) collective-permute-start(bf16[192,3072]{1,0:T(8,128)(2,1)} %shard_map.77), channel_id=1, source_target_pairs={{0,8},{4,12},{24,16},{28,20},{1,9},{5,13},{25,17},{29,21},{2,10},{... | collective-permute-start | bytes 3538952 | tf_op jit(solution)/shard_map/ppermute | solution.py:29
  104.1 27.5 %collective-permute-start.17 = (bf16[4,80,2048]{2,1,0:T(8,128)(2,1)S(1)}, bf16[4,80,2048]{2,1,0:T(8,128)(2,1)S(1)}, u32[]{:S(2)}, u32[]{:S(2)}) collective-permute-start(bf16[4,80,2048]{2,1,0:T(8,128)(2,1)S(1)} %pad_maximum_fusion.2.refs_1_), channel_id=1, source_target_pairs={{0,2},{1,3},{2,0},{3,1},{4,6},{5,7},{6,4},{7,5},{8,10},{9,11},{10,... | collective-permute-start | bytes 3932168 | tf_op jit(solution)/shard_map/ppermute | solution.py:25
  105.8 26.8 %collective-permute-start.19 = (bf16[4,80,2048]{2,1,0:T(8,128)(2,1)S(1)}, bf16[4,80,2048]{2,1,0:T(8,128)(2,1)S(1)}, u32[]{:S(2)}, u32[]{:S(2)}) collective-permute-start(bf16[4,80,2048]{2,1,0:T(8,128)(2,1)S(1)} %pad_maximum_fusion.2.refs_1_), channel_id=1, source_target_pairs={{0,1},{1,0},{2,3},{3,2},{4,5},{5,4},{6,7},{7,6},{8,9},{9,8},{10,11... | collective-permute-start | bytes 3932168 | tf_op jit(solution)/shard_map/ppermute | solution.py:25
  124.6 22.7 %collective-permute-start.22 = (bf16[192,3072]{1,0:T(8,128)(2,1)S(1)}, bf16[192,3072]{1,0:T(8,128)(2,1)}, u32[]{:S(2)}, u32[]{:S(2)}) collective-permute-start(bf16[192,3072]{1,0:T(8,128)(2,1)S(1)} %add_convert_fusion.7), channel_id=1, source_target_pairs={{0,8},{4,12},{8,16},{12,20},{1,9},{5,13},{9,17},{13,21},{2,10},{6,... | collective-permute-start | bytes 3538952 | tf_op jit(solution)/shard_map/ppermute | solution.py:29
  130.0 17.3 %collective-permute-start.23 = (bf16[192,3072]{1,0:T(8,128)(2,1)S(1)}, bf16[192,3072]{1,0:T(8,128)(2,1)}, u32[]{:S(2)}, u32[]{:S(2)}) collective-permute-start(bf16[192,3072]{1,0:T(8,128)(2,1)S(1)} %add_convert_fusion.7), channel_id=1, source_target_pairs={{16,8},{20,12},{24,16},{28,20},{17,9},{21,13},{25,17},{29,21},{18,... | collective-permute-start | bytes 3538952 | tf_op jit(solution)/shard_map/ppermute | solution.py:29
  131.7 10.7 %collective-permute-start.18 = (bf16[2,80,2048]{2,1,0:T(8,128)(2,1)S(1)}, bf16[2,80,2048]{2,1,0:T(8,128)(2,1)S(1)}, u32[]{:S(2)}, u32[]{:S(2)}) collective-permute-start(bf16[2,80,2048]{2,1,0:T(8,128)(2,1)S(1)} %slice.130), channel_id=1, source_target_pairs={{0,1},{1,0},{2,3},{3,2},{4,5},{5,4},{6,7},{7,6},{8,9},{9,8},{10,11... | collective-permute-start | bytes 1966088 | tf_op jit(solution)/shard_map/ppermute | solution.py:25
  133.8 10.7 %collective-permute-start.20 = (bf16[2,80,2048]{2,1,0:T(8,128)(2,1)S(1)}, bf16[2,80,2048]{2,1,0:T(8,128)(2,1)S(1)}, u32[]{:S(2)}, u32[]{:S(2)}) collective-permute-start(bf16[2,80,2048]{2,1,0:T(8,128)(2,1)S(1)} %slice.131), channel_id=1, source_target_pairs={{0,2},{1,3},{2,0},{3,1},{4,6},{5,7},{6,4},{7,5},{8,10},{9,11},{10,... | collective-permute-start | bytes 1966088 | tf_op jit(solution)/shard_map/ppermute | solution.py:25
  150.6 23.6 %collective-permute-start.24 = (bf16[192,3072]{1,0:T(8,128)(2,1)S(1)}, bf16[192,3072]{1,0:T(8,128)(2,1)S(1)}, u32[]{:S(2)}, u32[]{:S(2)}) collective-permute-start(bf16[192,3072]{1,0:T(8,128)(2,1)S(1)} %get-tuple-element.70), channel_id=1, source_target_pairs={{0,8},{4,12},{8,16},{12,20},{16,24},{20,28},{1,9},{5,13},{9,17},{1... | collective-permute-start | bytes 3538952 | tf_op jit(solution)/shard_map/ppermute | solution.py:29
  155.1 19.0 %collective-permute-start.25 = (bf16[192,3072]{1,0:T(8,128)(2,1)S(1)}, bf16[192,3072]{1,0:T(8,128)(2,1)S(1)}, u32[]{:S(2)}, u32[]{:S(2)}) collective-permute-start(bf16[192,3072]{1,0:T(8,128)(2,1)S(1)} %get-tuple-element.69), channel_id=1, source_target_pairs={{8,0},{12,4},{16,8},{20,12},{24,16},{28,20},{9,1},{13,5},{17,9},{2... | collective-permute-start | bytes 3538952 | tf_op jit(solution)/shard_map/ppermute | solution.py:29
  176.2 41.1 %collective-permute-start.26 = (bf16[320,3072]{1,0:T(8,128)(2,1)}, bf16[320,3072]{1,0:T(8,128)(2,1)S(1)}, u32[]{:S(2)}, u32[]{:S(2)}) collective-permute-start(bf16[320,3072]{1,0:T(8,128)(2,1)} %bitcast.66), channel_id=1, source_target_pairs={{0,8},{4,12},{24,16},{28,20},{1,9},{5,13},{25,17},{29,21},{2,10},{... | collective-permute-start | bytes 5898248 | tf_op jit(solution)/shard_map/ppermute | solution.py:29
  219.7 39.3 %collective-permute-start.27 = (bf16[320,3072]{1,0:T(8,128)(2,1)S(1)}, bf16[320,3072]{1,0:T(8,128)(2,1)S(1)}, u32[]{:S(2)}, u32[]{:S(2)}) collective-permute-start(bf16[320,3072]{1,0:T(8,128)(2,1)S(1)} %add_convert_fusion.3), channel_id=1, source_target_pairs={{0,8},{4,12},{8,16},{12,20},{1,9},{5,13},{9,17},{13,21},{2,10},{6,... | collective-permute-start | bytes 5898248 | tf_op jit(solution)/shard_map/ppermute | solution.py:29
  224.2 34.8 %collective-permute-start.29 = (bf16[320,3072]{1,0:T(8,128)(2,1)S(1)}, bf16[320,3072]{1,0:T(8,128)(2,1)S(1)}, u32[]{:S(2)}, u32[]{:S(2)}) collective-permute-start(bf16[320,3072]{1,0:T(8,128)(2,1)S(1)} %add_convert_fusion.3), channel_id=1, source_target_pairs={{16,8},{20,12},{24,16},{28,20},{17,9},{21,13},{25,17},{29,21},{18,... | collective-permute-start | bytes 5898248 | tf_op jit(solution)/shard_map/ppermute | solution.py:29
  262.7 36.3 %collective-permute-start.28 = (bf16[320,3072]{1,0:T(8,128)(2,1)S(1)}, bf16[320,3072]{1,0:T(8,128)(2,1)S(1)}, u32[]{:S(2)}, u32[]{:S(2)}) collective-permute-start(bf16[320,3072]{1,0:T(8,128)(2,1)S(1)} %get-tuple-element.67), channel_id=1, source_target_pairs={{0,8},{4,12},{8,16},{12,20},{16,24},{20,28},{1,9},{5,13},{9,17},{1... | collective-permute-start | bytes 5898248 | tf_op jit(solution)/shard_map/ppermute | solution.py:29
  267.2 31.8 %collective-permute-start.30 = (bf16[320,3072]{1,0:T(8,128)(2,1)S(1)}, bf16[320,3072]{1,0:T(8,128)(2,1)S(1)}, u32[]{:S(2)}, u32[]{:S(2)}) collective-permute-start(bf16[320,3072]{1,0:T(8,128)(2,1)S(1)} %get-tuple-element.68), channel_id=1, source_target_pairs={{8,0},{12,4},{16,8},{20,12},{24,16},{28,20},{9,1},{13,5},{17,9},{2... | collective-permute-start | bytes 5898248 | tf_op jit(solution)/shard_map/ppermute | solution.py:29
  271.0 30.8 %collective-permute-start.31 = (bf16[176,1024]{1,0:T(8,128)(2,1)S(1)}, bf16[176,1024]{1,0:T(8,128)(2,1)S(1)}, u32[]{:S(2)}, u32[]{:S(2)}) collective-permute-start(bf16[176,1024]{1,0:T(8,128)(2,1)S(1)} %pad_maximum_fusion.5), channel_id=1, source_target_pairs={{0,4},{4,8},{8,12},{12,16},{16,20},{20,24},{24,28},{1,5},{5,9},{9,... | collective-permute-start | bytes 1081352 | tf_op jit(solution)/shard_map/ppermute | solution.py:153
  (61 other events, 501.0 us)
